TPU v7x, 32 devices: a whole 2x2x4 slice. The times are simulated.
32 devices in a mesh: pipe: 4 (over z), ctx: 4 (over x, core), head: 2 (over y).
Axes of the slice: x: 2, y: 2, z: 4, core: 2. Of those that a mesh axis runs over, the one named last changes fastest.
Arguments:
- queries: bfloat16 [4, 512, 8192], P('pipe', 'ctx', 'head'), may hold values from -6 to 6
- key_states: bfloat16 [4, 512, 1024], P('pipe', 'ctx', 'head'), may hold values from -6 to 6
- value_states: bfloat16 [4, 512, 1024], P('pipe', 'ctx', 'head'), may hold values from -6 to 6
- upstream: bfloat16 [4, 512, 8192], P('pipe', ('ctx', 'head')), may hold values from -6 to 6
- selected: int32 [4, 8, 8, 8], P('pipe', 'head', 'ctx'), may hold values from 0 to 7, as said below
Outputs:
- query_grad: bfloat16 [4, 512, 8192], P('pipe', 'ctx', 'head')
- key_grad: bfloat16 [4, 512, 1024], P('pipe', 'ctx', 'head')
- value_grad: bfloat16 [4, 512, 1024], P('pipe', 'ctx', 'head')
Inputs may be any that keep to these rules, and one draw needn't show every extreme that they name: `selected`: for query block b, entry 0 is b; the other 7 entries are distinct; min(b, 7) of them name blocks before b, the rest name blocks after b.
All inputs are finite; a program needn't handle non-finite values.
Results may differ from a plain program's by a relative error of at most 0.015.
Values may be sent and summed in bfloat16 or wider, within the bound.
No kernel may reach another device: no remote copies, remote signals or barrier semaphores. Data moves between devices by JAX's collectives and lax.ppermute only.
A program may use at most 64 MiB of HBM per device.

v0:
```python
import jax
import jax.numpy as jnp
from jax import lax
from jax.sharding import PartitionSpec as P

HD = 128
BLK = 64
TOPB = 8
GROUP = 8


def shifted_2(value, axis, steps):
    count = lax.axis_size(axis)
    pairs = [(source, (source + steps) % count) for source in range(count)]
    return lax.ppermute(value, axis, pairs)


def passed_along(block, axis, distance):
    devices = range(lax.axis_size(axis))
    route = [(i - distance, i) for i in devices if i - distance in devices]
    return lax.ppermute(block, axis, route)


def per_device(queries, key_states, value_states, upstream, selected):
    arrived = shifted_2(upstream, "pipe", -1)
    out_grad = lax.all_to_all(arrived, "head", split_axis=2, concat_axis=1, tiled=True)
    whole_keys, whole_values = (
        lax.all_gather(key_states, "ctx", axis=1, tiled=True),
        lax.all_gather(value_states, "ctx", axis=1, tiled=True),
    )
    tokens = whole_keys.shape[1]
    tok_dev = queries.shape[1]
    local_heads = key_states.shape[2] // HD
    local_blocks = tok_dev // BLK
    first_block = lax.axis_index("ctx") * local_blocks
    score_scale = HD ** (-0.5)
    key_table = whole_keys[0].reshape(tokens, local_heads, HD)
    value_table = whole_values[0].reshape(tokens, local_heads, HD)
    query_tiles = queries[0].reshape(local_blocks, BLK, local_heads, GROUP, HD)
    grad_tiles = out_grad[0].reshape(local_blocks, BLK, local_heads, GROUP, HD)
    chosen = jnp.transpose(selected[0], (1, 0, 2))
    block_ids = first_block + jnp.arange(local_blocks, dtype=jnp.int32)
    offsets = jnp.arange(BLK, dtype=jnp.int32)
    head_index = jnp.arange(local_heads, dtype=jnp.int32)[:, None]

    def block_step(running, inputs):
        key_sums, value_sums = running
        query_blk, grad_blk, chosen_blk, block_index = inputs
        row_index = (chosen_blk[:, :, None] * BLK + offsets).reshape(local_heads, TOPB * BLK)
        key_rows = key_table[row_index, head_index]
        value_rows = value_table[row_index, head_index]
        scores = (
            jnp.einsum("icgh,cjh->cgij", query_blk, key_rows, preferred_element_type=jnp.float32)
            * score_scale
        )
        query_pos = block_index * BLK + offsets
        visible = row_index[:, None, None, :] <= query_pos[None, None, :, None]
        scores = jnp.where(visible, scores, -jnp.inf)
        row_max = jnp.max(scores, axis=-1, keepdims=True)
        shifted = jnp.exp(scores - row_max)
        weights = shifted / jnp.sum(shifted, axis=-1, keepdims=True)
        weight_grad = jnp.einsum(
            "icgh,cjh->cgij", grad_blk, value_rows, preferred_element_type=jnp.float32
        )
        row_delta = jnp.sum(weights * weight_grad, axis=-1, keepdims=True)
        score_grad = (weights * (weight_grad - row_delta) * score_scale).astype(jnp.bfloat16)
        weight_half = weights.astype(jnp.bfloat16)
        query_part = jnp.einsum(
            "cgij,cjh->icgh", score_grad, key_rows, preferred_element_type=jnp.float32
        )
        key_part = jnp.einsum(
            "cgij,icgh->cjh", score_grad, query_blk, preferred_element_type=jnp.float32
        )
        value_part = jnp.einsum(
            "cgij,icgh->cjh", weight_half, grad_blk, preferred_element_type=jnp.float32
        )
        key_sums = key_sums.at[row_index, head_index].add(key_part)
        value_sums = value_sums.at[row_index, head_index].add(value_part)
        return ((key_sums, value_sums), query_part.astype(jnp.bfloat16))

    start = (
        jnp.zeros((tokens, local_heads, HD), jnp.float32),
        jnp.zeros((tokens, local_heads, HD), jnp.float32),
    )
    (key_sums, value_sums), query_parts = lax.scan(
        block_step, start, (query_tiles, grad_tiles, chosen, block_ids)
    )
    key_flat = key_sums.reshape(tokens, local_heads * HD)
    value_flat = value_sums.reshape(tokens, local_heads * HD)

    def partial_rows(begin, count):
        return jnp.concatenate(
            [
                lax.dynamic_slice_in_dim(key_flat, begin, count, 0),
                lax.dynamic_slice_in_dim(value_flat, begin, count, 0),
            ],
            axis=1,
        )

    ctx_count = lax.axis_size("ctx")
    ctx_place = lax.axis_index("ctx")

    def chain_turn(turn, carried):
        owner = turn + ctx_place - ctx_count + 1
        usable = (owner >= 0) & (owner < ctx_place)
        safe_owner = jnp.clip(owner, 0, ctx_count - 1)
        outgoing = jnp.where(usable, partial_rows(safe_owner * tok_dev, tok_dev) + carried, 0.0)
        return passed_along(outgoing.astype(jnp.bfloat16), "ctx", -1).astype(outgoing.dtype)

    empty = jnp.zeros((tok_dev, 2 * local_heads * HD), jnp.float32)
    received = lax.fori_loop(0, ctx_count - 1, chain_turn, empty)
    summed = partial_rows(ctx_place * tok_dev, tok_dev) + received
    half_width = local_heads * HD
    query_grad = query_parts.reshape(1, tok_dev, local_heads * GROUP * HD)
    key_grad = summed[:, :half_width].astype(jnp.bfloat16)[None]
    value_grad = summed[:, half_width:].astype(jnp.bfloat16)[None]
    return (query_grad, key_grad, value_grad)


def solution(mesh):
    placed = (
        P("pipe", "ctx", "head"),
        P("pipe", "ctx", "head"),
        P("pipe", "ctx", "head"),
        P("pipe", ("ctx", "head"), None),
        P("pipe", "head", "ctx", None),
    )
    return jax.shard_map(
        per_device,
        mesh=mesh,
        in_specs=placed,
        out_specs=(P("pipe", "ctx", "head"), P("pipe", "ctx", "head"), P("pipe", "ctx", "head")),
        check_vma=False,
    )
```

profile of v0, /device:TPU:24, one launch (start us, length us, event | category | flops | bytes accessed | tf_op | source)
XLA Modules:
  0.0 401.2 jit_solution(2539343274933907596)
XLA Ops:
  1.1 26.5 %collective-permute-done.1 = bf16[1,64,8192]{2,1,0:T(8,128)(2,1)S(1)} collective-permute-done((bf16[1,64,8192]{2,1,0:T(8,128)(2,1)}, bf16[1,64,8192]{2,1,0:T(8,128)(2,1)S(1)}, u32[]{:S(2)}, u32[]{:S(2)}) %collective-permute-start.1) | collective-permute-done | bytes 1048608 | tf_op jit(solution)/shard_map/ppermute | solution.py:15
  27.6 6.8 %copy.28 = bf16[1,64,8192]{1,0,2:T(2,128)(2,1)} copy(bf16[1,64,8192]{2,1,0:T(8,128)(2,1)S(1)} %collective-permute-done.1) | data formatting | bytes 2097152 | tf_op jit(solution)/shard_map/ppermute | solution.py:15
  34.9 45.2 %reduce.12 = bf16[8192,64]{1,0:T(8,128)(2,1)S(1)} reduce(bf16[8192,1,64]{2,1,0:T(2,128)(2,1)} %bitcast.180, bf16[]{:T(256)} %broadcast.228), dimensions={1}, to_apply=%bitcast.104.reduce_sub_computation | reduce | bytes 2097154
  80.1 2.5 reshape.188
  82.6 3.6 all-to-all-start
  86.2 1.3 copy.48
  87.5 7.2 %all_gather.6 = bf16[1,512,512]{2,1,0:T(8,128)(2,1)S(1)} all-gather(bf16[1,128,512]{2,1,0:T(8,128)(2,1)S(1)} %copy-done.7), channel_id=1, replica_groups=mesh['pipe'=4,'ctx'=4,'head'=2] {'ctx'}, dimensions={1}, use_global_device_ids=true | all-gather | bytes 655360 | tf_op jit(solution)/shard_map/all_gather | solution.py:28
  94.8 7.3 %all_gather.7 = bf16[1,512,512]{2,1,0:T(8,128)(2,1)S(1)} all-gather(bf16[1,128,512]{2,1,0:T(8,128)(2,1)S(1)} %copy-done.8), channel_id=1, replica_groups=mesh['pipe'=4,'ctx'=4,'head'=2] {'ctx'}, dimensions={1}, use_global_device_ids=true | all-gather | bytes 655360 | tf_op jit(solution)/shard_map/all_gather | solution.py:29
  102.3 2.8 reshape.189
  105.0 8.2 %copy.29 = bf16[1,64,8192]{2,1,0:T(8,128)(2,1)S(1)} copy(bf16[1,64,8192]{1,0,2:T(2,128)(2,1)} %bitcast.181) | data formatting | bytes 2097152 | tf_op jit(solution)/shard_map/all_to_all | solution.py:26
  114.0 1.6 reshape.187
  115.9 259.2 %while.34 = (s32[]{:T(128)}, f32[512,4,128]{2,1,0:T(4,128)S(1)}, f32[512,4,128]{2,1,0:T(4,128)S(1)}, bf16[2,64,4,8,128]{4,3,2,1,0:T(8,128)(2,1)}, s32[2,4,8]{2,0...) while((s32[]{:T(128)}, f32[512,4,128]{2,1,0:T(4,128)S(1)}, ...), condition=%wide.region_6.7_spmd.clone.clone, body=%wide.region_0.6_spmd.clone.clone.sunk | while | flops 1366216192 | bytes 60317588 | solution.py:85
  116.5 20.3 %gather_fusion.1 = bf16[2048,128]{1,0:T(8,128)(2,1)} fusion(bf16[512,4,128]{2,1,0:T(4,128)(2,1)S(1)} %get-tuple-element.545, s32[2048]{0:T(1024)S(1)} %bitcast.167), kind=kCustom, calls=%fused_computation.clone.clone.1 | custom fusion | bytes 1064960 | tf_op jit(solution)/shard_map/while/body/eval_jaxpr/gather | solution.py:50
  136.8 1.1 constant_dynamic-slice_fusion.13
  138.7 3.7 fusion.54
  143.8 6.9 %fusion.55 = (f32[4,8,64]{2,1,0:T(8,128)S(1)}, f32[4,8,64,512]{3,2,1,0:T(8,128)}) fusion(f32[4,512,64,8]{1,2,3,0:T(8,128)} %fusion.54, pred[4,64,512]{2,1,0:T(8,128)(4,1)S(1)} %broadcast_compare_fusion.2), kind=kOutput, calls=%fused_computation.67.clone.1 | output fusion | flops 6291967 | bytes 8527872 | tf_op jit(solution)/shard_map/while/body/eval_jaxpr/sub | solution.py:60
  150.7 20.3 %gather_fusion = bf16[2048,128]{1,0:T(8,128)(2,1)} fusion(bf16[512,4,128]{2,1,0:T(4,128)(2,1)S(1)} %get-tuple-element.547, s32[2048]{0:T(1024)S(1)} %bitcast.168), kind=kCustom, calls=%fused_computation.1.clone.clone.1 | custom fusion | bytes 1064960 | tf_op jit(solution)/shard_map/while/body/eval_jaxpr/gather | solution.py:51
  171.0 1.1 constant_dynamic-slice_fusion.12
  172.9 3.7 fusion.53
  176.7 18.1 %fusion.58 = bf16[1,64,4,8,128]{4,1,3,2,0:T(8,128)(2,1)} fusion(bf16[4,512,128,1]{2,1,3,0:T(8,128)(2,1)} %bitcast.176, f32[4,512,64,8]{1,2,3,0:T(8,128)} %fusion.53, f32[4,8,64,512]{3,2,1,0:T(8,128)} %get-tuple-element.502, f32[4,8,64]{2,1,0:T(8,128)S(1)} %get-tuple-element.503), kind=kOutput, calls=%fused_computation.26.clone.1 | convolution fusion | flops 276040192 | bytes 9445376 | tf_op jit(solution)/shard_map/while/body/eval_jaxpr/cgij,cjh->icgh/dot_general | solution.py:68
  194.7 2.2 copy_dynamic-update-slice_fusion.2
  196.9 4.5 %fusion.57 = f32[4,512,128,1]{2,1,3,0:T(8,128)} fusion(bf16[1,64,4,8,128]{4,3,2,0,1:T(8,128)(2,1)} %copy-done.1, f32[4,8,64,512]{3,2,1,0:T(8,128)} %get-tuple-element.502, f32[4,8,64]{2,1,0:T(8,128)S(1)} %get-tuple-element.503), kind=kOutput, calls=%fused_computation.16.clone.1 | convolution fusion | flops 270532608 | bytes 5775360 | tf_op jit(solution)/shard_map/while/body/eval_jaxpr/cgij,icgh->cjh/dot_general | solution.py:74
  201.6 12.2 %scatter_fusion.1 = f32[2048,128]{1,0:T(8,128)S(1)} fusion(f32[2048,128]{1,0:T(8,128)S(1)} %bitcast.172, s32[2048]{0:T(1024)S(1)} %bitcast.184, f32[2048,128]{1,0:T(8,128)} %bitcast.178), kind=kCustom, calls=%fused_computation.3.clone.clone.1 | custom fusion | flops 262144 | bytes 3153920 | tf_op jit(solution)/shard_map/while
  213.8 19.6 %fusion.56 = f32[4,512,128,1]{2,1,3,0:T(8,128)} fusion(f32[4,512,64,8]{1,2,3,0:T(8,128)} %fusion.53, bf16[1,64,4,8,128]{4,3,2,1,0:T(8,128)(2,1)} %copy-done, f32[4,8,64,512]{3,2,1,0:T(8,128)} %get-tuple-element.502, f32[4,8,64]{2,1,0:T(8,128)S(1)} %get-tuple-element.503), kind=kOutput, calls=%fused_computation.24.clone.1 | convolution fusion | flops 275778048 | bytes 9969664 | tf_op jit(solution)/shard_map/while/body/eval_jaxpr/cgij,icgh->cjh/dot_general | solution.py:71
  233.4 12.2 %scatter_fusion = f32[2048,128]{1,0:T(8,128)S(1)} fusion(f32[2048,128]{1,0:T(8,128)S(1)} %bitcast.169, s32[2048]{0:T(1024)S(1)} %bitcast.185, f32[2048,128]{1,0:T(8,128)} %bitcast.179), kind=kCustom, calls=%fused_computation.2.clone.clone.1 | custom fusion | flops 262144 | bytes 3153920 | tf_op jit(solution)/shard_map/while
  246.0 20.3 %gather_fusion.1 = bf16[2048,128]{1,0:T(8,128)(2,1)} fusion(bf16[512,4,128]{2,1,0:T(4,128)(2,1)S(1)} %get-tuple-element.545, s32[2048]{0:T(1024)S(1)} %bitcast.167), kind=kCustom, calls=%fused_computation.clone.clone.1 | custom fusion | bytes 1064960 | tf_op jit(solution)/shard_map/while/body/eval_jaxpr/gather | solution.py:50
  266.3 1.1 constant_dynamic-slice_fusion.13
  268.2 3.7 fusion.54
  273.3 6.9 %fusion.55 = (f32[4,8,64]{2,1,0:T(8,128)S(1)}, f32[4,8,64,512]{3,2,1,0:T(8,128)}) fusion(f32[4,512,64,8]{1,2,3,0:T(8,128)} %fusion.54, pred[4,64,512]{2,1,0:T(8,128)(4,1)S(1)} %broadcast_compare_fusion.2), kind=kOutput, calls=%fused_computation.67.clone.1 | output fusion | flops 6291967 | bytes 8527872 | tf_op jit(solution)/shard_map/while/body/eval_jaxpr/sub | solution.py:60
  280.2 20.3 %gather_fusion = bf16[2048,128]{1,0:T(8,128)(2,1)} fusion(bf16[512,4,128]{2,1,0:T(4,128)(2,1)S(1)} %get-tuple-element.547, s32[2048]{0:T(1024)S(1)} %bitcast.168), kind=kCustom, calls=%fused_computation.1.clone.clone.1 | custom fusion | bytes 1064960 | tf_op jit(solution)/shard_map/while/body/eval_jaxpr/gather | solution.py:51
  300.5 1.1 constant_dynamic-slice_fusion.12
  302.4 3.7 fusion.53
  306.2 18.1 %fusion.58 = bf16[1,64,4,8,128]{4,1,3,2,0:T(8,128)(2,1)} fusion(bf16[4,512,128,1]{2,1,3,0:T(8,128)(2,1)} %bitcast.176, f32[4,512,64,8]{1,2,3,0:T(8,128)} %fusion.53, f32[4,8,64,512]{3,2,1,0:T(8,128)} %get-tuple-element.502, f32[4,8,64]{2,1,0:T(8,128)S(1)} %get-tuple-element.503), kind=kOutput, calls=%fused_computation.26.clone.1 | convolution fusion | flops 276040192 | bytes 9445376 | tf_op jit(solution)/shard_map/while/body/eval_jaxpr/cgij,cjh->icgh/dot_general | solution.py:68
  324.3 2.2 copy_dynamic-update-slice_fusion.2
  326.4 4.5 %fusion.57 = f32[4,512,128,1]{2,1,3,0:T(8,128)} fusion(bf16[1,64,4,8,128]{4,3,2,0,1:T(8,128)(2,1)} %copy-done.1, f32[4,8,64,512]{3,2,1,0:T(8,128)} %get-tuple-element.502, f32[4,8,64]{2,1,0:T(8,128)S(1)} %get-tuple-element.503), kind=kOutput, calls=%fused_computation.16.clone.1 | convolution fusion | flops 270532608 | bytes 5775360 | tf_op jit(solution)/shard_map/while/body/eval_jaxpr/cgij,icgh->cjh/dot_general | solution.py:74
  331.1 12.2 %scatter_fusion.1 = f32[2048,128]{1,0:T(8,128)S(1)} fusion(f32[2048,128]{1,0:T(8,128)S(1)} %bitcast.172, s32[2048]{0:T(1024)S(1)} %bitcast.184, f32[2048,128]{1,0:T(8,128)} %bitcast.178), kind=kCustom, calls=%fused_computation.3.clone.clone.1 | custom fusion | flops 262144 | bytes 3153920 | tf_op jit(solution)/shard_map/while
  343.4 19.6 %fusion.56 = f32[4,512,128,1]{2,1,3,0:T(8,128)} fusion(f32[4,512,64,8]{1,2,3,0:T(8,128)} %fusion.53, bf16[1,64,4,8,128]{4,3,2,1,0:T(8,128)(2,1)} %copy-done, f32[4,8,64,512]{3,2,1,0:T(8,128)} %get-tuple-element.502, f32[4,8,64]{2,1,0:T(8,128)S(1)} %get-tuple-element.503), kind=kOutput, calls=%fused_computation.24.clone.1 | convolution fusion | flops 275778048 | bytes 9969664 | tf_op jit(solution)/shard_map/while/body/eval_jaxpr/cgij,icgh->cjh/dot_general | solution.py:71
  362.9 12.2 %scatter_fusion = f32[2048,128]{1,0:T(8,128)S(1)} fusion(f32[2048,128]{1,0:T(8,128)S(1)} %bitcast.169, s32[2048]{0:T(1024)S(1)} %bitcast.185, f32[2048,128]{1,0:T(8,128)} %bitcast.179), kind=kCustom, calls=%fused_computation.2.clone.clone.1 | custom fusion | flops 262144 | bytes 3153920 | tf_op jit(solution)/shard_map/while
  376.7 22.4 %while.35 = (s32[]{:T(128)}, f32[128,1024]{1,0:T(8,128)S(1)}, s32[]{:T(128)}, f32[512,512]{1,0:T(8,128)}, f32[512,512]{1,0:T(8,128)}, /*index=5*/s32[]{:T(128)},...) while((s32[]{:T(128)}, f32[128,1024]{1,0:T(8,128)S(1)}, s32[]{:T(128)}, ...), condition=%wide.region_8.9_spmd.clone, body=%wide.region_7.8_spmd.clone.sunk | while | flops 786446 | bytes 4194583 | solution.py:111
  376.7 1.2 constant_dynamic-slice_fusion.14
  378.0 1.3 collective-permute-start
  379.3 2.1 collective-permute-done
  381.5 1.1 constant_dynamic-slice_fusion.14
  382.7 1.3 collective-permute-start
  384.0 6.2 %collective-permute-done = bf16[128,1024]{1,0:T(8,128)(2,1)S(1)} collective-permute-done((bf16[128,1024]{1,0:T(8,128)(2,1)S(1)}, bf16[128,1024]{1,0:T(8,128)(2,1)S(1)}, u32[]{:S(2)}, u32[]{:S(2)}) %collective-permute-start) | collective-permute-done | bytes 262176 | tf_op jit(solution)/shard_map/while/body/eval_jaxpr/ppermute | solution.py:21
  391.4 1.3 collective-permute-start
  392.7 6.4 %collective-permute-done = bf16[128,1024]{1,0:T(8,128)(2,1)S(1)} collective-permute-done((bf16[128,1024]{1,0:T(8,128)(2,1)S(1)}, bf16[128,1024]{1,0:T(8,128)(2,1)S(1)}, u32[]{:S(2)}, u32[]{:S(2)}) %collective-permute-start) | collective-permute-done | bytes 262176 | tf_op jit(solution)/shard_map/while/body/eval_jaxpr/ppermute | solution.py:21
  400.0 1.3 reshape.124
  (89 shorter events, 11.9 us)
Async XLA Ops:
  0.6 27.0 %collective-permute-start.1 = (bf16[1,64,8192]{2,1,0:T(8,128)(2,1)}, bf16[1,64,8192]{2,1,0:T(8,128)(2,1)S(1)}, u32[]{:S(2)}, u32[]{:S(2)}) collective-permute-start(bf16[1,64,8192]{2,1,0:T(8,128)(2,1)} %param.12), channel_id=1, source_target_pairs={{0,24},{8,0},{16,8},{24,16},{1,25},{9,1},{17,9},{25,17},{2,26},{10... | collective-permute-start | bytes 3145736 | tf_op jit(solution)/shard_map/ppermute | solution.py:15
  80.1 6.1 %copy-start.5 = (bf16[1,128,4096]{2,1,0:T(8,128)(2,1)S(1)}, bf16[1,128,4096]{2,1,0:T(8,128)(2,1)}, u32[]{:S(2)}) copy-start(bf16[1,128,4096]{2,1,0:T(8,128)(2,1)} %param.9) | copy-start | bytes 3145732
  80.1 7.4 %copy-start.7 = (bf16[1,128,512]{2,1,0:T(8,128)(2,1)S(1)}, bf16[1,128,512]{2,1,0:T(8,128)(2,1)}, u32[]{:S(2)}) copy-start(bf16[1,128,512]{2,1,0:T(8,128)(2,1)} %param.10) | copy-start | bytes 393220
  80.1 14.7 %copy-start.8 = (bf16[1,128,512]{2,1,0:T(8,128)(2,1)S(1)}, bf16[1,128,512]{2,1,0:T(8,128)(2,1)}, u32[]{:S(2)}) copy-start(bf16[1,128,512]{2,1,0:T(8,128)(2,1)} %param.11) | copy-start | bytes 393220
  82.6 19.7 %all-to-all-start = ((bf16[2,2,131072]{2,1,0:T(2,128)(2,1)}), bf16[2,2,131072]{2,1,0:T(2,128)(2,1)S(1)}, u32[]{:S(2)}, u32[]{:S(2)}) async-start(bf16[2,2,131072]{2,1,0:T(2,128)(2,1)} %reshape.188), calls=%async_computation | async-start | bytes 2097152 | tf_op jit(solution)/shard_map/all_to_all | solution.py:26
  113.2 2.7 copy-start.9
  113.2 2.7 copy-start.10
  113.2 2.7 copy-start.11
  137.9 0.8 copy-start
  172.1 0.8 copy-start.1
  267.4 0.8 copy-start
  301.6 0.8 copy-start.1
  375.2 1.6 copy-start.2
  375.4 1.0 copy-start.3
  375.4 1.4 copy-start.4
  376.7 23.2 %copy-start.6 = (bf16[2,64,4,8,128]{4,3,2,1,0:T(8,128)(2,1)S(1)}, bf16[2,64,4,8,128]{4,3,2,1,0:T(8,128)(2,1)}, u32[]{:S(2)}) copy-start(bf16[2,64,4,8,128]{4,3,2,1,0:T(8,128)(2,1)} %get-tuple-element.243) | copy-start | bytes 3145732
  378.0 3.4 collective-permute-start
  382.7 7.5 %collective-permute-start = (bf16[128,1024]{1,0:T(8,128)(2,1)S(1)}, bf16[128,1024]{1,0:T(8,128)(2,1)S(1)}, u32[]{:S(2)}, u32[]{:S(2)}) collective-permute-start(bf16[128,1024]{1,0:T(8,128)(2,1)S(1)} %fusion.59), channel_id=1, source_target_pairs={{2,0},{4,2},{6,4},{3,1},{5,3},{7,5},{10,8},{12,10},{14,12},{11,9},... | collective-permute-start | bytes 786440 | tf_op jit(solution)/shard_map/while/body/eval_jaxpr/ppermute | solution.py:21
  391.4 7.7 %collective-permute-start = (bf16[128,1024]{1,0:T(8,128)(2,1)S(1)}, bf16[128,1024]{1,0:T(8,128)(2,1)S(1)}, u32[]{:S(2)}, u32[]{:S(2)}) collective-permute-start(bf16[128,1024]{1,0:T(8,128)(2,1)S(1)} %fusion.59), channel_id=1, source_target_pairs={{2,0},{4,2},{6,4},{3,1},{5,3},{7,5},{10,8},{12,10},{14,12},{11,9},... | collective-permute-start | bytes 786440 | tf_op jit(solution)/shard_map/while/body/eval_jaxpr/ppermute | solution.py:21
where the time goes:
time: 408 us; the launch traced here: 401 us
  local copies, waits for them, and re-layouts  127 us (31%)
  other arithmetic  109 us (27%)
  matrix products  99.2 us (24%)
  waiting for transfers between devices  41.2 us (10%)
  blocking collectives  14.4 us (4%)
  starting transfers between devices  7.96 us (2%)
    while x12, other arithmetic  49.4 us
    unnamed x2, other arithmetic  45.2 us
    gather x2, local copies, waits for them, and re-layouts, block_step(): value_rows = value_table[row_index, head_index]  40.7 us
    gather x2, local copies, waits for them, and re-layouts, block_step(): key_rows = key_table[row_index, head_index]  40.7 us
    dot_general x2, matrix products, block_step(): jnp.einsum('cgij,icgh->cjh', score_grad, query_blk, preferred_element_typ...  39.1 us
    dot_general x2, matrix products, block_step(): jnp.einsum('cgij,cjh->icgh', score_grad, key_rows, preferred_element_type...  36.2 us
    ppermute x1, waiting for transfers between devices, shifted_2(): return lax.ppermute(value, axis, pairs)  26.5 us
    ppermute x3, waiting for transfers between devices, passed_along(): return lax.ppermute(block, axis, route)  14.8 us
  transfers between devices with their start and end apart: 5, of which 4 were waited for; matrix products, arithmetic and copies ran while one was open for 0% of the time, Pallas kernels for 0%

commit v1 on v0

v1 whole, which is shorter than its diff:
```python
import functools

import jax
import jax.numpy as jnp
from jax import lax
from jax.experimental import pallas as pl
from jax.experimental.pallas import tpu as pltpu
from jax.sharding import PartitionSpec as P

HD = 128
BLK = 64
GROUP = 8
PAIR = 2 * HD
HEAD_COLS = GROUP * HD
LOG2E = 1.4426950408889634
SCALE = HD**-0.5
VMEM = pltpu.MemorySpace.VMEM


def in_vmem():
    return pl.BlockSpec(memory_space=VMEM)


def contract(a, b, dims):
    return lax.dot_general(a, b, (dims, ((), ())), preferred_element_type=jnp.float32)


def two_heads(ref, column):
    wide = ref[:, pl.ds(pl.multiple_of(column, PAIR), PAIR)]
    return jnp.concatenate([wide[:, :HD], wide[:, HD:]], axis=0)


def stacked(refs, head):
    return jnp.concatenate([ref[:, head * HD : (head + 1) * HD] for ref in refs], axis=0)


def weights_kernel(slots, heads, q_ref, bias_ref, *refs):
    key_refs, out_ref = refs[:slots], refs[slots]
    tok_dev = q_ref.shape[0]
    keys = slots * tok_dev
    for head in range(heads):
        key_rows = stacked(key_refs, head)
        bias = bias_ref[head]
        bias = jnp.concatenate([bias, bias], axis=1)
        key_at = lax.broadcasted_iota(jnp.int32, (tok_dev, PAIR), 0)
        query_at = lax.broadcasted_iota(jnp.int32, (tok_dev, PAIR), 1) % tok_dev
        causal = key_at <= query_at

        def pair_step(pair, carry):
            rows = two_heads(q_ref, head * HEAD_COLS + pair * PAIR)
            scores = contract(key_rows, rows, ((1,), (1,))) * (SCALE * LOG2E)
            parts = []
            for kb in range(keys // BLK):
                part = scores[kb * BLK : (kb + 1) * BLK] + bias[kb : kb + 1]
                if kb * BLK < tok_dev:
                    part = jnp.where(causal[kb * BLK : (kb + 1) * BLK], part, -jnp.inf)
                parts.append(part)
            scores = jnp.concatenate(parts, axis=0)
            shifted = jnp.exp2(scores - jnp.max(scores, axis=0, keepdims=True))
            weights = shifted * (1.0 / jnp.sum(shifted, axis=0, keepdims=True))
            out_ref[head, :, pl.ds(pl.multiple_of(pair * PAIR, PAIR), PAIR)] = weights.astype(jnp.bfloat16)
            return carry

        lax.fori_loop(0, GROUP // 2, pair_step, 0)


def grads_kernel(slots, pieces, first, count, p_ref, q_ref, *refs):
    key_refs, refs = refs[:slots], refs[slots:]
    value_refs, refs = refs[:slots], refs[slots:]
    piece_refs, refs = refs[:pieces], refs[pieces:]
    dq_ref, keep_ref, send_ref, grad_ref, sum_ref = refs
    here = lax.axis_index("head")
    rows = piece_refs[0].shape[0]
    for step, piece in enumerate(piece_refs):
        source = lax.rem(here + pieces - step, pieces)
        grad_ref[pl.ds(pl.multiple_of(source * rows, rows), rows), :] = piece[...]
    half = send_ref.shape[0]
    for local in range(count):
        head = first + local
        key_rows = stacked(key_refs, head)
        value_rows = stacked(value_refs, head)
        sum_ref[...] = jnp.zeros_like(sum_ref)

        def pair_step(pair, carry):
            grads = two_heads(grad_ref, local * HEAD_COLS + pair * PAIR)
            queries = two_heads(q_ref, head * HEAD_COLS + pair * PAIR)
            half_weights = p_ref[head, :, pl.ds(pl.multiple_of(pair * PAIR, PAIR), PAIR)]
            weights = half_weights.astype(jnp.float32)
            weight_grad = contract(value_rows, grads, ((1,), (1,)))
            delta = jnp.sum(weights * weight_grad, axis=0, keepdims=True)
            score_grad = (weights * (weight_grad - delta)).astype(jnp.bfloat16)
            sum_ref[:, :HD] += contract(score_grad, queries, ((1,), (0,)))
            sum_ref[:, HD:] += contract(half_weights, grads, ((1,), (0,)))
            turned = contract(key_rows, score_grad, ((0,), (0,))) * SCALE
            tokens = turned.shape[1] // 2
            query_grad = jnp.concatenate([turned[:, :tokens].T, turned[:, tokens:].T], axis=1)
            column = pl.multiple_of(local * HEAD_COLS + pair * PAIR, PAIR)
            dq_ref[:, pl.ds(column, PAIR)] = query_grad.astype(jnp.bfloat16)
            return carry

        lax.fori_loop(0, GROUP // 2, pair_step, 0)
        for at, factor in ((0, SCALE), (1, 1.0)):
            total = sum_ref[:, at * HD : (at + 1) * HD] * factor
            columns = slice((at * count + local) * HD, (at * count + local + 1) * HD)
            keep_ref[:, columns] = total[:half]
            send_ref[:, columns] = total[half:].astype(jnp.bfloat16)


def per_device(queries, key_states, value_states, upstream, selected):
    ctx, here = lax.axis_size("ctx"), lax.axis_index("ctx")
    pipe, split = lax.axis_size("pipe"), lax.axis_size("head")
    head_place = lax.axis_index("head")
    tok_dev = queries.shape[1]
    heads = key_states.shape[2] // HD
    blocks = tok_dev // BLK
    chunks = [(0, 2), (2, 1), (3, 1)] if heads == 4 else [(at, 1) for at in range(heads)]

    def swapped(value, mask):
        return lax.ppermute(value, "ctx", [(place, place ^ mask) for place in range(ctx)])

    def arriving(first, count):
        pieces = []
        for step in range(split):
            route = [
                (sec * split + at, (sec - 1) % pipe * split + (at + step) % split)
                for sec in range(pipe)
                for at in range(split)
            ]
            target = lax.rem(head_place + step, split)
            start = (target * heads + first) * HEAD_COLS
            part = lax.dynamic_slice_in_dim(upstream[0], start, count * HEAD_COLS, 1)
            pieces.append(lax.ppermute(part, ("pipe", "head"), route))
        return pieces

    pieces = [arriving(first, count) for first, count in chunks]

    masks = [1 << bit for bit in reversed(range(ctx.bit_length() - 1))]
    order = [0]
    key_slots, value_slots = [key_states[0]], [value_states[0]]
    for mask in masks:
        order = order + [slot ^ mask for slot in order]
        key_slots = key_slots + [swapped(part, mask) for part in key_slots]
        value_slots = value_slots + [swapped(part, mask) for part in value_slots]

    slot_owner = here ^ jnp.array(order, dtype=jnp.int32)
    key_block = (slot_owner[:, None] * blocks + jnp.arange(blocks, dtype=jnp.int32)).reshape(-1)
    query_block = here * blocks + jnp.arange(blocks, dtype=jnp.int32)
    chosen = jnp.any(selected[0][:, :, :, None] == key_block, axis=2)
    usable = chosen & (key_block[None, None, :] <= query_block[None, :, None])
    bias = jnp.where(usable, 0.0, -jnp.inf).astype(jnp.float32)
    bias = jnp.repeat(jnp.transpose(bias, (0, 2, 1)), BLK, axis=2)

    slots = len(order)
    keys = slots * tok_dev
    rows = GROUP * tok_dev
    weights = pl.pallas_call(
        functools.partial(weights_kernel, slots, heads),
        out_shape=jax.ShapeDtypeStruct((heads, keys, rows), jnp.bfloat16),
        in_specs=[in_vmem()] * (2 + slots),
        out_specs=in_vmem(),
        name="weights",
        cost_estimate=pl.CostEstimate(
            flops=2 * heads * keys * rows * HD, bytes_accessed=8 << 20, transcendentals=heads * keys * rows
        ),
        compiler_params=pltpu.CompilerParams(vmem_limit_bytes=24 << 20),
    )(queries[0], bias, *key_slots)

    query_parts, key_parts, value_parts = [], [], []
    for (first, count), parts in zip(chunks, pieces):
        width = 2 * count * HD
        query_part, keep, send = pl.pallas_call(
            functools.partial(grads_kernel, slots, split, first, count),
            out_shape=(
                jax.ShapeDtypeStruct((tok_dev, count * HEAD_COLS), jnp.bfloat16),
                jax.ShapeDtypeStruct((keys // 2, width), jnp.float32),
                jax.ShapeDtypeStruct((keys // 2, width), jnp.bfloat16),
            ),
            in_specs=[in_vmem()] * (2 + 2 * slots + split),
            out_specs=(in_vmem(),) * 3,
            scratch_shapes=[
                pltpu.VMEM((tok_dev, count * HEAD_COLS), jnp.bfloat16),
                pltpu.VMEM((keys, 2 * HD), jnp.float32),
            ],
            name=f"grads_{first}",
            cost_estimate=pl.CostEstimate(
                flops=8 * count * keys * rows * HD, bytes_accessed=4 << 20, transcendentals=0
            ),
            compiler_params=pltpu.CompilerParams(vmem_limit_bytes=24 << 20),
        )(weights, queries[0], *key_slots, *value_slots, *parts)
        query_parts.append(query_part)
        for mask in reversed(masks):
            total = keep + swapped(send, mask).astype(jnp.float32)
            half = total.shape[0] // 2
            if mask != masks[0]:
                keep, send = total[:half], total[half:].astype(jnp.bfloat16)
            else:
                keep = total
        key_parts.append(keep[:, : width // 2].astype(jnp.bfloat16))
        value_parts.append(keep[:, width // 2 :].astype(jnp.bfloat16))
    query_grad = jnp.concatenate(query_parts, axis=1)[None]
    key_grad = jnp.concatenate(key_parts, axis=1)[None]
    value_grad = jnp.concatenate(value_parts, axis=1)[None]
    return query_grad, key_grad, value_grad


def solution(mesh):
    split = P("pipe", "ctx", "head")
    placed = (split, split, split, P("pipe", ("ctx", "head"), None), P("pipe", "head", "ctx", None))
    return jax.shard_map(
        per_device, mesh=mesh, in_specs=placed, out_specs=(split, split, split), check_vma=False
    )
```

time: 408 us -> 54.5 us (0.13)
  the two profiles are of different devices: /device:TPU:24 before, /device:TPU:0 now
where the time goes in v1:
time: 54.5 us; the launch traced here: 54.3 us
  starting transfers between devices  20.4 us (37%)
  Pallas kernels  19.2 us (35%)
  waiting for transfers between devices  7.58 us (14%)
  other arithmetic  3.55 us (7%)
  local copies, waits for them, and re-layouts  2.64 us (5%)
  between operations  0.87 us (2%)
    pallas_call x3, Pallas kernels, per_device(): pl.pallas_call(functools.partial(grads_kernel, slots, split, first, count...  12.4 us
    ppermute x6, starting transfers between devices, arriving(): pieces.append(lax.ppermute(part, ('pipe', 'head'), route))  11.8 us
    ppermute x12, starting transfers between devices, swapped(): lax.ppermute(value, 'ctx', [(place, place ^ mask) for place in range(ctx)])  8.61 us
    ppermute x12, waiting for transfers between devices, swapped(): lax.ppermute(value, 'ctx', [(place, place ^ mask) for place in range(ctx)])  7.57 us
    pallas_call x1, Pallas kernels, per_device(): pl.pallas_call(functools.partial(weights_kernel, slots, heads), out_shape...  6.8 us
    dynamic_slice x2, local copies, waits for them, and re-layouts, arriving(): part = lax.dynamic_slice_in_dim(upstream[0], start, count * HEAD_COLS, 1)  2.2 us
  transfers between devices with their start and end apart: 18, of which 3 were waited for; matrix products, arithmetic and copies ran while one was open for 10% of the time, Pallas kernels for 35%

profile of v1, /device:TPU:0, one launch (start us, length us, event | category | flops | bytes accessed | tf_op | source)
XLA Modules:
  0.0 54.3 jit_solution(14704195348370580104)
XLA Ops:
  0.6 3.0 %collective-permute-start = (bf16[128,512]{1,0:T(8,128)(2,1)}, bf16[128,512]{1,0:T(8,128)(2,1)S(1)}, u32[]{:S(2)}, u32[]{:S(2)}) collective-permute-start(bf16[128,512]{1,0:T(8,128)(2,1)} %bitcast.30), channel_id=1, source_target_pairs={{0,4},{2,6},{4,0},{6,2},{1,5},{3,7},{5,1},{7,3},{8,12},{10,14},{12... | collective-permute-start | bytes 393224 | tf_op jit(solution)/shard_map/ppermute | solution.py:119
  3.7 0.0 collective-permute-start.1
  3.7 0.2 collective-permute-start.3
  3.8 0.4 collective-permute-start.4
  4.2 1.1 %dynamic-slice_bitcast_fusion = (bf16[64,2048]{1,0:T(8,128)(2,1)S(1)}, bf16[64,2048]{1,0:T(8,128)(2,1)S(1)}) fusion(bf16[1,64,8192]{2,1,0:T(8,128)(2,1)} %param.9, s32[]{:T(128)S(6)} %select_n.25, s32[]{:T(128)S(6)} %select_n.24), kind=kLoop, calls=%fused_computation.7 | loop fusion | bytes 1048584 | tf_op jit(solution)/shard_map/dynamic_slice | solution.py:131
  5.2 3.9 %collective-permute-start.6 = (bf16[64,2048]{1,0:T(8,128)(2,1)S(1)}, bf16[64,2048]{1,0:T(8,128)(2,1)S(1)}, u32[]{:S(2)}, u32[]{:S(2)}) collective-permute-start(bf16[64,2048]{1,0:T(8,128)(2,1)S(1)} %get-tuple-element.22), channel_id=1, source_target_pairs={{0,24},{1,25},{8,0},{9,1},{16,8},{17,9},{24,16},{25,17},{2,26},{3,... | collective-permute-start | bytes 786440 | tf_op jit(solution)/shard_map/ppermute | solution.py:132
  9.2 0.7 %xor_multiply_fusion = s32[4]{0:T(128)S(1)} fusion(s32[4]{0:T(128)} %constant.44.clone, s32[]{:T(128)S(6)} %axis_index.23), kind=kLoop, calls=%fused_computation.27 | loop fusion | flops 8 | bytes 36 | tf_op jit(solution)/shard_map/mul | solution.py:146
  9.8 0.1 iota_add_fusion
  9.9 0.1 add.90
  10.0 0.1 broadcast_compare_fusion
  10.0 0.8 %compare_reduce_fusion = pred[4,2,8]{2,1,0:T(4,128)(4,1)S(1)} fusion(s32[8]{0:T(128)S(1)} %add.90, s32[4,2,8]{2,1,0:T(2,128)} %bitcast.41), kind=kLoop, calls=%fused_computation.21 | loop fusion | flops 960 | bytes 352 | tf_op jit(solution)/shard_map/reduce_or | solution.py:148
  10.8 0.0 collective-permute-done.refs_1_
  10.8 2.0 %collective-permute-start.7 = (bf16[64,2048]{1,0:T(8,128)(2,1)S(1)}, bf16[64,2048]{1,0:T(8,128)(2,1)S(1)}, u32[]{:S(2)}, u32[]{:S(2)}) collective-permute-start(bf16[64,2048]{1,0:T(8,128)(2,1)S(1)} %get-tuple-element.21), channel_id=1, source_target_pairs={{0,25},{1,24},{8,1},{9,0},{16,9},{17,8},{24,17},{25,16},{2,27},{3,... | collective-permute-start | bytes 786440 | tf_op jit(solution)/shard_map/ppermute | solution.py:132
  12.8 0.1 copy.9
  12.9 0.1 broadcast_in_dim.25
  13.0 0.1 reshape.81.bias_ref
  13.1 0.0 collective-permute-done.3.refs_5_
  13.1 0.5 collective-permute-start.5
  13.7 1.1 %dynamic-slice_bitcast_fusion.4 = (bf16[64,1024]{1,0:T(8,128)(2,1)S(1)}, bf16[64,1024]{1,0:T(8,128)(2,1)S(1)}, bf16[64,1024]{1,0:T(8,128)(2,1)S(1)}, bf16[64,1024]{1,0:T(8,128)(2,1)S(1)}) fusion(bf16[1,64,8192]{2,1,0:T(8,128)(2,1)} %param.9, s32[]{:T(128)S(6)} %select_n.27, s32[]{:T(128)S(6)} %select_n.26, s32[]{:T(128)S(6)} %select_n.29, s32[]{:T(128)S(6)} %select_n.28), kind=kLoop, calls=%fused_computation.19 | loop fusion | bytes 1048592 | tf_op jit(solution)/shard_map/dynamic_slice | solution.py:131
  14.8 0.0 collective-permute-done.4.refs_6_
  14.8 0.5 collective-permute-start.8
  15.3 0.0 collective-permute-done.2.refs_3_
  15.3 1.3 %collective-permute-start.9 = (bf16[64,1024]{1,0:T(8,128)(2,1)S(1)}, bf16[64,1024]{1,0:T(8,128)(2,1)S(1)}, u32[]{:S(2)}, u32[]{:S(2)}) collective-permute-start(bf16[64,1024]{1,0:T(8,128)(2,1)S(1)} %get-tuple-element.23), channel_id=1, source_target_pairs={{0,25},{1,24},{8,1},{9,0},{16,9},{17,8},{24,17},{25,16},{2,27},{3,... | collective-permute-start | bytes 393224 | tf_op jit(solution)/shard_map/ppermute | solution.py:132
  16.6 6.8 %weights.1.p_ref = bf16[4,512,1024]{2,1,0:T(8,128)(2,1)S(1)} custom-call(bf16[128,4096]{1,0:T(8,128)(2,1)S(1)} %bitcast.26, f32[4,8,128]{2,1,0:T(8,128)S(1)} %reshape.81.bias_ref, bf16[128,512]{1,0:T(8,128)(2,1)S(1)} %bitcast.32, bf16[128,512]{1,0:T(8,128)(2,1)S(1)} %collective-permute-done.refs_1_, bf16[128,512]{1,0:T(8,128)(2,1)S(1)} %collective-permute-done.1.refs_2_, ...), custom_call_target="tpu_custom_call" | custom-call | flops 536870912 | bytes 8388608 | tf_op jit(solution)/shard_map/weights/pallas_call | solution.py:156
  23.4 0.0 collective-permute-done.6.refs_8_
  23.5 2.2 %collective-permute-start.10 = (bf16[64,1024]{1,0:T(8,128)(2,1)S(1)}, bf16[64,1024]{1,0:T(8,128)(2,1)S(1)}, u32[]{:S(2)}, u32[]{:S(2)}) collective-permute-start(bf16[64,1024]{1,0:T(8,128)(2,1)S(1)} %get-tuple-element.26), channel_id=1, source_target_pairs={{0,24},{1,25},{8,0},{9,1},{16,8},{17,9},{24,16},{25,17},{2,26},{3,... | collective-permute-start | bytes 393224 | tf_op jit(solution)/shard_map/ppermute | solution.py:132
  25.7 0.0 collective-permute-done.7.refs_9_
  25.7 1.9 %collective-permute-start.11 = (bf16[64,1024]{1,0:T(8,128)(2,1)S(1)}, bf16[64,1024]{1,0:T(8,128)(2,1)S(1)}, u32[]{:S(2)}, u32[]{:S(2)}) collective-permute-start(bf16[64,1024]{1,0:T(8,128)(2,1)S(1)} %get-tuple-element.25), channel_id=1, source_target_pairs={{0,25},{1,24},{8,1},{9,0},{16,9},{17,8},{24,17},{25,16},{2,27},{3,... | collective-permute-start | bytes 393224 | tf_op jit(solution)/shard_map/ppermute | solution.py:132
  27.6 0.0 collective-permute-done.5.refs_7_
  27.6 6.2 %grads_0.1 = (bf16[128,2048]{1,0:T(8,128)(2,1)S(1)}, f32[256,512]{1,0:T(8,128)S(1)}, bf16[256,512]{1,0:T(8,128)(2,1)S(1)}) custom-call(bf16[4,512,1024]{2,1,0:T(8,128)(2,1)S(1)} %weights.1.p_ref, bf16[128,4096]{1,0:T(8,128)(2,1)S(1)} %bitcast.27, bf16[128,512]{1,0:T(8,128)(2,1)S(1)} %bitcast.33, bf16[128,512]{1,0:T(8,128)(2,1)S(1)} %collective-permute-done.refs_1_, ...), custom_call_target="tpu_custom_call" | custom-call | flops 1073741824 | bytes 4194304 | tf_op jit(solution)/shard_map/grads_0/pallas_call | solution.py:171
  33.8 0.1 collective-permute-start.12
  33.9 0.0 collective-permute-done.8.refs_8_
  33.9 0.0 collective-permute-done.9.refs_9_
  33.9 3.1 %grads_2.1 = (bf16[128,1024]{1,0:T(8,128)(2,1)S(1)}, f32[256,256]{1,0:T(8,128)S(1)}, bf16[256,256]{1,0:T(8,128)(2,1)S(1)}) custom-call(bf16[4,512,1024]{2,1,0:T(8,128)(2,1)S(1)} %weights.1.p_ref, bf16[128,4096]{1,0:T(8,128)(2,1)S(1)} %bitcast.28, bf16[128,512]{1,0:T(8,128)(2,1)S(1)} %bitcast.34, bf16[128,512]{1,0:T(8,128)(2,1)S(1)} %collective-permute-done.refs_1_, ...), custom_call_target="tpu_custom_call" | custom-call | flops 536870912 | bytes 4194304 | tf_op jit(solution)/shard_map/grads_2/pallas_call | solution.py:171
  37.0 0.5 collective-permute-start.14
  37.6 0.0 collective-permute-done.11.refs_9_
  37.6 3.1 %grads_3.1 = (bf16[128,1024]{1,0:T(8,128)(2,1)S(1)}, f32[256,256]{1,0:T(8,128)S(1)}, bf16[256,256]{1,0:T(8,128)(2,1)S(1)}) custom-call(bf16[4,512,1024]{2,1,0:T(8,128)(2,1)S(1)} %weights.1.p_ref, bf16[128,4096]{1,0:T(8,128)(2,1)S(1)} %bitcast.29, bf16[128,512]{1,0:T(8,128)(2,1)S(1)} %bitcast.35, bf16[128,512]{1,0:T(8,128)(2,1)S(1)} %collective-permute-done.refs_1_, ...), custom_call_target="tpu_custom_call" | custom-call | flops 536870912 | bytes 4194304 | tf_op jit(solution)/shard_map/grads_3/pallas_call | solution.py:171
  40.7 0.1 collective-permute-start.16
  40.8 1.1 %maximum_bitcast_fusion = bf16[1,128,4096]{2,1,0:T(8,128)(2,1)} fusion(bf16[128,1024]{1,0:T(8,128)(2,1)S(1)} %get-tuple-element.14, bf16[128,1024]{1,0:T(8,128)(2,1)S(1)} %get-tuple-element.13, bf16[128,2048]{1,0:T(8,128)(2,1)S(1)} %get-tuple-element.12), kind=kLoop, calls=%fused_computation | loop fusion | flops 3145728 | bytes 2097152 | tf_op jit(solution)/shard_map/broadcast_in_dim | solution.py:200
  41.9 0.0 collective-permute-done.14
  41.9 2.1 %collective-permute-start.15 = (bf16[128,256]{1,0:T(8,128)(2,1)S(1)}, bf16[128,256]{1,0:T(8,128)(2,1)S(1)}, u32[]{:S(2)}, u32[]{:S(2)}) collective-permute-start(bf16[128,256]{1,0:T(8,128)(2,1)S(1)} %slice.83), channel_id=1, source_target_pairs={{0,4},{2,6},{4,0},{6,2},{1,5},{3,7},{5,1},{7,3},{8,12},{10,14},{12... | collective-permute-start | bytes 196616 | tf_op jit(solution)/shard_map/ppermute | solution.py:119
  44.0 0.2 collective-permute-start.17
  44.3 2.5 %collective-permute-done.15 = bf16[128,256]{1,0:T(8,128)(2,1)S(1)} collective-permute-done((bf16[128,256]{1,0:T(8,128)(2,1)S(1)}, bf16[128,256]{1,0:T(8,128)(2,1)S(1)}, u32[]{:S(2)}, u32[]{:S(2)}) %collective-permute-start.15) | collective-permute-done | bytes 65568 | tf_op jit(solution)/shard_map/ppermute | solution.py:119
  46.8 1.6 %collective-permute-done.17 = bf16[128,256]{1,0:T(8,128)(2,1)S(1)} collective-permute-done((bf16[128,256]{1,0:T(8,128)(2,1)S(1)}, bf16[128,256]{1,0:T(8,128)(2,1)S(1)}, u32[]{:S(2)}, u32[]{:S(2)}) %collective-permute-start.17) | collective-permute-done | bytes 65568 | tf_op jit(solution)/shard_map/ppermute | solution.py:119
  48.4 0.1 convert_add_fusion
  48.5 1.6 %collective-permute-start.13 = (bf16[128,512]{1,0:T(8,128)(2,1)S(1)}, bf16[128,512]{1,0:T(8,128)(2,1)S(1)}, u32[]{:S(2)}, u32[]{:S(2)}) collective-permute-start(bf16[128,512]{1,0:T(8,128)(2,1)S(1)} %slice.81), channel_id=1, source_target_pairs={{0,4},{2,6},{4,0},{6,2},{1,5},{3,7},{5,1},{7,3},{8,12},{10,14},{12... | collective-permute-start | bytes 393224 | tf_op jit(solution)/shard_map/ppermute | solution.py:119
  50.1 3.5 %collective-permute-done.13 = bf16[128,512]{1,0:T(8,128)(2,1)S(1)} collective-permute-done((bf16[128,512]{1,0:T(8,128)(2,1)S(1)}, bf16[128,512]{1,0:T(8,128)(2,1)S(1)}, u32[]{:S(2)}, u32[]{:S(2)}) %collective-permute-start.13) | collective-permute-done | bytes 131104 | tf_op jit(solution)/shard_map/ppermute | solution.py:119
  53.6 0.7 %maximum_bitcast_fusion.1 = (bf16[1,128,512]{2,1,0:T(8,128)(2,1)}, bf16[1,128,512]{2,1,0:T(8,128)(2,1)}) fusion(bf16[128,128]{1,0:T(8,128)(2,1)S(1)} %get-tuple-element.32, bf16[128,128]{1,0:T(8,128)(2,1)S(1)} %get-tuple-element.30, bf16[128,256]{1,0:T(8,128)(2,1)S(1)} %get-tuple-element.28, bf16[128,128]{1,0:T(8,128)(2,1)S(1)} %get-tuple-element.31, ...), kind=kLoop, calls=%fused_computation.15 | loop fusion | flops 786432 | bytes 524288 | tf_op jit(solution)/shard_map/broadcast_in_dim | solution.py:201
  (24 shorter events, 0.2 us)
Async XLA Ops:
  0.6 16.0 %copy-start.1 = (bf16[1,128,512]{2,1,0:T(8,128)(2,1)S(1)}, bf16[1,128,512]{2,1,0:T(8,128)(2,1)}, u32[]{:S(2)}) copy-start(bf16[1,128,512]{2,1,0:T(8,128)(2,1)} %param.7) | copy-start | bytes 393220
  0.6 16.0 %copy-start = (bf16[1,128,4096]{2,1,0:T(8,128)(2,1)S(1)}, bf16[1,128,4096]{2,1,0:T(8,128)(2,1)}, u32[]{:S(2)}) copy-start(bf16[1,128,4096]{2,1,0:T(8,128)(2,1)} %param.6) | copy-start | bytes 3145732
  0.6 10.2 %collective-permute-start = (bf16[128,512]{1,0:T(8,128)(2,1)}, bf16[128,512]{1,0:T(8,128)(2,1)S(1)}, u32[]{:S(2)}, u32[]{:S(2)}) collective-permute-start(bf16[128,512]{1,0:T(8,128)(2,1)} %bitcast.30), channel_id=1, source_target_pairs={{0,4},{2,6},{4,0},{6,2},{1,5},{3,7},{5,1},{7,3},{8,12},{10,14},{12... | collective-permute-start | bytes 393224 | tf_op jit(solution)/shard_map/ppermute | solution.py:119
  3.7 9.2 %collective-permute-start.1 = (bf16[128,512]{1,0:T(8,128)(2,1)}, bf16[128,512]{1,0:T(8,128)(2,1)S(1)}, u32[]{:S(2)}, u32[]{:S(2)}) collective-permute-start(bf16[128,512]{1,0:T(8,128)(2,1)} %bitcast.31), channel_id=1, source_target_pairs={{0,2},{2,0},{4,6},{6,4},{1,3},{3,1},{5,7},{7,5},{8,10},{10,8},{12,... | collective-permute-start | bytes 393224 | tf_op jit(solution)/shard_map/ppermute | solution.py:119
  3.7 9.5 %collective-permute-start.3 = (bf16[128,512]{1,0:T(8,128)(2,1)}, bf16[128,512]{1,0:T(8,128)(2,1)S(1)}, u32[]{:S(2)}, u32[]{:S(2)}) collective-permute-start(bf16[128,512]{1,0:T(8,128)(2,1)} %bitcast.36), channel_id=1, source_target_pairs={{0,4},{2,6},{4,0},{6,2},{1,5},{3,7},{5,1},{7,3},{8,12},{10,14},{12... | collective-permute-start | bytes 393224 | tf_op jit(solution)/shard_map/ppermute | solution.py:119
  3.8 11.0 %collective-permute-start.4 = (bf16[128,512]{1,0:T(8,128)(2,1)}, bf16[128,512]{1,0:T(8,128)(2,1)S(1)}, u32[]{:S(2)}, u32[]{:S(2)}) collective-permute-start(bf16[128,512]{1,0:T(8,128)(2,1)} %bitcast.37), channel_id=1, source_target_pairs={{0,2},{2,0},{4,6},{6,4},{1,3},{3,1},{5,7},{7,5},{8,10},{10,8},{12,... | collective-permute-start | bytes 393224 | tf_op jit(solution)/shard_map/ppermute | solution.py:119
  5.2 18.2 %collective-permute-start.6 = (bf16[64,2048]{1,0:T(8,128)(2,1)S(1)}, bf16[64,2048]{1,0:T(8,128)(2,1)S(1)}, u32[]{:S(2)}, u32[]{:S(2)}) collective-permute-start(bf16[64,2048]{1,0:T(8,128)(2,1)S(1)} %get-tuple-element.22), channel_id=1, source_target_pairs={{0,24},{1,25},{8,0},{9,1},{16,8},{17,9},{24,16},{25,17},{2,26},{3,... | collective-permute-start | bytes 786440 | tf_op jit(solution)/shard_map/ppermute | solution.py:132
  10.8 14.8 %collective-permute-start.7 = (bf16[64,2048]{1,0:T(8,128)(2,1)S(1)}, bf16[64,2048]{1,0:T(8,128)(2,1)S(1)}, u32[]{:S(2)}, u32[]{:S(2)}) collective-permute-start(bf16[64,2048]{1,0:T(8,128)(2,1)S(1)} %get-tuple-element.21), channel_id=1, source_target_pairs={{0,25},{1,24},{8,1},{9,0},{16,9},{17,8},{24,17},{25,16},{2,27},{3,... | collective-permute-start | bytes 786440 | tf_op jit(solution)/shard_map/ppermute | solution.py:132
  12.8 2.5 %collective-permute-start.2 = (bf16[128,512]{1,0:T(8,128)(2,1)S(1)}, bf16[128,512]{1,0:T(8,128)(2,1)S(1)}, u32[]{:S(2)}, u32[]{:S(2)}) collective-permute-start(bf16[128,512]{1,0:T(8,128)(2,1)S(1)} %collective-permute-done.refs_1_), channel_id=1, source_target_pairs={{0,2},{2,0},{4,6},{6,4},{1,3},{3,1},{5,7},{7,5},{8,10},{10,8},{12,... | collective-permute-start | bytes 393224 | tf_op jit(solution)/shard_map/ppermute | solution.py:119
  13.1 14.4 %collective-permute-start.5 = (bf16[128,512]{1,0:T(8,128)(2,1)S(1)}, bf16[128,512]{1,0:T(8,128)(2,1)S(1)}, u32[]{:S(2)}, u32[]{:S(2)}) collective-permute-start(bf16[128,512]{1,0:T(8,128)(2,1)S(1)} %collective-permute-done.3.refs_5_), channel_id=1, source_target_pairs={{0,2},{2,0},{4,6},{6,4},{1,3},{3,1},{5,7},{7,5},{8,10},{10,8},{12,... | collective-permute-start | bytes 393224 | tf_op jit(solution)/shard_map/ppermute | solution.py:119
  14.8 19.1 %collective-permute-start.8 = (bf16[64,1024]{1,0:T(8,128)(2,1)S(1)}, bf16[64,1024]{1,0:T(8,128)(2,1)S(1)}, u32[]{:S(2)}, u32[]{:S(2)}) collective-permute-start(bf16[64,1024]{1,0:T(8,128)(2,1)S(1)} %get-tuple-element.24), channel_id=1, source_target_pairs={{0,24},{1,25},{8,0},{9,1},{16,8},{17,9},{24,16},{25,17},{2,26},{3,... | collective-permute-start | bytes 393224 | tf_op jit(solution)/shard_map/ppermute | solution.py:132
  15.3 18.6 %collective-permute-start.9 = (bf16[64,1024]{1,0:T(8,128)(2,1)S(1)}, bf16[64,1024]{1,0:T(8,128)(2,1)S(1)}, u32[]{:S(2)}, u32[]{:S(2)}) collective-permute-start(bf16[64,1024]{1,0:T(8,128)(2,1)S(1)} %get-tuple-element.23), channel_id=1, source_target_pairs={{0,25},{1,24},{8,1},{9,0},{16,9},{17,8},{24,17},{25,16},{2,27},{3,... | collective-permute-start | bytes 393224 | tf_op jit(solution)/shard_map/ppermute | solution.py:132
  16.6 11.0 %copy-start.2 = (bf16[1,128,512]{2,1,0:T(8,128)(2,1)S(1)}, bf16[1,128,512]{2,1,0:T(8,128)(2,1)}, u32[]{:S(2)}) copy-start(bf16[1,128,512]{2,1,0:T(8,128)(2,1)} %param.8) | copy-start | bytes 393220
  23.5 14.1 %collective-permute-start.10 = (bf16[64,1024]{1,0:T(8,128)(2,1)S(1)}, bf16[64,1024]{1,0:T(8,128)(2,1)S(1)}, u32[]{:S(2)}, u32[]{:S(2)}) collective-permute-start(bf16[64,1024]{1,0:T(8,128)(2,1)S(1)} %get-tuple-element.26), channel_id=1, source_target_pairs={{0,24},{1,25},{8,0},{9,1},{16,8},{17,9},{24,16},{25,17},{2,26},{3,... | collective-permute-start | bytes 393224 | tf_op jit(solution)/shard_map/ppermute | solution.py:132
  25.7 11.9 %collective-permute-start.11 = (bf16[64,1024]{1,0:T(8,128)(2,1)S(1)}, bf16[64,1024]{1,0:T(8,128)(2,1)S(1)}, u32[]{:S(2)}, u32[]{:S(2)}) collective-permute-start(bf16[64,1024]{1,0:T(8,128)(2,1)S(1)} %get-tuple-element.25), channel_id=1, source_target_pairs={{0,25},{1,24},{8,1},{9,0},{16,9},{17,8},{24,17},{25,16},{2,27},{3,... | collective-permute-start | bytes 393224 | tf_op jit(solution)/shard_map/ppermute | solution.py:132
  33.8 14.6 %collective-permute-start.12 = (bf16[256,512]{1,0:T(8,128)(2,1)S(1)}, bf16[256,512]{1,0:T(8,128)(2,1)S(1)}, u32[]{:S(2)}, u32[]{:S(2)}) collective-permute-start(bf16[256,512]{1,0:T(8,128)(2,1)S(1)} %get-tuple-element.16), channel_id=1, source_target_pairs={{0,2},{2,0},{4,6},{6,4},{1,3},{3,1},{5,7},{7,5},{8,10},{10,8},{12,... | collective-permute-start | bytes 786440 | tf_op jit(solution)/shard_map/ppermute | solution.py:119
  37.0 4.8 %collective-permute-start.14 = (bf16[256,256]{1,0:T(8,128)(2,1)S(1)}, bf16[256,256]{1,0:T(8,128)(2,1)S(1)}, u32[]{:S(2)}, u32[]{:S(2)}) collective-permute-start(bf16[256,256]{1,0:T(8,128)(2,1)S(1)} %get-tuple-element.18), channel_id=1, source_target_pairs={{0,2},{2,0},{4,6},{6,4},{1,3},{3,1},{5,7},{7,5},{8,10},{10,8},{12,... | collective-permute-start | bytes 393224 | tf_op jit(solution)/shard_map/ppermute | solution.py:119
  40.7 3.3 %collective-permute-start.16 = (bf16[256,256]{1,0:T(8,128)(2,1)S(1)}, bf16[256,256]{1,0:T(8,128)(2,1)S(1)}, u32[]{:S(2)}, u32[]{:S(2)}) collective-permute-start(bf16[256,256]{1,0:T(8,128)(2,1)S(1)} %get-tuple-element.20), channel_id=1, source_target_pairs={{0,2},{2,0},{4,6},{6,4},{1,3},{3,1},{5,7},{7,5},{8,10},{10,8},{12,... | collective-permute-start | bytes 393224 | tf_op jit(solution)/shard_map/ppermute | solution.py:119
  41.9 4.8 %collective-permute-start.15 = (bf16[128,256]{1,0:T(8,128)(2,1)S(1)}, bf16[128,256]{1,0:T(8,128)(2,1)S(1)}, u32[]{:S(2)}, u32[]{:S(2)}) collective-permute-start(bf16[128,256]{1,0:T(8,128)(2,1)S(1)} %slice.83), channel_id=1, source_target_pairs={{0,4},{2,6},{4,0},{6,2},{1,5},{3,7},{5,1},{7,3},{8,12},{10,14},{12... | collective-permute-start | bytes 196616 | tf_op jit(solution)/shard_map/ppermute | solution.py:119
  44.0 4.3 %collective-permute-start.17 = (bf16[128,256]{1,0:T(8,128)(2,1)S(1)}, bf16[128,256]{1,0:T(8,128)(2,1)S(1)}, u32[]{:S(2)}, u32[]{:S(2)}) collective-permute-start(bf16[128,256]{1,0:T(8,128)(2,1)S(1)} %slice.82), channel_id=1, source_target_pairs={{0,4},{2,6},{4,0},{6,2},{1,5},{3,7},{5,1},{7,3},{8,12},{10,14},{12... | collective-permute-start | bytes 196616 | tf_op jit(solution)/shard_map/ppermute | solution.py:119
  48.5 5.0 %collective-permute-start.13 = (bf16[128,512]{1,0:T(8,128)(2,1)S(1)}, bf16[128,512]{1,0:T(8,128)(2,1)S(1)}, u32[]{:S(2)}, u32[]{:S(2)}) collective-permute-start(bf16[128,512]{1,0:T(8,128)(2,1)S(1)} %slice.81), channel_id=1, source_target_pairs={{0,4},{2,6},{4,0},{6,2},{1,5},{3,7},{5,1},{7,3},{8,12},{10,14},{12... | collective-permute-start | bytes 393224 | tf_op jit(solution)/shard_map/ppermute | solution.py:119

commit v2 on v0

v2 whole, which is shorter than its diff:
```python
import functools

import jax
import jax.numpy as jnp
from jax import lax
from jax.experimental import pallas as pl
from jax.experimental.pallas import tpu as pltpu
from jax.sharding import PartitionSpec as P

HD = 128
BLK = 64
GROUP = 8
HEAD_COLS = GROUP * HD
LOG2E = 1.4426950408889634
SCALE = HD**-0.5
VMEM = pltpu.MemorySpace.VMEM
HBM = pltpu.MemorySpace.HBM
BF16 = jnp.bfloat16
F32 = jnp.float32


def spec(space=VMEM):
    return pl.BlockSpec(memory_space=space)


def in_hbm(value):
    return pltpu.with_memory_space_constraint(value, HBM)


def shape(dims, dtype=BF16):
    return jax.ShapeDtypeStruct(dims, dtype)


def call(body, name, out_shape, in_specs, out_specs, traffic=1024, **rest):
    return pl.pallas_call(
        body,
        out_shape=out_shape,
        in_specs=in_specs,
        out_specs=out_specs,
        name=name,
        cost_estimate=pl.CostEstimate(flops=1024, bytes_accessed=traffic, transcendentals=0),
        compiler_params=pltpu.CompilerParams(vmem_limit_bytes=24 << 20),
        **rest,
    )


def contract(a, b, dims):
    return lax.dot_general(a, b, (dims, ((), ())), preferred_element_type=F32)


def head_rows(ref, head):
    first = head * HEAD_COLS
    return jnp.concatenate([ref[:, first + g * HD : first + (g + 1) * HD] for g in range(GROUP)], axis=0)


def key_rows(refs, head):
    return jnp.concatenate([ref[:, head * HD : (head + 1) * HD] for ref in refs], axis=0)


def value_rows(refs, head):
    first = refs[0].shape[1] // 2 + head * HD
    return jnp.concatenate([ref[:, first : first + HD] for ref in refs], axis=0)


def store_rows(ref, column, turned):
    rows = ref.shape[0]
    for g in range(GROUP):
        ref[:, column + g * HD : column + (g + 1) * HD] = turned[:, g * rows : (g + 1) * rows].T


def run_copies(copies, sem):
    copies = [pltpu.make_async_copy(src, dst, sem.at[at]) for at, (src, dst) in enumerate(copies)]
    for copy in copies:
        copy.start()
    for copy in copies:
        copy.wait()


def cut_copies(sends, split, heads, up_ref, piece_refs):
    here = lax.axis_index("head")
    copies = []
    for at, (first, count) in enumerate(sends):
        for step in range(split):
            target = lax.rem(here + step, split)
            start = pl.multiple_of((target * heads * GROUP + first) * HD, HD)
            copies.append((up_ref.at[:, pl.ds(start, count * HD)], piece_refs[at * split + step]))
    return copies


def first_load_kernel(sends, split, heads, up_ref, k_ref, v_ref, *refs):
    *piece_refs, kv_out, sem = refs
    wide = k_ref.shape[1]
    copies = [(k_ref, kv_out.at[:, :wide]), (v_ref, kv_out.at[:, wide:])]
    run_copies(copies + cut_copies(sends, split, heads, up_ref, piece_refs), sem)


def later_load_kernel(sends, split, heads, up_ref, q_ref, *refs):
    *piece_refs, q_out, sem = refs
    run_copies([*cut_copies(sends, split, heads, up_ref, piece_refs), (q_ref, q_out)], sem)


def block_bias(order, selected_ref, head, tok_dev):
    blocks = tok_dev // BLK
    total = len(order) * blocks
    here = lax.axis_index("ctx")
    at = lax.broadcasted_iota(jnp.int32, (total, 1), 0)
    slot = jnp.zeros_like(at)
    for index, mask in enumerate(order):
        slot = jnp.where(at // blocks == index, mask, slot)
    key_block = (here ^ slot) * blocks + at % blocks
    columns = []
    for qb in range(blocks):
        hit = jnp.where(selected_ref[head, qb : qb + 1, :] == key_block, 1, 0)
        chosen = jnp.max(hit, axis=1, keepdims=True) > 0
        bias = jnp.where(chosen & (key_block <= here * blocks + qb), 0.0, -jnp.inf)
        columns.append(jnp.broadcast_to(bias, (total, BLK)))
    return jnp.concatenate(columns * GROUP, axis=1)


def weights_kernel(order, heads, q_ref, selected_ref, *refs):
    kv_refs, p_ref = refs[:-1], refs[-1]
    tok_dev = q_ref.shape[0]
    rows = GROUP * tok_dev
    keys = len(order) * tok_dev
    key_at = lax.broadcasted_iota(jnp.int32, (tok_dev, rows), 0)
    query_at = lax.broadcasted_iota(jnp.int32, (tok_dev, rows), 1) % tok_dev
    causal = key_at <= query_at
    for head in range(heads):
        bias = block_bias(order, selected_ref, head, tok_dev)
        scores = contract(key_rows(kv_refs, head), head_rows(q_ref, head), ((1,), (1,)))
        scores = scores * (SCALE * LOG2E)
        parts = []
        for kb in range(keys // BLK):
            part = scores[kb * BLK : (kb + 1) * BLK] + bias[kb : kb + 1]
            if kb * BLK < tok_dev:
                part = jnp.where(causal[kb * BLK : (kb + 1) * BLK], part, -jnp.inf)
            parts.append(part)
        scores = jnp.concatenate(parts, axis=0)
        shifted = jnp.exp2(scores - jnp.max(scores, axis=0, keepdims=True))
        p_ref[head] = (shifted * (1.0 / jnp.sum(shifted, axis=0, keepdims=True))).astype(BF16)


def outs_kernel(heads, p_ref, *refs):
    kv_refs, o_ref = refs[:-1], refs[-1]
    for head in range(heads):
        turned = contract(value_rows(kv_refs, head).T, p_ref[head], ((1,), (0,))).astype(BF16)
        store_rows(o_ref, head * HEAD_COLS, turned)


def overlaps(sends, first, count):
    begin, end = first * GROUP, (first + count) * GROUP
    return [at for at, (start, size) in enumerate(sends) if start < end and start + size > begin]


def put_pieces(sends, first, split, grad_ref, piece_refs):
    here = lax.axis_index("head")
    begin, width = first * GROUP, grad_ref.shape[1] // HD
    for at, index in enumerate(overlaps(sends, first, width // GROUP)):
        start, size = sends[index]
        low, high = max(start, begin), min(start + size, begin + width)
        for step in range(split):
            piece = piece_refs[at * split + step]
            rows = piece.shape[0]
            source = lax.rem(here + split - step, split)
            grad_ref[
                pl.ds(pl.multiple_of(source * rows, rows), rows), (low - begin) * HD : (high - begin) * HD
            ] = piece[:, (low - start) * HD : (high - start) * HD]


def head_grads(head, grads, p_ref, o_ref, q_ref, value_rows, first, last):
    queries, outs = head_rows(q_ref, head), head_rows(o_ref, head)
    delta = (grads.astype(F32) * outs.astype(F32)).astype(BF16)
    weights = p_ref[head, first:last]
    left = jnp.concatenate([value_rows, jnp.full(value_rows.shape, -1, BF16)], axis=1)
    centred = contract(left, jnp.concatenate([grads, delta], axis=1), ((1,), (1,)))
    score_grad = (weights.astype(F32) * centred).astype(BF16)
    key_part = contract(score_grad, queries, ((1,), (0,))) * SCALE
    value_part = contract(weights, grads, ((1,), (0,)))
    return score_grad, key_part, value_part


def put_query_grad(head, keys_of_head, score_grad, stage_ref, column, dq_ref, sem):
    turned = (contract(keys_of_head.T, score_grad, ((1,), (0,))) * SCALE).astype(BF16)
    store_rows(stage_ref, column, turned)
    copy = pltpu.make_async_copy(
        stage_ref.at[:, column : column + HEAD_COLS],
        dq_ref.at[:, head * HEAD_COLS : (head + 1) * HEAD_COLS],
        sem,
    )
    copy.start()
    return copy


def put_sums(ref, count, local, key_part, value_part):
    ref[:, local * HD : (local + 1) * HD] = key_part.astype(ref.dtype)
    ref[:, (count + local) * HD : (count + local + 1) * HD] = value_part.astype(ref.dtype)


def chunk_kernel(order, sends, split, first, count, aliased, p_ref, o_ref, q_ref, *refs):
    slots = len(order)
    kv_refs, refs = refs[:slots], refs[slots:]
    piece_refs, (dq_ref, keep_ref, send_ref, grad_ref, stage_ref, sem) = refs[: -6 - aliased], refs[-6:]
    put_pieces(sends, first, split, grad_ref, piece_refs)
    half = keep_ref.shape[0]
    copies = []
    for local in range(count):
        head = first + local
        score_grad, key_part, value_part = head_grads(
            head, head_rows(grad_ref, local), p_ref, o_ref, q_ref, value_rows(kv_refs, head), 0, 2 * half
        )
        keys_of_head = key_rows(kv_refs, head)
        copies.append(
            put_query_grad(
                head, keys_of_head, score_grad, stage_ref, local * HEAD_COLS, dq_ref, sem.at[local]
            )
        )
        tok_dev = q_ref.shape[0]
        for ref, slots_of in ((keep_ref, range(slots // 2)), (send_ref, range(slots // 2, slots))):
            for at, slot in enumerate(slots_of):
                part = slice(order.index(slot) * tok_dev, (order.index(slot) + 1) * tok_dev)
                put_sums(
                    ref.at[at * tok_dev : (at + 1) * tok_dev], count, local, key_part[part], value_part[part]
                )
    for copy in copies:
        copy.wait()


def half_kernel(half, sends, split, first, count, begin, p_ref, o_ref, q_ref, *refs):
    kv_refs, refs = refs[:half], refs[half:]
    if split:
        piece_refs, (ds_ref, sums_ref, grad_ref) = refs[:-3], refs[-3:]
        put_pieces(sends, first, split, grad_ref, piece_refs)
    else:
        grad_ref, ds_ref, sums_ref = refs
    for local in range(count):
        head = first + local
        score_grad, key_part, value_part = head_grads(
            head,
            head_rows(grad_ref, local),
            p_ref,
            o_ref,
            q_ref,
            value_rows(kv_refs, head),
            begin,
            begin + sums_ref.shape[0],
        )
        ds_ref[local] = score_grad
        put_sums(sums_ref, count, local, key_part, value_part)


def query_kernel(slots, first, count, aliased, near_ref, far_ref, *refs):
    kv_refs, (dq_ref, stage_ref, sem) = refs[:slots], refs[slots + aliased :]
    copies = []
    for local in range(count):
        score_grad = jnp.concatenate([near_ref[local], far_ref[local]], axis=0)
        keys_of_head = key_rows(kv_refs, first + local)
        copies.append(
            put_query_grad(
                first + local, keys_of_head, score_grad, stage_ref, local * HEAD_COLS, dq_ref, sem.at[local]
            )
        )
    for copy in copies:
        copy.wait()


def add_kernel(keep_ref, received_ref, *refs):
    total = keep_ref[...] + received_ref[...].astype(F32)
    half = refs[0].shape[0]
    refs[0][...] = total[:half]
    refs[1][...] = total[half:].astype(BF16)


def finish_kernel(groups, *refs):
    key_ref, value_ref = refs[-2:]
    for at, (first, count) in enumerate(groups):
        total = refs[2 * at][...] + refs[2 * at + 1][...].astype(F32)
        key_ref[:, first * HD : (first + count) * HD] = total[:, : count * HD].astype(BF16)
        value_ref[:, first * HD : (first + count) * HD] = total[:, count * HD :].astype(BF16)


def per_device(queries, key_states, value_states, upstream, selected):
    ctx = lax.axis_size("ctx")
    pipe, split = lax.axis_size("pipe"), lax.axis_size("head")
    tok_dev, rows_in = queries.shape[1], upstream.shape[1]
    heads = key_states.shape[2] // HD
    groups = [(0, 2), (2, 2)] if heads == 4 else [(head, 1) for head in range(heads)]
    sends = [(0, 18), (18, 14)] if heads == 4 else [(head * GROUP, GROUP) for head in range(heads)]

    def swapped(value, mask):
        return lax.ppermute(value, "ctx", [(place, place ^ mask) for place in range(ctx)])

    def across(parts):
        for step in range(split):
            route = [
                (sec * split + at, (sec - 1) % pipe * split + (at + step) % split)
                for sec in range(pipe)
                for at in range(split)
            ]
            yield lax.ppermute(parts[step], ("pipe", "head"), route)

    wide = heads * HD
    up, own_queries, own_keys, own_values = (
        in_hbm(value[0]) for value in (upstream, queries, key_states, value_states)
    )

    def cut_shapes(sends):
        return [shape((rows_in, count * HD)) for _, count in sends for _ in range(split)]

    *cut, own_kv = call(
        functools.partial(first_load_kernel, sends[:1], split, heads),
        "first_load",
        [*cut_shapes(sends[:1]), shape((tok_dev, 2 * wide))],
        [spec(HBM)] * 3,
        [spec()] * (split + 1),
        scratch_shapes=[pltpu.SemaphoreType.DMA((split + 2,))],
    )(up, own_keys, own_values)
    later = (len(sends) - 1) * split
    *more, own_queries = call(
        functools.partial(later_load_kernel, sends[1:], split, heads),
        "later_load",
        [*cut_shapes(sends[1:]), shape(queries.shape[1:])],
        [spec(HBM)] * 2,
        [spec()] * (later + 1),
        scratch_shapes=[pltpu.SemaphoreType.DMA((later + 1,))],
    )(up, own_queries)
    cut = cut + more
    pieces = [list(across(cut[at * split : (at + 1) * split])) for at in range(len(sends))]

    def pieces_of(first, count):
        return [piece for at in overlaps(sends, first, count) for piece in pieces[at]]

    masks = [1 << bit for bit in reversed(range(ctx.bit_length() - 1))]
    order = [0]
    for mask in masks:
        order = order + [slot ^ mask for slot in order]

    kv = [own_kv, *(swapped(own_kv, slot) for slot in order[1:])]

    slots = ctx
    keys, rows = slots * tok_dev, GROUP * tok_dev
    half = keys // 2
    weights = call(
        functools.partial(weights_kernel, order, heads),
        "weights",
        shape((heads, keys, rows)),
        [spec()] * (2 + slots),
        spec(),
    )(own_queries, selected[0], *kv)
    outs = call(
        functools.partial(outs_kernel, heads),
        "outs",
        shape((tok_dev, heads * HEAD_COLS)),
        [spec()] * (1 + slots),
        spec(),
    )(weights, *kv)

    given = (weights, outs, own_queries)
    query_shape = shape((tok_dev, heads * HEAD_COLS))
    query_grad = None

    def combined(keep, send, masks):
        for mask in masks:
            received = swapped(send, mask)
            if mask == masks[-1]:
                return keep, received
            part = (keep.shape[0] // 2, keep.shape[1])
            keep, send = call(
                add_kernel, "add", [shape(part, F32), shape(part)], [spec()] * 2, [spec()] * 2
            )(keep, received)

    sums, early = [], []
    for first, count in groups[:-1]:
        before = () if query_grad is None else (query_grad,)
        ins = (*given, *kv, *pieces_of(first, count))
        query_grad, keep, send = call(
            functools.partial(chunk_kernel, order, sends, split, first, count, len(before)),
            f"grads_{first}",
            [query_shape, shape((half, 2 * count * HD), F32), shape((half, 2 * count * HD))],
            [spec()] * len(ins) + [spec(HBM)] * len(before),
            [spec(HBM), spec(), spec()],
            scratch_shapes=[
                pltpu.VMEM((tok_dev, count * HEAD_COLS), BF16),
                pltpu.VMEM((tok_dev, count * HEAD_COLS), BF16),
                pltpu.SemaphoreType.DMA((count,)),
            ],
            input_output_aliases={len(ins): 0} if before else {},
        )(*ins, *before)
        early.append(send)
        sums.extend(combined(keep, send, masks))

    first, count = groups[-1]
    sum_cols = 2 * count * HD
    ins = (*given, *kv[slots // 2 :], *pieces_of(first, count), *early)
    far_scores, send, grads = call(
        functools.partial(half_kernel, slots // 2, sends, split, first, count, half),
        "sums_sent",
        [shape((count, half, rows)), shape((half, sum_cols)), shape((tok_dev, count * HEAD_COLS))],
        [spec()] * len(ins),
        [spec()] * 3,
    )(*ins)
    ins = (*given, *kv[: slots // 2], grads)
    near_scores, keep = call(
        functools.partial(half_kernel, slots // 2, sends, 0, first, count, 0),
        "sums_kept",
        [shape((count, half, rows)), shape((half, sum_cols), F32)],
        [spec()] * len(ins),
        [spec()] * 2,
        traffic=3 << 20,
    )(*ins)
    before = () if query_grad is None else (query_grad,)
    ins = (near_scores, far_scores, *kv)
    query_grad = call(
        functools.partial(query_kernel, slots, first, count, len(before)),
        "query",
        query_shape,
        [spec()] * len(ins) + [spec(HBM)] * len(before),
        spec(HBM),
        traffic=4 << 20,
        scratch_shapes=[pltpu.VMEM((tok_dev, count * HEAD_COLS), BF16), pltpu.SemaphoreType.DMA((count,))],
        input_output_aliases={len(ins): 0} if before else {},
    )(*ins, *before)
    sums.extend(combined(keep, send, masks[::-1]))

    key_grad, value_grad = call(
        functools.partial(finish_kernel, groups),
        "finish",
        [shape((tok_dev, wide))] * 2,
        [spec()] * len(sums),
        [spec()] * 2,
    )(*sums)
    return query_grad[None], key_grad[None], value_grad[None]


def solution(mesh):
    split = P("pipe", "ctx", "head")
    placed = (split, split, split, P("pipe", ("ctx", "head"), None), P("pipe", "head", "ctx", None))
    return jax.shard_map(
        per_device, mesh=mesh, in_specs=placed, out_specs=(split, split, split), check_vma=False
    )
```

time: 408 us -> 40.8 us (0.10); the launches traced: 401 us -> 40.6 us
  local copies, waits for them, and re-layouts: 127 us -> 0.69 us
  other arithmetic: 109 us -> 0 us
  matrix products: 99.2 us -> 0 us
  waiting for transfers between devices: 41.2 us -> 16.7 us
  Pallas kernels: 0 us -> 14.7 us
  blocking collectives: 14.4 us -> 0 us
    dot_general x10 -> x0, matrix products: 99.2 us -> none  [the longest x2 39.1 us: block_step(): jnp.einsum('cgij,icgh->cjh', score_grad, query_blk, preferred_element_typ...]
    gather x4 -> x0, local copies, waits for them, and re-layouts: 81.3 us -> none  [the longest x2 40.7 us: block_step(): value_rows = value_table[row_index, head_index]]
    while x12 -> x0, other arithmetic: 49.4 us -> none
    unnamed x2 -> x0, other arithmetic: 45.2 us -> none
    ppermute x4 -> x11, waiting for transfers between devices: 41.2 us -> 16.7 us  [the longest x7 10.5 us: swapped(): lax.ppermute(value, 'ctx', [(place, place ^ mask) for place in range(ctx)])]
    pallas_call x0 -> x11, Pallas kernels: none -> 14.7 us  [the longest x1 3.82 us: per_device(): call(functools.partial(weights_kernel, order, heads), 'weights', shape((h...]
    all_gather x2 -> x0, blocking collectives: 14.4 us -> none  [the longest x1 7.29 us: per_device(): lax.all_gather(value_states, 'ctx', axis=1, tiled=True)]
    sub x2 -> x0, other arithmetic: 13.8 us -> none  [block_step(): shifted = jnp.exp(scores - row_max)]
  transfers between devices with their start and end apart: 5 -> 11, of which waited for: 4 -> 6; matrix products, arithmetic and copies ran while one was open for 0% -> 0% of each run, Pallas kernels for 0% -> 31%
where the time goes in v2:
time: 40.8 us; the launch traced here: 40.6 us
  waiting for transfers between devices  16.7 us (41%)
  Pallas kernels  14.7 us (36%)
  starting transfers between devices  7.75 us (19%)
  between operations  0.74 us (2%)
  local copies, waits for them, and re-layouts  0.69 us (2%)
    ppermute x7, waiting for transfers between devices, swapped(): lax.ppermute(value, 'ctx', [(place, place ^ mask) for place in range(ctx)])  10.5 us
    ppermute x4, waiting for transfers between devices, across(): yield lax.ppermute(parts[step], ('pipe', 'head'), route)  6.19 us
    ppermute x7, starting transfers between devices, swapped(): lax.ppermute(value, 'ctx', [(place, place ^ mask) for place in range(ctx)])  4.04 us
    pallas_call x1, Pallas kernels, per_device(): call(functools.partial(weights_kernel, order, heads), 'weights', shape((h...  3.82 us
    ppermute x4, starting transfers between devices, across(): yield lax.ppermute(parts[step], ('pipe', 'head'), route)  3.71 us
    pallas_call x1, Pallas kernels, per_device(): call(functools.partial(chunk_kernel, order, sends, split, first, count, l...  3.03 us
    pallas_call x1, Pallas kernels, per_device(): call(functools.partial(later_load_kernel, sends[1:], split, heads), 'late...  1.49 us
    pallas_call x1, Pallas kernels, per_device(): call(functools.partial(query_kernel, slots, first, count, len(before)), '...  1.28 us
  transfers between devices with their start and end apart: 11, of which 6 were waited for; matrix products, arithmetic and copies ran while one was open for 0% of the time, Pallas kernels for 31%

profile of v2, /device:TPU:24, one launch (start us, length us, event | category | flops | bytes accessed | tf_op | source)
XLA Modules:
  0.0 40.6 jit_solution(18188674226763108198)
XLA Ops:
  0.6 1.2 %first_load.1 = (bf16[64,2304]{1,0:T(8,128)(2,1)S(1)}, bf16[64,2304]{1,0:T(8,128)(2,1)S(1)}, bf16[128,1024]{1,0:T(8,128)(2,1)S(1)}) custom-call(bf16[64,8192]{1,0:T(8,128)(2,1)} %bitcast.9, bf16[128,512]{1,0:T(8,128)(2,1)} %bitcast.13, bf16[128,512]{1,0:T(8,128)(2,1)} %bitcast.14), custom_call_target="tpu_custom_call" | custom-call | flops 1024 | bytes 1024 | tf_op jit(solution)/shard_map/first_load/pallas_call | solution.py:309
  1.9 1.0 %collective-permute-start.2 = (bf16[128,1024]{1,0:T(8,128)(2,1)S(1)}, bf16[128,1024]{1,0:T(8,128)(2,1)S(1)}, u32[]{:S(2)}, u32[]{:S(2)}) collective-permute-start(bf16[128,1024]{1,0:T(8,128)(2,1)S(1)} %get-tuple-element.24.refs_0_), channel_id=1, source_target_pairs={{0,6},{2,4},{4,2},{6,0},{1,7},{3,5},{5,3},{7,1},{8,14},{10,12},{12... | collective-permute-start | bytes 786440 | tf_op jit(solution)/shard_map/ppermute | solution.py:290
  2.9 0.7 %collective-permute-start.1 = (bf16[128,1024]{1,0:T(8,128)(2,1)S(1)}, bf16[128,1024]{1,0:T(8,128)(2,1)S(1)}, u32[]{:S(2)}, u32[]{:S(2)}) collective-permute-start(bf16[128,1024]{1,0:T(8,128)(2,1)S(1)} %get-tuple-element.24.refs_0_), channel_id=1, source_target_pairs={{0,2},{2,0},{4,6},{6,4},{1,3},{3,1},{5,7},{7,5},{8,10},{10,8},{12,... | collective-permute-start | bytes 786440 | tf_op jit(solution)/shard_map/ppermute | solution.py:290
  3.5 0.4 %collective-permute-start.3 = (bf16[64,2304]{1,0:T(8,128)(2,1)S(1)}, bf16[64,2304]{1,0:T(8,128)(2,1)S(1)}, u32[]{:S(2)}, u32[]{:S(2)}) collective-permute-start(bf16[64,2304]{1,0:T(8,128)(2,1)S(1)} %get-tuple-element.25), channel_id=1, source_target_pairs={{0,24},{1,25},{8,0},{9,1},{16,8},{17,9},{24,16},{25,17},{2,26},{3,... | collective-permute-start | bytes 884744 | tf_op jit(solution)/shard_map/ppermute | solution.py:299
  4.0 1.4 %collective-permute-start.4 = (bf16[64,2304]{1,0:T(8,128)(2,1)S(1)}, bf16[64,2304]{1,0:T(8,128)(2,1)S(1)}, u32[]{:S(2)}, u32[]{:S(2)}) collective-permute-start(bf16[64,2304]{1,0:T(8,128)(2,1)S(1)} %get-tuple-element.26), channel_id=1, source_target_pairs={{0,25},{1,24},{8,1},{9,0},{16,9},{17,8},{24,17},{25,16},{2,27},{3,... | collective-permute-start | bytes 884744 | tf_op jit(solution)/shard_map/ppermute | solution.py:299
  5.4 0.5 %collective-permute-start = (bf16[128,1024]{1,0:T(8,128)(2,1)S(1)}, bf16[128,1024]{1,0:T(8,128)(2,1)S(1)}, u32[]{:S(2)}, u32[]{:S(2)}) collective-permute-start(bf16[128,1024]{1,0:T(8,128)(2,1)S(1)} %get-tuple-element.24.refs_0_), channel_id=1, source_target_pairs={{0,4},{2,6},{4,0},{6,2},{1,5},{3,7},{5,1},{7,3},{8,12},{10,14},{12... | collective-permute-start | bytes 786440 | tf_op jit(solution)/shard_map/ppermute | solution.py:290
  5.9 1.5 %later_load.1 = (bf16[64,1792]{1,0:T(8,128)(2,1)S(1)}, bf16[64,1792]{1,0:T(8,128)(2,1)S(1)}, bf16[128,4096]{1,0:T(8,128)(2,1)S(1)}) custom-call(bf16[64,8192]{1,0:T(8,128)(2,1)} %bitcast.10, bf16[128,4096]{1,0:T(8,128)(2,1)} %bitcast.12), custom_call_target="tpu_custom_call" | custom-call | flops 1024 | bytes 1024 | tf_op jit(solution)/shard_map/later_load/pallas_call | solution.py:318
  7.4 3.1 %collective-permute-done.2.refs_3_.refs_1_ = bf16[128,1024]{1,0:T(8,128)(2,1)S(1)} collective-permute-done((bf16[128,1024]{1,0:T(8,128)(2,1)S(1)}, bf16[128,1024]{1,0:T(8,128)(2,1)S(1)}, u32[]{:S(2)}, u32[]{:S(2)}) %collective-permute-start.2) | collective-permute-done | bytes 262176 | tf_op jit(solution)/shard_map/ppermute | solution.py:290
  10.5 0.4 %collective-permute-start.5 = (bf16[64,1792]{1,0:T(8,128)(2,1)S(1)}, bf16[64,1792]{1,0:T(8,128)(2,1)S(1)}, u32[]{:S(2)}, u32[]{:S(2)}) collective-permute-start(bf16[64,1792]{1,0:T(8,128)(2,1)S(1)} %get-tuple-element.27), channel_id=1, source_target_pairs={{0,24},{1,25},{8,0},{9,1},{16,8},{17,9},{24,16},{25,17},{2,26},{3,... | collective-permute-start | bytes 688136 | tf_op jit(solution)/shard_map/ppermute | solution.py:299
  10.9 0.0 collective-permute-done.1.refs_2_.refs_0_
  10.9 1.4 %collective-permute-start.6 = (bf16[64,1792]{1,0:T(8,128)(2,1)S(1)}, bf16[64,1792]{1,0:T(8,128)(2,1)S(1)}, u32[]{:S(2)}, u32[]{:S(2)}) collective-permute-start(bf16[64,1792]{1,0:T(8,128)(2,1)S(1)} %get-tuple-element.28), channel_id=1, source_target_pairs={{0,25},{1,24},{8,1},{9,0},{16,9},{17,8},{24,17},{25,16},{2,27},{3,... | collective-permute-start | bytes 688136 | tf_op jit(solution)/shard_map/ppermute | solution.py:299
  12.3 3.8 %collective-permute-done.refs_1_ = bf16[128,1024]{1,0:T(8,128)(2,1)S(1)} collective-permute-done((bf16[128,1024]{1,0:T(8,128)(2,1)S(1)}, bf16[128,1024]{1,0:T(8,128)(2,1)S(1)}, u32[]{:S(2)}, u32[]{:S(2)}) %collective-permute-start) | collective-permute-done | bytes 262176 | tf_op jit(solution)/shard_map/ppermute | solution.py:290
  16.2 0.0 copy-start
  16.2 0.7 %copy-done = s32[1,4,2,8]{3,2,1,0:T(2,128)S(1)} copy-done((s32[1,4,2,8]{3,2,1,0:T(2,128)S(1)}, s32[1,4,2,8]{3,2,1,0:T(2,128)}, u32[]{:S(2)}) %copy-start) | copy-done | bytes 280
  16.8 3.8 %weights.1.p_ref = bf16[4,512,1024]{2,1,0:T(8,128)(2,1)S(1)} custom-call(bf16[128,4096]{1,0:T(8,128)(2,1)S(1)} %get-tuple-element.23.q_ref, s32[4,2,8]{2,1,0:T(2,128)S(1)} %bitcast.8, bf16[128,1024]{1,0:T(8,128)(2,1)S(1)} %get-tuple-element.24.refs_0_, bf16[128,1024]{1,0:T(8,128)(2,1)S(1)} %collective-permute-done.refs_1_, ...), custom_call_target="tpu_custom_call" | custom-call | flops 1024 | bytes 1024 | tf_op jit(solution)/shard_map/weights/pallas_call | solution.py:342
  20.7 0.8 %outs.1.o_ref = bf16[128,4096]{1,0:T(8,128)(2,1)S(1)} custom-call(bf16[4,512,1024]{2,1,0:T(8,128)(2,1)S(1)} %weights.1.p_ref, bf16[128,1024]{1,0:T(8,128)(2,1)S(1)} %get-tuple-element.24.refs_0_, bf16[128,1024]{1,0:T(8,128)(2,1)S(1)} %collective-permute-done.refs_1_, bf16[128,1024]{1,0:T(8,128)(2,1)S(1)} %collective-permute-done.1.refs_2_.refs_0_, ...), custom_call_target="tpu_custom_call" | custom-call | flops 1024 | bytes 1024 | tf_op jit(solution)/shard_map/outs/pallas_call | solution.py:349
  21.5 0.0 collective-permute-done.3.refs_4_.refs_2_
  21.5 1.0 %collective-permute-done.4.refs_5_.refs_3_ = bf16[64,2304]{1,0:T(8,128)(2,1)S(1)} collective-permute-done((bf16[64,2304]{1,0:T(8,128)(2,1)S(1)}, bf16[64,2304]{1,0:T(8,128)(2,1)S(1)}, u32[]{:S(2)}, u32[]{:S(2)}) %collective-permute-start.4) | collective-permute-done | bytes 294944 | tf_op jit(solution)/shard_map/ppermute | solution.py:299
  22.5 3.0 %grads_0.1 = (bf16[128,4096]{1,0:T(8,128)(2,1)}, f32[256,512]{1,0:T(8,128)S(1)}, bf16[256,512]{1,0:T(8,128)(2,1)S(1)}) custom-call(bf16[4,512,1024]{2,1,0:T(8,128)(2,1)S(1)} %weights.1.p_ref, bf16[128,4096]{1,0:T(8,128)(2,1)S(1)} %outs.1.o_ref, bf16[128,4096]{1,0:T(8,128)(2,1)S(1)} %get-tuple-element.23.q_ref, ...), custom_call_target="tpu_custom_call" | custom-call | flops 1024 | bytes 1024 | tf_op jit(solution)/shard_map/grads_0/pallas_call | solution.py:375
  25.5 0.6 %collective-permute-start.7 = (bf16[256,512]{1,0:T(8,128)(2,1)S(1)}, bf16[256,512]{1,0:T(8,128)(2,1)S(1)}, u32[]{:S(2)}, u32[]{:S(2)}) collective-permute-start(bf16[256,512]{1,0:T(8,128)(2,1)S(1)} %get-tuple-element.29.refs_6_), channel_id=1, source_target_pairs={{0,4},{2,6},{4,0},{6,2},{1,5},{3,7},{5,1},{7,3},{8,12},{10,14},{12... | collective-permute-start | bytes 786440 | tf_op jit(solution)/shard_map/ppermute | solution.py:290
  26.1 0.3 collective-permute-done.5.refs_4_
  26.4 4.9 %collective-permute-done.6.refs_5_ = bf16[64,1792]{1,0:T(8,128)(2,1)S(1)} collective-permute-done((bf16[64,1792]{1,0:T(8,128)(2,1)S(1)}, bf16[64,1792]{1,0:T(8,128)(2,1)S(1)}, u32[]{:S(2)}, u32[]{:S(2)}) %collective-permute-start.6) | collective-permute-done | bytes 229408 | tf_op jit(solution)/shard_map/ppermute | solution.py:299
  31.4 1.1 %sums_sent.1 = (bf16[2,256,1024]{2,1,0:T(8,128)(2,1)S(1)}, bf16[256,512]{1,0:T(8,128)(2,1)S(1)}, bf16[128,2048]{1,0:T(8,128)(2,1)S(1)}) custom-call(bf16[4,512,1024]{2,1,0:T(8,128)(2,1)S(1)} %weights.1.p_ref, bf16[128,4096]{1,0:T(8,128)(2,1)S(1)} %outs.1.o_ref, bf16[128,4096]{1,0:T(8,128)(2,1)S(1)} %get-tuple-element.23.q_ref, ...), custom_call_target="tpu_custom_call" | custom-call | flops 1024 | bytes 1024 | tf_op jit(solution)/shard_map/sums_sent/pallas_call | solution.py:394
  32.5 0.1 collective-permute-start.9
  32.6 1.1 %sums_kept.1 = (bf16[2,256,1024]{2,1,0:T(8,128)(2,1)S(1)}, f32[256,512]{1,0:T(8,128)S(1)}) custom-call(bf16[4,512,1024]{2,1,0:T(8,128)(2,1)S(1)} %weights.1.p_ref, bf16[128,4096]{1,0:T(8,128)(2,1)S(1)} %outs.1.o_ref, bf16[128,4096]{1,0:T(8,128)(2,1)S(1)} %get-tuple-element.23.q_ref, bf16[128,1024]{1,0:T(8,128)(2,1)S(1)} %get-tuple-element.24.refs_0_, ...), custom_call_target="tpu_custom_call" | custom-call | flops 1024 | bytes 3145728 | tf_op jit(solution)/shard_map/sums_kept/pallas_call | solution.py:402
  33.6 0.0 collective-permute-done.7.received_ref
  33.7 0.6 %collective-permute-start.8 = (bf16[128,512]{1,0:T(8,128)(2,1)S(1)}, bf16[128,512]{1,0:T(8,128)(2,1)S(1)}, u32[]{:S(2)}, u32[]{:S(2)}) collective-permute-start(bf16[128,512]{1,0:T(8,128)(2,1)S(1)} %get-tuple-element.36), channel_id=1, source_target_pairs={{0,2},{2,0},{4,6},{6,4},{1,3},{3,1},{5,7},{7,5},{8,10},{10,8},{12,... | collective-permute-start | bytes 393224 | tf_op jit(solution)/shard_map/ppermute | solution.py:290
  34.3 0.0 collective-permute-done.9.received_ref
  34.3 0.6 %collective-permute-start.10 = (bf16[128,512]{1,0:T(8,128)(2,1)S(1)}, bf16[128,512]{1,0:T(8,128)(2,1)S(1)}, u32[]{:S(2)}, u32[]{:S(2)}) collective-permute-start(bf16[128,512]{1,0:T(8,128)(2,1)S(1)} %get-tuple-element.40), channel_id=1, source_target_pairs={{0,4},{2,6},{4,0},{6,2},{1,5},{3,7},{5,1},{7,3},{8,12},{10,14},{12... | collective-permute-start | bytes 393224 | tf_op jit(solution)/shard_map/ppermute | solution.py:290
  34.9 1.3 %query.1 = bf16[128,4096]{1,0:T(8,128)(2,1)} custom-call(bf16[2,256,1024]{2,1,0:T(8,128)(2,1)S(1)} %get-tuple-element.31.near_ref, bf16[2,256,1024]{2,1,0:T(8,128)(2,1)S(1)} %get-tuple-element.32.far_ref, bf16[128,1024]{1,0:T(8,128)(2,1)S(1)} %get-tuple-element.24.refs_0_, ...), custom_call_target="tpu_custom_call", output_to_operand_aliasing={{}: (6, {})} | custom-call | flops 1024 | bytes 4194304 | tf_op jit(solution)/shard_map/query/pallas_call | solution.py:412
  36.2 0.0 collective-permute-done.8.refs_1_
  36.2 3.6 %collective-permute-done.10.refs_3_ = bf16[128,512]{1,0:T(8,128)(2,1)S(1)} collective-permute-done((bf16[128,512]{1,0:T(8,128)(2,1)S(1)}, bf16[128,512]{1,0:T(8,128)(2,1)S(1)}, u32[]{:S(2)}, u32[]{:S(2)}) %collective-permute-start.10) | collective-permute-done | bytes 131104 | tf_op jit(solution)/shard_map/ppermute | solution.py:290
  39.8 0.7 %finish.1 = (bf16[128,512]{1,0:T(8,128)(2,1)}, bf16[128,512]{1,0:T(8,128)(2,1)}) custom-call(f32[128,512]{1,0:T(8,128)S(1)} %get-tuple-element.35.refs_0_, bf16[128,512]{1,0:T(8,128)(2,1)S(1)} %collective-permute-done.8.refs_1_, f32[128,512]{1,0:T(8,128)S(1)} %get-tuple-element.39.refs_2_, bf16[128,512]{1,0:T(8,128)(2,1)S(1)} %collective-permute-done.10.refs_3_), custom_call_target="tpu_custom_call" | custom-call | flops 1024 | bytes 1024 | tf_op jit(solution)/shard_map/finish/pallas_call | solution.py:424
  (2 shorter events, 0.1 us)
Async XLA Ops:
  1.9 8.6 %collective-permute-start.2 = (bf16[128,1024]{1,0:T(8,128)(2,1)S(1)}, bf16[128,1024]{1,0:T(8,128)(2,1)S(1)}, u32[]{:S(2)}, u32[]{:S(2)}) collective-permute-start(bf16[128,1024]{1,0:T(8,128)(2,1)S(1)} %get-tuple-element.24.refs_0_), channel_id=1, source_target_pairs={{0,6},{2,4},{4,2},{6,0},{1,7},{3,5},{5,3},{7,1},{8,14},{10,12},{12... | collective-permute-start | bytes 786440 | tf_op jit(solution)/shard_map/ppermute | solution.py:290
  2.9 8.1 %collective-permute-start.1 = (bf16[128,1024]{1,0:T(8,128)(2,1)S(1)}, bf16[128,1024]{1,0:T(8,128)(2,1)S(1)}, u32[]{:S(2)}, u32[]{:S(2)}) collective-permute-start(bf16[128,1024]{1,0:T(8,128)(2,1)S(1)} %get-tuple-element.24.refs_0_), channel_id=1, source_target_pairs={{0,2},{2,0},{4,6},{6,4},{1,3},{3,1},{5,7},{7,5},{8,10},{10,8},{12,... | collective-permute-start | bytes 786440 | tf_op jit(solution)/shard_map/ppermute | solution.py:290
  3.5 18.0 %collective-permute-start.3 = (bf16[64,2304]{1,0:T(8,128)(2,1)S(1)}, bf16[64,2304]{1,0:T(8,128)(2,1)S(1)}, u32[]{:S(2)}, u32[]{:S(2)}) collective-permute-start(bf16[64,2304]{1,0:T(8,128)(2,1)S(1)} %get-tuple-element.25), channel_id=1, source_target_pairs={{0,24},{1,25},{8,0},{9,1},{16,8},{17,9},{24,16},{25,17},{2,26},{3,... | collective-permute-start | bytes 884744 | tf_op jit(solution)/shard_map/ppermute | solution.py:299
  4.0 18.5 %collective-permute-start.4 = (bf16[64,2304]{1,0:T(8,128)(2,1)S(1)}, bf16[64,2304]{1,0:T(8,128)(2,1)S(1)}, u32[]{:S(2)}, u32[]{:S(2)}) collective-permute-start(bf16[64,2304]{1,0:T(8,128)(2,1)S(1)} %get-tuple-element.26), channel_id=1, source_target_pairs={{0,25},{1,24},{8,1},{9,0},{16,9},{17,8},{24,17},{25,16},{2,27},{3,... | collective-permute-start | bytes 884744 | tf_op jit(solution)/shard_map/ppermute | solution.py:299
  5.4 10.8 %collective-permute-start = (bf16[128,1024]{1,0:T(8,128)(2,1)S(1)}, bf16[128,1024]{1,0:T(8,128)(2,1)S(1)}, u32[]{:S(2)}, u32[]{:S(2)}) collective-permute-start(bf16[128,1024]{1,0:T(8,128)(2,1)S(1)} %get-tuple-element.24.refs_0_), channel_id=1, source_target_pairs={{0,4},{2,6},{4,0},{6,2},{1,5},{3,7},{5,1},{7,3},{8,12},{10,14},{12... | collective-permute-start | bytes 786440 | tf_op jit(solution)/shard_map/ppermute | solution.py:290
  10.5 16.0 %collective-permute-start.5 = (bf16[64,1792]{1,0:T(8,128)(2,1)S(1)}, bf16[64,1792]{1,0:T(8,128)(2,1)S(1)}, u32[]{:S(2)}, u32[]{:S(2)}) collective-permute-start(bf16[64,1792]{1,0:T(8,128)(2,1)S(1)} %get-tuple-element.27), channel_id=1, source_target_pairs={{0,24},{1,25},{8,0},{9,1},{16,8},{17,9},{24,16},{25,17},{2,26},{3,... | collective-permute-start | bytes 688136 | tf_op jit(solution)/shard_map/ppermute | solution.py:299
  10.9 20.4 %collective-permute-start.6 = (bf16[64,1792]{1,0:T(8,128)(2,1)S(1)}, bf16[64,1792]{1,0:T(8,128)(2,1)S(1)}, u32[]{:S(2)}, u32[]{:S(2)}) collective-permute-start(bf16[64,1792]{1,0:T(8,128)(2,1)S(1)} %get-tuple-element.28), channel_id=1, source_target_pairs={{0,25},{1,24},{8,1},{9,0},{16,9},{17,8},{24,17},{25,16},{2,27},{3,... | collective-permute-start | bytes 688136 | tf_op jit(solution)/shard_map/ppermute | solution.py:299
  16.2 0.7 %copy-start = (s32[1,4,2,8]{3,2,1,0:T(2,128)S(1)}, s32[1,4,2,8]{3,2,1,0:T(2,128)}, u32[]{:S(2)}) copy-start(s32[1,4,2,8]{3,2,1,0:T(2,128)} %param.9) | copy-start | bytes 772
  25.5 8.1 %collective-permute-start.7 = (bf16[256,512]{1,0:T(8,128)(2,1)S(1)}, bf16[256,512]{1,0:T(8,128)(2,1)S(1)}, u32[]{:S(2)}, u32[]{:S(2)}) collective-permute-start(bf16[256,512]{1,0:T(8,128)(2,1)S(1)} %get-tuple-element.29.refs_6_), channel_id=1, source_target_pairs={{0,4},{2,6},{4,0},{6,2},{1,5},{3,7},{5,1},{7,3},{8,12},{10,14},{12... | collective-permute-start | bytes 786440 | tf_op jit(solution)/shard_map/ppermute | solution.py:290
  32.5 1.8 %collective-permute-start.9 = (bf16[256,512]{1,0:T(8,128)(2,1)S(1)}, bf16[256,512]{1,0:T(8,128)(2,1)S(1)}, u32[]{:S(2)}, u32[]{:S(2)}) collective-permute-start(bf16[256,512]{1,0:T(8,128)(2,1)S(1)} %get-tuple-element.38), channel_id=1, source_target_pairs={{0,2},{2,0},{4,6},{6,4},{1,3},{3,1},{5,7},{7,5},{8,10},{10,8},{12,... | collective-permute-start | bytes 786440 | tf_op jit(solution)/shard_map/ppermute | solution.py:290
  33.7 2.5 %collective-permute-start.8 = (bf16[128,512]{1,0:T(8,128)(2,1)S(1)}, bf16[128,512]{1,0:T(8,128)(2,1)S(1)}, u32[]{:S(2)}, u32[]{:S(2)}) collective-permute-start(bf16[128,512]{1,0:T(8,128)(2,1)S(1)} %get-tuple-element.36), channel_id=1, source_target_pairs={{0,2},{2,0},{4,6},{6,4},{1,3},{3,1},{5,7},{7,5},{8,10},{10,8},{12,... | collective-permute-start | bytes 393224 | tf_op jit(solution)/shard_map/ppermute | solution.py:290
  34.3 5.5 %collective-permute-start.10 = (bf16[128,512]{1,0:T(8,128)(2,1)S(1)}, bf16[128,512]{1,0:T(8,128)(2,1)S(1)}, u32[]{:S(2)}, u32[]{:S(2)}) collective-permute-start(bf16[128,512]{1,0:T(8,128)(2,1)S(1)} %get-tuple-element.40), channel_id=1, source_target_pairs={{0,4},{2,6},{4,0},{6,2},{1,5},{3,7},{5,1},{7,3},{8,12},{10,14},{12... | collective-permute-start | bytes 393224 | tf_op jit(solution)/shard_map/ppermute | solution.py:290

commit v3 on v0

v3 whole, which is shorter than its diff:
```python
import functools

import jax
import jax.numpy as jnp
from jax import lax
from jax.experimental import pallas as pl
from jax.experimental.pallas import tpu as pltpu
from jax.sharding import PartitionSpec as P

HD = 128
BLK = 64
GROUP = 8
HEAD_COLS = GROUP * HD
LOG2E = 1.4426950408889634
SCALE = HD**-0.5
VMEM = pltpu.MemorySpace.VMEM
HBM = pltpu.MemorySpace.HBM
BF16 = jnp.bfloat16
F32 = jnp.float32


def spec(space=VMEM):
    return pl.BlockSpec(memory_space=space)


def in_hbm(value):
    return pltpu.with_memory_space_constraint(value, HBM)


def shape(dims, dtype=BF16):
    return jax.ShapeDtypeStruct(dims, dtype)


def call(body, name, out_shape, in_specs, out_specs, **rest):
    return pl.pallas_call(
        body,
        out_shape=out_shape,
        in_specs=in_specs,
        out_specs=out_specs,
        name=name,
        cost_estimate=pl.CostEstimate(flops=1024, bytes_accessed=1024, transcendentals=0),
        compiler_params=pltpu.CompilerParams(vmem_limit_bytes=24 << 20),
        **rest,
    )


def contract(a, b, dims):
    return lax.dot_general(a, b, (dims, ((), ())), preferred_element_type=F32)


def head_rows(ref, head):
    first = head * HEAD_COLS
    return jnp.concatenate([ref[:, first + g * HD : first + (g + 1) * HD] for g in range(GROUP)], axis=0)


def key_rows(kv_refs, head):
    return jnp.concatenate([ref[:, head * HD : (head + 1) * HD] for ref in kv_refs], axis=0)


def value_rows(kv_refs, head):
    first = kv_refs[0].shape[1] // 2 + head * HD
    return jnp.concatenate([ref[:, first : first + HD] for ref in kv_refs], axis=0)


def store_rows(ref, column, turned):
    rows = ref.shape[0]
    for g in range(GROUP):
        ref[:, column + g * HD : column + (g + 1) * HD] = turned[:, g * rows : (g + 1) * rows].T


def run_copies(copies, sem):
    copies = [pltpu.make_async_copy(src, dst, sem.at[at]) for at, (src, dst) in enumerate(copies)]
    for copy in copies:
        copy.start()
    for copy in copies:
        copy.wait()


def cut_copies(sends, split, heads, up_ref, piece_refs):
    here = lax.axis_index("head")
    copies = []
    for at, (first, count) in enumerate(sends):
        for step in range(split):
            target = lax.rem(here + step, split)
            start = pl.multiple_of((target * heads * GROUP + first) * HD, HD)
            copies.append((up_ref.at[:, pl.ds(start, count * HD)], piece_refs[at * split + step]))
    return copies


def first_load_kernel(sends, split, heads, up_ref, k_ref, v_ref, *refs):
    *piece_refs, kv_out, sem = refs
    wide = k_ref.shape[1]
    copies = cut_copies(sends, split, heads, up_ref, piece_refs)
    run_copies([*copies, (k_ref, kv_out.at[:, :wide]), (v_ref, kv_out.at[:, wide:])], sem)


def later_load_kernel(sends, split, heads, others, up_ref, q_ref, *refs):
    other_refs, (*piece_refs, q_out), other_outs, sem = (
        refs[:others],
        refs[others : -1 - others],
        refs[-1 - others : -1],
        refs[-1],
    )
    copies = cut_copies(sends, split, heads, up_ref, piece_refs)
    run_copies([*copies, *zip(other_refs, other_outs), (q_ref, q_out)], sem)


def overlaps(sends, first, count):
    begin, end = first * GROUP, (first + count) * GROUP
    return [at for at, (start, size) in enumerate(sends) if start < end and start + size > begin]


def put_pieces(sends, first, split, grad_ref, piece_refs):
    here = lax.axis_index("head")
    begin, width = first * GROUP, grad_ref.shape[1] // HD
    for at, index in enumerate(overlaps(sends, first, width // GROUP)):
        start, size = sends[index]
        low, high = max(start, begin), min(start + size, begin + width)
        for step in range(split):
            piece = piece_refs[at * split + step]
            rows = piece.shape[0]
            source = lax.rem(here + split - step, split)
            grad_ref[
                pl.ds(pl.multiple_of(source * rows, rows), rows), (low - begin) * HD : (high - begin) * HD
            ] = piece[:, (low - start) * HD : (high - start) * HD]


def block_bias(slots, selected_ref, head, tok_dev):
    blocks = tok_dev // BLK
    here = lax.axis_index("ctx")
    at = lax.broadcasted_iota(jnp.int32, (slots * blocks, 1), 0)
    key_block = (here ^ (at // blocks)) * blocks + at % blocks
    columns = []
    for qb in range(blocks):
        hit = jnp.where(selected_ref[head, qb : qb + 1, :] == key_block, 1, 0)
        chosen = jnp.max(hit, axis=1, keepdims=True) > 0
        bias = jnp.where(chosen & (key_block <= here * blocks + qb), 0.0, -jnp.inf)
        columns.append(jnp.broadcast_to(bias, (slots * blocks, BLK)))
    return jnp.concatenate(columns * GROUP, axis=1)


def weights_kernel(slots, heads, q_ref, selected_ref, *refs):
    kv_refs, (p_ref, o_ref) = refs[:slots], refs[slots:]
    tok_dev = q_ref.shape[0]
    rows = GROUP * tok_dev
    key_at = lax.broadcasted_iota(jnp.int32, (tok_dev, rows), 0)
    query_at = lax.broadcasted_iota(jnp.int32, (tok_dev, rows), 1) % tok_dev
    causal = key_at <= query_at
    for head in range(heads):
        bias = block_bias(slots, selected_ref, head, tok_dev)
        scores = contract(key_rows(kv_refs, head), head_rows(q_ref, head), ((1,), (1,)))
        scores = scores * (SCALE * LOG2E)
        parts = []
        for kb in range(slots * tok_dev // BLK):
            part = scores[kb * BLK : (kb + 1) * BLK] + bias[kb : kb + 1]
            if kb * BLK < tok_dev:
                part = jnp.where(causal[kb * BLK : (kb + 1) * BLK], part, -jnp.inf)
            parts.append(part)
        scores = jnp.concatenate(parts, axis=0)
        shifted = jnp.exp2(scores - jnp.max(scores, axis=0, keepdims=True))
        weights = (shifted * (1.0 / jnp.sum(shifted, axis=0, keepdims=True))).astype(BF16)
        p_ref[head] = weights
        turned = contract(value_rows(kv_refs, head).T, weights, ((1,), (0,))).astype(BF16)
        store_rows(o_ref, head * HEAD_COLS, turned)


def sums_kernel(slots, first, count, sends, split, before, layout, p_ref, o_ref, q_ref, *refs):
    begin, end = slots
    kv_refs, refs = refs[: end - begin], refs[end - begin :]
    if before:
        for ref, done_ref, (_, _, kinds) in zip(refs[-len(layout) :], refs, layout):
            for at in range(len(kinds)):
                to = at * (before + count) * HD
                ref[:, to : to + before * HD] = done_ref[:, at * before * HD : (at + 1) * before * HD]
        refs = refs[len(layout) :]
    if split:
        piece_refs = refs[: -2 - len(layout)]
        grad_ref, ds_ref, *sum_refs = refs[-2 - len(layout) :]
        put_pieces(sends, first, split, grad_ref, piece_refs)
    else:
        grad_ref, ds_ref, *sum_refs = refs[0], *refs[-1 - len(layout) :]
    tok_dev = q_ref.shape[0]
    for local in range(count):
        head = first + local
        grads, queries, outs = head_rows(grad_ref, local), head_rows(q_ref, head), head_rows(o_ref, head)
        delta = (grads.astype(F32) * outs.astype(F32)).astype(BF16)
        weights = p_ref[head, begin * tok_dev : end * tok_dev]
        values = value_rows(kv_refs, head)
        left = jnp.concatenate([values, jnp.full(values.shape, -1, BF16)], axis=1)
        centred = contract(left, jnp.concatenate([grads, delta], axis=1), ((1,), (1,)))
        score_grad = (weights.astype(F32) * centred).astype(BF16)
        ds_ref[local] = score_grad
        sums = {
            "key": contract(score_grad, queries, ((1,), (0,))) * SCALE,
            "value": contract(weights, grads, ((1,), (0,))),
        }
        for ref, (from_slot, to_slot, kinds) in zip(sum_refs, layout):
            for at, kind in enumerate(kinds):
                column = (at * (before + count) + before + local) * HD
                part = sums[kind][(from_slot - begin) * tok_dev : (to_slot - begin) * tok_dev]
                ref[:, column : column + HD] = part.astype(ref.dtype)


def query_kernel(slots, places, parts, *refs):
    ds_refs, kv_refs, (dq_ref, stage_ref, sem) = refs[:parts], refs[parts : parts + slots], refs[-3:]
    copies = []
    for head, (found, row) in enumerate(places):
        score_grad = jnp.concatenate([ds_refs[at][row] for at in found], axis=0)
        turned = (contract(key_rows(kv_refs, head).T, score_grad, ((1,), (0,))) * SCALE).astype(BF16)
        store_rows(stage_ref, head * HEAD_COLS, turned)
        columns = slice(head * HEAD_COLS, (head + 1) * HEAD_COLS)
        copies.append(
            pltpu.make_async_copy(stage_ref.at[:, columns], dq_ref.at[:, columns], sem.at[head])
        )
        copies[-1].start()
    for copy in copies:
        copy.wait()


def add_kernel(outs, keep_ref, received_ref, *refs):
    total = keep_ref[...] + received_ref[...].astype(F32)
    done = 0
    for ref in refs[-outs:]:
        ref[...] = total[done : done + ref.shape[0]].astype(ref.dtype)
        done += ref.shape[0]


def finish_kernel(groups, counts, *refs):
    key_ref, value_ref = refs[-2:]
    refs = list(refs[:-2])
    for (first, count), (whole, halves) in zip(groups, counts):
        parts, refs = refs[: whole + 2 * halves], refs[whole + 2 * halves :]
        width = count * HD
        keys = [ref[:, :width] for ref in parts[:whole]] + [ref[...] for ref in parts[whole::2]]
        values = [ref[:, width:] for ref in parts[:whole]] + [ref[...] for ref in parts[whole + 1 :: 2]]
        for ref, found in ((key_ref, keys), (value_ref, values)):
            total = sum(part.astype(F32) for part in found[1:]) + found[0]
            ref[:, first * HD : (first + count) * HD] = total.astype(BF16)


def per_device(queries, key_states, value_states, upstream, selected):
    slots = lax.axis_size("ctx")
    pipe, split = lax.axis_size("pipe"), lax.axis_size("head")
    tok_dev, rows_in = queries.shape[1], upstream.shape[1]
    heads = key_states.shape[2] // HD
    wide, rows = heads * HD, GROUP * tok_dev
    paired = heads == 4 and slots == 4
    groups = [(0, 2), (2, 2)] if paired else [(0, heads)]
    sends = [(0, 24), (24, 8)] if paired else [(0, heads * GROUP)]

    def swapped(value, mask):
        return lax.ppermute(value, "ctx", [(place, place ^ mask) for place in range(slots)])

    def across(part, step):
        route = [
            (sec * split + at, (sec - 1) % pipe * split + (at + step) % split)
            for sec in range(pipe)
            for at in range(split)
        ]
        return lax.ppermute(part, ("pipe", "head"), route)

    up, own_queries, own_keys, own_values = (
        in_hbm(value[0]) for value in (upstream, queries, key_states, value_states)
    )

    def cut_shapes(sends):
        return [shape((rows_in, count * HD)) for _, count in sends for _ in range(split)]

    *cut, own_kv = call(
        functools.partial(first_load_kernel, sends[:1], split, heads),
        "first_load",
        [*cut_shapes(sends[:1]), shape((tok_dev, 2 * wide))],
        [spec(HBM)] * 3,
        [spec()] * (split + 1),
        scratch_shapes=[pltpu.SemaphoreType.DMA((split + 2,))],
    )(up, own_keys, own_values)

    def gathered(own):
        found = {0: own}
        for mask in [1 << bit for bit in reversed(range(slots.bit_length() - 1))]:
            found.update({slot ^ mask: swapped(part, mask) for slot, part in found.items()})
        return [found[slot] for slot in range(1, slots)]

    def alone(own):
        return [own] * (slots - 1)

    others = slots - 1
    received = lax.cond(lax.axis_index("ctx") < slots, gathered, alone, own_kv)
    later = (len(sends) - 1) * split
    more = call(
        functools.partial(later_load_kernel, sends[1:], split, heads, others),
        "later_load",
        [*cut_shapes(sends[1:]), shape(queries.shape[1:])] + [shape((tok_dev, 2 * wide))] * others,
        [spec(HBM)] * (2 + others),
        [spec()] * (later + 1 + others),
        scratch_shapes=[pltpu.SemaphoreType.DMA((later + 1 + others,))],
    )(up, own_queries, *(in_hbm(part) for part in received))
    own_queries, kv = more[later], [own_kv, *more[later + 1 :]]
    cut = [*cut, *more[:later]]
    pieces = [
        [across(cut[at * split + step], step) for step in range(split)] for at in range(len(sends))
    ]

    def pieces_of(first, count):
        return [piece for at in overlaps(sends, first, count) for piece in pieces[at]]

    ins = (own_queries, selected[0], *kv)
    weights, outs = call(
        functools.partial(weights_kernel, slots, heads),
        "weights",
        [shape((heads, slots * tok_dev, rows)), shape((tok_dev, heads * HEAD_COLS))],
        [spec()] * len(ins),
        [spec()] * 2,
    )(*ins)

    def sums_of(name, group, span, layout, grads=None, done=()):
        first, count = group
        used = pieces_of(first, count) if grads is None else [grads]
        before = done[0].shape[1] // (len(layout[0][2]) * HD) if done else 0
        ins = (weights, outs, own_queries, *kv[span[0] : span[1]], *done, *used)
        results = [shape((tok_dev, count * HEAD_COLS))] if grads is None else []
        results.append(shape((count, (span[1] - span[0]) * tok_dev, rows)))
        results.extend(
            shape(((to - at) * tok_dev, len(kinds) * (before + count) * HD), dtype)
            for at, to, kinds, dtype in layout
        )
        return call(
            functools.partial(
                sums_kernel,
                span,
                first,
                count,
                sends,
                0 if grads is not None else split,
                before,
                [part[:3] for part in layout],
            ),
            name,
            results,
            [spec()] * len(ins),
            [spec()] * len(results),
        )(*ins)

    def query_of(score_grads, places):
        ins = (*score_grads, *kv)
        return call(
            functools.partial(query_kernel, slots, places, len(score_grads)),
            "query",
            shape((tok_dev, heads * HEAD_COLS)),
            [spec()] * len(ins),
            spec(HBM),
            scratch_shapes=[
                pltpu.VMEM((tok_dev, heads * HEAD_COLS), BF16),
                pltpu.SemaphoreType.DMA((heads,)),
            ],
        )(*ins)

    def added(keep, received, outs, *after):
        ins = (keep, received, *after)
        return call(
            functools.partial(add_kernel, len(outs)), "add", outs, [spec()] * len(ins), [spec()] * len(outs)
        )(*ins)

    both = ("key", "value")
    if paired:
        _, scores_a, keep, send = sums_of("sums_early", (0, 2), (0, 4), [(0, 2, both, F32), (2, 4, both, BF16)])
        part = (tok_dev, 4 * HD)
        own, send = added(keep, swapped(send, 2), [shape(part, F32), shape(part)])
        found = [own, swapped(send, 1)]

        near = [(0, 1, both, F32), (1, 2, ("key",), BF16), (1, 2, ("value",), BF16)]
        kept, sent = (2, 3, both, F32), (3, 4, both, BF16)
        _, scores_b, *near_done, keep, send = sums_of("sums_middle", (2, 1), (0, 4), [*near, kept, sent])
        grads, scores_3, send = sums_of("sums_3", (3, 1), (3, 4), [sent], done=[send])
        scores_2, keep = sums_of("sums_2", (3, 1), (2, 3), [kept], grads, [keep])
        scores_01, own, *sends_1 = sums_of("sums_01", (3, 1), (0, 2), near, grads, near_done)
        (send,) = added(keep, swapped(send, 1), [shape(part)], own)
        query_grad = query_of(
            [scores_a, scores_b, scores_01, scores_2, scores_3],
            [((0,), 0), ((0,), 1), ((1,), 0), ((2, 3, 4), 0)],
        )
        found.extend([own, swapped(send, 2), *(swapped(part, 1) for part in sends_1)])
        counts = [(2, 0), (2, 1)]
    else:
        layout = [(0, 1, both, F32)] + [(slot, slot + 1, both, BF16) for slot in range(1, slots)]
        _, scores, own, *send = sums_of("sums", groups[0], (0, slots), layout)
        query_grad = query_of([scores], [((0,), head) for head in range(heads)])
        found = [own, *(swapped(part, slot) for slot, part in enumerate(send, 1))]
        counts = [(slots, 0)]

    key_grad, value_grad = call(
        functools.partial(finish_kernel, groups, counts),
        "finish",
        [shape((tok_dev, wide))] * 2,
        [spec()] * len(found),
        [spec()] * 2,
    )(*found)
    return query_grad[None], key_grad[None], value_grad[None]


def solution(mesh):
    split = P("pipe", "ctx", "head")
    placed = (split, split, split, P("pipe", ("ctx", "head"), None), P("pipe", "head", "ctx", None))
    return jax.shard_map(
        per_device, mesh=mesh, in_specs=placed, out_specs=(split, split, split), check_vma=False
    )
```

time: 408 us -> 38.3 us (0.09); the launches traced: 401 us -> 38.2 us
  local copies, waits for them, and re-layouts: 127 us -> 0.01 us
  other arithmetic: 109 us -> 0 us
  matrix products: 99.2 us -> 0 us
  waiting for transfers between devices: 41.2 us -> 12.2 us
  blocking collectives: 14.4 us -> 0 us
  Pallas kernels: 0 us -> 14 us
    dot_general x10 -> x0, matrix products: 99.2 us -> none  [the longest x2 39.1 us: block_step(): jnp.einsum('cgij,icgh->cjh', score_grad, query_blk, preferred_element_typ...]
    gather x4 -> x0, local copies, waits for them, and re-layouts: 81.3 us -> none  [the longest x2 40.7 us: block_step(): value_rows = value_table[row_index, head_index]]
    while x12 -> x0, other arithmetic: 49.4 us -> none
    unnamed x2 -> x0, other arithmetic: 45.2 us -> none
    ppermute x4 -> x13, waiting for transfers between devices: 41.2 us -> 12.2 us  [the longest x9 10.1 us: swapped(): lax.ppermute(value, 'ctx', [(place, place ^ mask) for place in range(slot...]
    all_gather x2 -> x0, blocking collectives: 14.4 us -> none  [the longest x1 7.29 us: per_device(): lax.all_gather(value_states, 'ctx', axis=1, tiled=True)]
    pallas_call x0 -> x12, Pallas kernels: none -> 14 us  [the longest x5 4.62 us: sums_of(): call(functools.partial(sums_kernel, span, first, count, sends, 0 if grads...]
    sub x2 -> x0, other arithmetic: 13.8 us -> none  [block_step(): shifted = jnp.exp(scores - row_max)]
  transfers between devices with their start and end apart: 5 -> 13, of which waited for: 4 -> 6; matrix products, arithmetic and copies ran while one was open for 0% -> 0% of each run, Pallas kernels for 0% -> 31%
where the time goes in v3:
time: 38.3 us; the launch traced here: 38.2 us
  Pallas kernels  14 us (37%)
  waiting for transfers between devices  12.2 us (32%)
  starting transfers between devices  11.2 us (29%)
  between operations  0.77 us (2%)
    ppermute x9, waiting for transfers between devices, swapped(): lax.ppermute(value, 'ctx', [(place, place ^ mask) for place in range(slot...  10.1 us
    ppermute x4, starting transfers between devices, across(): return lax.ppermute(part, ('pipe', 'head'), route)  5.95 us
    ppermute x9, starting transfers between devices, swapped(): lax.ppermute(value, 'ctx', [(place, place ^ mask) for place in range(slot...  5.28 us
    pallas_call x5, Pallas kernels, sums_of(): call(functools.partial(sums_kernel, span, first, count, sends, 0 if grads...  4.62 us
    pallas_call x1, Pallas kernels, per_device(): call(functools.partial(weights_kernel, slots, heads), 'weights', [shape((...  4.09 us
    ppermute x4, waiting for transfers between devices, across(): return lax.ppermute(part, ('pipe', 'head'), route)  2.04 us
    pallas_call x1, Pallas kernels, per_device(): call(functools.partial(later_load_kernel, sends[1:], split, heads, others...  1.66 us
    pallas_call x1, Pallas kernels, query_of(): call(functools.partial(query_kernel, slots, places, len(score_grads)), 'q...  1.58 us
  transfers between devices with their start and end apart: 13, of which 6 were waited for; matrix products, arithmetic and copies ran while one was open for 0% of the time, Pallas kernels for 31%

profile of v3, /device:TPU:24, one launch (start us, length us, event | category | flops | bytes accessed | tf_op | source)
XLA Modules:
  0.0 38.2 jit_solution(7039859738090863519)
XLA Ops:
  0.6 0.0 copy-start
  0.6 1.2 %first_load.1 = (bf16[64,3072]{1,0:T(8,128)(2,1)S(1)}, bf16[64,3072]{1,0:T(8,128)(2,1)S(1)}, bf16[128,1024]{1,0:T(8,128)(2,1)S(1)}) custom-call(bf16[64,8192]{1,0:T(8,128)(2,1)} %bitcast.9, bf16[128,512]{1,0:T(8,128)(2,1)} %bitcast.13, bf16[128,512]{1,0:T(8,128)(2,1)} %bitcast.14), custom_call_target="tpu_custom_call" | custom-call | flops 1024 | bytes 1024 | tf_op jit(solution)/shard_map/first_load/pallas_call | solution.py:269
  1.9 0.5 %collective-permute-start.3 = (bf16[64,3072]{1,0:T(8,128)(2,1)S(1)}, bf16[64,3072]{1,0:T(8,128)(2,1)S(1)}, u32[]{:S(2)}, u32[]{:S(2)}) collective-permute-start(bf16[64,3072]{1,0:T(8,128)(2,1)S(1)} %get-tuple-element.51), channel_id=1, source_target_pairs={{0,24},{1,25},{8,0},{9,1},{16,8},{17,9},{24,16},{25,17},{2,26},{3,... | collective-permute-start | bytes 1179656 | tf_op jit(solution)/shard_map/ppermute | solution.py:260
  2.4 1.4 %collective-permute-start.4 = (bf16[64,3072]{1,0:T(8,128)(2,1)S(1)}, bf16[64,3072]{1,0:T(8,128)(2,1)S(1)}, u32[]{:S(2)}, u32[]{:S(2)}) collective-permute-start(bf16[64,3072]{1,0:T(8,128)(2,1)S(1)} %get-tuple-element.52), channel_id=1, source_target_pairs={{0,25},{1,24},{8,1},{9,0},{16,9},{17,8},{24,17},{25,16},{2,27},{3,... | collective-permute-start | bytes 1179656 | tf_op jit(solution)/shard_map/ppermute | solution.py:260
  3.8 9.5 %conditional.1 = (bf16[128,1024]{1,0:T(8,128)(2,1)}, bf16[128,1024]{1,0:T(8,128)(2,1)}, bf16[128,1024]{1,0:T(8,128)(2,1)}) conditional(s32[]{:T(128)} %convert_element_type.3, bf16[128,1024]{1,0:T(8,128)(2,1)S(1)} %get-tuple-element.41.refs_0_.refs_5_, bf16[128,1024]{1,0:T(8,128)(2,1)S(1)} %get-tuple-element.41.refs_0_.refs_5_), branch_computations={%region_0.0_spmd, %region_1.0_spmd} | conditional | bytes 3145872 | solution.py:288
  3.8 1.5 %collective-permute-start.1 = (bf16[128,1024]{1,0:T(8,128)(2,1)S(1)}, bf16[128,1024]{1,0:T(8,128)(2,1)}, u32[]{:S(2)}, u32[]{:S(2)}) collective-permute-start(bf16[128,1024]{1,0:T(8,128)(2,1)S(1)} %param.1), channel_id=1, source_target_pairs={{0,4},{2,6},{4,0},{6,2},{1,5},{3,7},{5,1},{7,3},{8,12},{10,14},{12... | collective-permute-start | bytes 786440 | tf_op jit(solution)/shard_map/cond/branch_1_fun/ppermute | solution.py:252
  5.3 0.0 collective-permute-start
  5.3 6.1 %collective-permute-done.1 = bf16[128,1024]{1,0:T(8,128)(2,1)} collective-permute-done((bf16[128,1024]{1,0:T(8,128)(2,1)S(1)}, bf16[128,1024]{1,0:T(8,128)(2,1)}, u32[]{:S(2)}, u32[]{:S(2)}) %collective-permute-start.1) | collective-permute-done | bytes 262176 | tf_op jit(solution)/shard_map/cond/branch_1_fun/ppermute | solution.py:252
  11.4 0.0 collective-permute-start.2
  11.4 0.0 collective-permute-done
  11.4 1.9 %collective-permute-done.2 = bf16[128,1024]{1,0:T(8,128)(2,1)} collective-permute-done((bf16[128,1024]{1,0:T(8,128)(2,1)}, bf16[128,1024]{1,0:T(8,128)(2,1)}, u32[]{:S(2)}, u32[]{:S(2)}) %collective-permute-start.2) | collective-permute-done | bytes 262176 | tf_op jit(solution)/shard_map/cond/branch_1_fun/ppermute | solution.py:252
  13.3 1.7 %later_load.1 = (bf16[64,1024]{1,0:T(8,128)(2,1)S(1)}, bf16[64,1024]{1,0:T(8,128)(2,1)S(1)}, bf16[128,4096]{1,0:T(8,128)(2,1)S(1)}, bf16[128,1024]{1,0:T(8,128)(...) custom-call(bf16[64,8192]{1,0:T(8,128)(2,1)} %bitcast.10, bf16[128,4096]{1,0:T(8,128)(2,1)} %bitcast.11, ...), custom_call_target="tpu_custom_call" | custom-call | flops 1024 | bytes 1024 | tf_op jit(solution)/shard_map/later_load/pallas_call | solution.py:290
  14.9 0.5 %collective-permute-start.5 = (bf16[64,1024]{1,0:T(8,128)(2,1)S(1)}, bf16[64,1024]{1,0:T(8,128)(2,1)S(1)}, u32[]{:S(2)}, u32[]{:S(2)}) collective-permute-start(bf16[64,1024]{1,0:T(8,128)(2,1)S(1)} %get-tuple-element.59), channel_id=1, source_target_pairs={{0,24},{1,25},{8,0},{9,1},{16,8},{17,9},{24,16},{25,17},{2,26},{3,... | collective-permute-start | bytes 393224 | tf_op jit(solution)/shard_map/ppermute | solution.py:260
  15.4 3.5 %collective-permute-start.6 = (bf16[64,1024]{1,0:T(8,128)(2,1)S(1)}, bf16[64,1024]{1,0:T(8,128)(2,1)S(1)}, u32[]{:S(2)}, u32[]{:S(2)}) collective-permute-start(bf16[64,1024]{1,0:T(8,128)(2,1)S(1)} %get-tuple-element.60), channel_id=1, source_target_pairs={{0,25},{1,24},{8,1},{9,0},{16,9},{17,8},{24,17},{25,16},{2,27},{3,... | collective-permute-start | bytes 393224 | tf_op jit(solution)/shard_map/ppermute | solution.py:260
  19.0 0.0 copy-done
  19.0 4.1 %weights.1 = (bf16[4,512,1024]{2,1,0:T(8,128)(2,1)S(1)}, bf16[128,4096]{1,0:T(8,128)(2,1)S(1)}) custom-call(bf16[128,4096]{1,0:T(8,128)(2,1)S(1)} %get-tuple-element.45.q_ref, s32[4,2,8]{2,1,0:T(2,128)S(1)} %bitcast.8, bf16[128,1024]{1,0:T(8,128)(2,1)S(1)} %get-tuple-element.41.refs_0_.refs_5_, bf16[128,1024]{1,0:T(8,128)(2,1)S(1)} %get-tuple-element.46.refs_1_.refs_6_, ...), custom_call_target="tpu_custom_call" | custom-call | flops 1024 | bytes 1024 | tf_op jit(solution)/shard_map/weights/pallas_call | solution.py:308
  23.1 0.0 collective-permute-done.3.refs_4_
  23.1 2.0 %collective-permute-done.4.refs_5_ = bf16[64,3072]{1,0:T(8,128)(2,1)S(1)} collective-permute-done((bf16[64,3072]{1,0:T(8,128)(2,1)S(1)}, bf16[64,3072]{1,0:T(8,128)(2,1)S(1)}, u32[]{:S(2)}, u32[]{:S(2)}) %collective-permute-start.4) | collective-permute-done | bytes 393248 | tf_op jit(solution)/shard_map/ppermute | solution.py:260
  25.1 1.9 %sums_early.1 = (bf16[128,2048]{1,0:T(8,128)(2,1)}, bf16[2,512,1024]{2,1,0:T(8,128)(2,1)S(1)}, f32[256,512]{1,0:T(8,128)S(1)}, bf16[256,512]{1,0:T(8,128)(2,1)S(1)}) custom-call(bf16[4,512,1024]{2,1,0:T(8,128)(2,1)S(1)} %get-tuple-element.49.p_ref, bf16[128,4096]{1,0:T(8,128)(2,1)S(1)} %get-tuple-element.50.o_ref, ...), custom_call_target="tpu_custom_call" | custom-call | flops 1024 | bytes 1024 | tf_op jit(solution)/shard_map/sums_early/pallas_call | solution.py:327
  27.0 1.6 %collective-permute-start.7 = (bf16[256,512]{1,0:T(8,128)(2,1)S(1)}, bf16[256,512]{1,0:T(8,128)(2,1)S(1)}, u32[]{:S(2)}, u32[]{:S(2)}) collective-permute-start(bf16[256,512]{1,0:T(8,128)(2,1)S(1)} %get-tuple-element.67), channel_id=1, source_target_pairs={{0,4},{2,6},{4,0},{6,2},{1,5},{3,7},{5,1},{7,3},{8,12},{10,14},{12... | collective-permute-start | bytes 786440 | tf_op jit(solution)/shard_map/ppermute | solution.py:252
  28.5 1.0 %sums_middle.1 = (bf16[128,1024]{1,0:T(8,128)(2,1)}, bf16[1,512,1024]{2,1,0:T(8,128)(2,1)S(1)}, f32[128,256]{1,0:T(8,128)S(1)}, bf16[128,128]{1,0:T(8,128)(2,1)S...) custom-call(bf16[4,512,1024]{2,1,0:T(8,128)(2,1)S(1)} %get-tuple-element.49.p_ref, ...), custom_call_target="tpu_custom_call" | custom-call | flops 1024 | bytes 1024 | tf_op jit(solution)/shard_map/sums_middle/pallas_call | solution.py:327
  29.6 0.0 collective-permute-done.5.refs_2_
  29.6 0.0 collective-permute-done.6.refs_3_
  29.6 0.5 %sums_3.1 = (bf16[128,1024]{1,0:T(8,128)(2,1)S(1)}, bf16[1,128,1024]{2,1,0:T(8,128)(2,1)S(1)}, bf16[128,512]{1,0:T(8,128)(2,1)S(1)}) custom-call(bf16[4,512,1024]{2,1,0:T(8,128)(2,1)S(1)} %get-tuple-element.49.p_ref, bf16[128,4096]{1,0:T(8,128)(2,1)S(1)} %get-tuple-element.50.o_ref, bf16[128,4096]{1,0:T(8,128)(2,1)S(1)} %get-tuple-element.45.q_ref, ...), custom_call_target="tpu_custom_call" | custom-call | flops 1024 | bytes 1024 | tf_op jit(solution)/shard_map/sums_3/pallas_call | solution.py:327
  30.2 0.1 collective-permute-start.9
  30.3 0.5 %sums_2.1 = (bf16[1,128,1024]{2,1,0:T(8,128)(2,1)S(1)}, f32[128,512]{1,0:T(8,128)S(1)}) custom-call(bf16[4,512,1024]{2,1,0:T(8,128)(2,1)S(1)} %get-tuple-element.49.p_ref, bf16[128,4096]{1,0:T(8,128)(2,1)S(1)} %get-tuple-element.50.o_ref, bf16[128,4096]{1,0:T(8,128)(2,1)S(1)} %get-tuple-element.45.q_ref, ...), custom_call_target="tpu_custom_call" | custom-call | flops 1024 | bytes 1024 | tf_op jit(solution)/shard_map/sums_2/pallas_call | solution.py:327
  30.8 0.6 %sums_01.1 = (bf16[1,256,1024]{2,1,0:T(8,128)(2,1)S(1)}, f32[128,512]{1,0:T(8,128)S(1)}, bf16[128,256]{1,0:T(8,128)(2,1)S(1)}, bf16[128,256]{1,0:T(8,128)(2,1)S(1)}) custom-call(bf16[4,512,1024]{2,1,0:T(8,128)(2,1)S(1)} %get-tuple-element.49.p_ref, bf16[128,4096]{1,0:T(8,128)(2,1)S(1)} %get-tuple-element.50.o_ref, ...), custom_call_target="tpu_custom_call" | custom-call | flops 1024 | bytes 1024 | tf_op jit(solution)/shard_map/sums_01/pallas_call | solution.py:327
  31.4 0.2 collective-permute-done.9.received_ref
  31.6 1.5 %collective-permute-start.10 = (bf16[128,512]{1,0:T(8,128)(2,1)S(1)}, bf16[128,512]{1,0:T(8,128)(2,1)S(1)}, u32[]{:S(2)}, u32[]{:S(2)}) collective-permute-start(bf16[128,512]{1,0:T(8,128)(2,1)S(1)} %add.3), channel_id=1, source_target_pairs={{0,4},{2,6},{4,0},{6,2},{1,5},{3,7},{5,1},{7,3},{8,12},{10,14},{12... | collective-permute-start | bytes 393224 | tf_op jit(solution)/shard_map/ppermute | solution.py:252
  33.1 0.3 collective-permute-done.7.received_ref
  33.5 0.1 collective-permute-start.8
  33.6 0.5 %collective-permute-start.11 = (bf16[128,256]{1,0:T(8,128)(2,1)S(1)}, bf16[128,256]{1,0:T(8,128)(2,1)S(1)}, u32[]{:S(2)}, u32[]{:S(2)}) collective-permute-start(bf16[128,256]{1,0:T(8,128)(2,1)S(1)} %get-tuple-element.73), channel_id=1, source_target_pairs={{0,2},{2,0},{4,6},{6,4},{1,3},{3,1},{5,7},{7,5},{8,10},{10,8},{12,... | collective-permute-start | bytes 196616 | tf_op jit(solution)/shard_map/ppermute | solution.py:252
  34.1 0.1 collective-permute-start.12
  34.1 1.6 %query.1 = bf16[128,4096]{1,0:T(8,128)(2,1)} custom-call(bf16[2,512,1024]{2,1,0:T(8,128)(2,1)S(1)} %get-tuple-element.53.refs_0_, bf16[1,512,1024]{2,1,0:T(8,128)(2,1)S(1)} %get-tuple-element.54.refs_1_, bf16[1,256,1024]{2,1,0:T(8,128)(2,1)S(1)} %get-tuple-element.62.refs_2_, bf16[1,128,1024]{2,1,0:T(8,128)(2,1)S(1)} %get-tuple-element.64.refs_3_, ...), custom_call_target="tpu_custom_call" | custom-call | flops 1024 | bytes 1024 | tf_op jit(solution)/shard_map/query/pallas_call | solution.py:346
  35.7 0.0 collective-permute-done.11.refs_4_
  35.7 0.0 collective-permute-done.12.refs_5_
  35.7 1.7 %collective-permute-done.10.refs_3_ = bf16[128,512]{1,0:T(8,128)(2,1)S(1)} collective-permute-done((bf16[128,512]{1,0:T(8,128)(2,1)S(1)}, bf16[128,512]{1,0:T(8,128)(2,1)S(1)}, u32[]{:S(2)}, u32[]{:S(2)}) %collective-permute-start.10) | collective-permute-done | bytes 131104 | tf_op jit(solution)/shard_map/ppermute | solution.py:252
  37.4 0.0 collective-permute-done.8.refs_1_
  37.4 0.7 %finish.1 = (bf16[128,512]{1,0:T(8,128)(2,1)}, bf16[128,512]{1,0:T(8,128)(2,1)}) custom-call(f32[128,512]{1,0:T(8,128)S(1)} %get-tuple-element.68.refs_0_, bf16[128,512]{1,0:T(8,128)(2,1)S(1)} %collective-permute-done.8.refs_1_, f32[128,512]{1,0:T(8,128)S(1)} %get-tuple-element.70.refs_0_.refs_2_, bf16[128,512]{1,0:T(8,128)(2,1)S(1)} %collective-permute-done.10.refs_3_, ...), custom_call_target="tpu_custom_call" | custom-call | flops 1024 | bytes 1024 | tf_op jit(solution)/shard_map/finish/pallas_call | solution.py:391
  (2 shorter events, 0.1 us)
Async XLA Ops:
  0.6 18.3 %copy-start = (s32[1,4,2,8]{3,2,1,0:T(2,128)S(1)}, s32[1,4,2,8]{3,2,1,0:T(2,128)}, u32[]{:S(2)}) copy-start(s32[1,4,2,8]{3,2,1,0:T(2,128)} %param.11) | copy-start | bytes 772
  1.9 21.2 %collective-permute-start.3 = (bf16[64,3072]{1,0:T(8,128)(2,1)S(1)}, bf16[64,3072]{1,0:T(8,128)(2,1)S(1)}, u32[]{:S(2)}, u32[]{:S(2)}) collective-permute-start(bf16[64,3072]{1,0:T(8,128)(2,1)S(1)} %get-tuple-element.51), channel_id=1, source_target_pairs={{0,24},{1,25},{8,0},{9,1},{16,8},{17,9},{24,16},{25,17},{2,26},{3,... | collective-permute-start | bytes 1179656 | tf_op jit(solution)/shard_map/ppermute | solution.py:260
  2.4 22.7 %collective-permute-start.4 = (bf16[64,3072]{1,0:T(8,128)(2,1)S(1)}, bf16[64,3072]{1,0:T(8,128)(2,1)S(1)}, u32[]{:S(2)}, u32[]{:S(2)}) collective-permute-start(bf16[64,3072]{1,0:T(8,128)(2,1)S(1)} %get-tuple-element.52), channel_id=1, source_target_pairs={{0,25},{1,24},{8,1},{9,0},{16,9},{17,8},{24,17},{25,16},{2,27},{3,... | collective-permute-start | bytes 1179656 | tf_op jit(solution)/shard_map/ppermute | solution.py:260
  3.8 7.6 %collective-permute-start.1 = (bf16[128,1024]{1,0:T(8,128)(2,1)S(1)}, bf16[128,1024]{1,0:T(8,128)(2,1)}, u32[]{:S(2)}, u32[]{:S(2)}) collective-permute-start(bf16[128,1024]{1,0:T(8,128)(2,1)S(1)} %param.1), channel_id=1, source_target_pairs={{0,4},{2,6},{4,0},{6,2},{1,5},{3,7},{5,1},{7,3},{8,12},{10,14},{12... | collective-permute-start | bytes 786440 | tf_op jit(solution)/shard_map/cond/branch_1_fun/ppermute | solution.py:252
  5.3 6.1 %collective-permute-start = (bf16[128,1024]{1,0:T(8,128)(2,1)S(1)}, bf16[128,1024]{1,0:T(8,128)(2,1)}, u32[]{:S(2)}, u32[]{:S(2)}) collective-permute-start(bf16[128,1024]{1,0:T(8,128)(2,1)S(1)} %param.1), channel_id=1, source_target_pairs={{0,2},{2,0},{4,6},{6,4},{1,3},{3,1},{5,7},{7,5},{8,10},{10,8},{12,... | collective-permute-start | bytes 786440 | tf_op jit(solution)/shard_map/cond/branch_1_fun/ppermute | solution.py:252
  11.4 1.9 %collective-permute-start.2 = (bf16[128,1024]{1,0:T(8,128)(2,1)}, bf16[128,1024]{1,0:T(8,128)(2,1)}, u32[]{:S(2)}, u32[]{:S(2)}) collective-permute-start(bf16[128,1024]{1,0:T(8,128)(2,1)} %collective-permute-done.1), channel_id=1, source_target_pairs={{0,2},{2,0},{4,6},{6,4},{1,3},{3,1},{5,7},{7,5},{8,10},{10,8},{12,... | collective-permute-start | bytes 786440 | tf_op jit(solution)/shard_map/cond/branch_1_fun/ppermute | solution.py:252
  14.9 14.7 %collective-permute-start.5 = (bf16[64,1024]{1,0:T(8,128)(2,1)S(1)}, bf16[64,1024]{1,0:T(8,128)(2,1)S(1)}, u32[]{:S(2)}, u32[]{:S(2)}) collective-permute-start(bf16[64,1024]{1,0:T(8,128)(2,1)S(1)} %get-tuple-element.59), channel_id=1, source_target_pairs={{0,24},{1,25},{8,0},{9,1},{16,8},{17,9},{24,16},{25,17},{2,26},{3,... | collective-permute-start | bytes 393224 | tf_op jit(solution)/shard_map/ppermute | solution.py:260
  15.4 14.2 %collective-permute-start.6 = (bf16[64,1024]{1,0:T(8,128)(2,1)S(1)}, bf16[64,1024]{1,0:T(8,128)(2,1)S(1)}, u32[]{:S(2)}, u32[]{:S(2)}) collective-permute-start(bf16[64,1024]{1,0:T(8,128)(2,1)S(1)} %get-tuple-element.60), channel_id=1, source_target_pairs={{0,25},{1,24},{8,1},{9,0},{16,9},{17,8},{24,17},{25,16},{2,27},{3,... | collective-permute-start | bytes 393224 | tf_op jit(solution)/shard_map/ppermute | solution.py:260
  27.0 6.4 %collective-permute-start.7 = (bf16[256,512]{1,0:T(8,128)(2,1)S(1)}, bf16[256,512]{1,0:T(8,128)(2,1)S(1)}, u32[]{:S(2)}, u32[]{:S(2)}) collective-permute-start(bf16[256,512]{1,0:T(8,128)(2,1)S(1)} %get-tuple-element.67), channel_id=1, source_target_pairs={{0,4},{2,6},{4,0},{6,2},{1,5},{3,7},{5,1},{7,3},{8,12},{10,14},{12... | collective-permute-start | bytes 786440 | tf_op jit(solution)/shard_map/ppermute | solution.py:252
  30.2 1.4 %collective-permute-start.9 = (bf16[128,512]{1,0:T(8,128)(2,1)S(1)}, bf16[128,512]{1,0:T(8,128)(2,1)S(1)}, u32[]{:S(2)}, u32[]{:S(2)}) collective-permute-start(bf16[128,512]{1,0:T(8,128)(2,1)S(1)} %get-tuple-element.72), channel_id=1, source_target_pairs={{0,2},{2,0},{4,6},{6,4},{1,3},{3,1},{5,7},{7,5},{8,10},{10,8},{12,... | collective-permute-start | bytes 393224 | tf_op jit(solution)/shard_map/ppermute | solution.py:252
  31.6 5.8 %collective-permute-start.10 = (bf16[128,512]{1,0:T(8,128)(2,1)S(1)}, bf16[128,512]{1,0:T(8,128)(2,1)S(1)}, u32[]{:S(2)}, u32[]{:S(2)}) collective-permute-start(bf16[128,512]{1,0:T(8,128)(2,1)S(1)} %add.3), channel_id=1, source_target_pairs={{0,4},{2,6},{4,0},{6,2},{1,5},{3,7},{5,1},{7,3},{8,12},{10,14},{12... | collective-permute-start | bytes 393224 | tf_op jit(solution)/shard_map/ppermute | solution.py:252
  33.5 3.9 %collective-permute-start.8 = (bf16[128,512]{1,0:T(8,128)(2,1)S(1)}, bf16[128,512]{1,0:T(8,128)(2,1)S(1)}, u32[]{:S(2)}, u32[]{:S(2)}) collective-permute-start(bf16[128,512]{1,0:T(8,128)(2,1)S(1)} %get-tuple-element.69), channel_id=1, source_target_pairs={{0,2},{2,0},{4,6},{6,4},{1,3},{3,1},{5,7},{7,5},{8,10},{10,8},{12,... | collective-permute-start | bytes 393224 | tf_op jit(solution)/shard_map/ppermute | solution.py:252
  33.6 2.2 %collective-permute-start.11 = (bf16[128,256]{1,0:T(8,128)(2,1)S(1)}, bf16[128,256]{1,0:T(8,128)(2,1)S(1)}, u32[]{:S(2)}, u32[]{:S(2)}) collective-permute-start(bf16[128,256]{1,0:T(8,128)(2,1)S(1)} %get-tuple-element.73), channel_id=1, source_target_pairs={{0,2},{2,0},{4,6},{6,4},{1,3},{3,1},{5,7},{7,5},{8,10},{10,8},{12,... | collective-permute-start | bytes 196616 | tf_op jit(solution)/shard_map/ppermute | solution.py:252
  34.1 1.7 %collective-permute-start.12 = (bf16[128,256]{1,0:T(8,128)(2,1)S(1)}, bf16[128,256]{1,0:T(8,128)(2,1)S(1)}, u32[]{:S(2)}, u32[]{:S(2)}) collective-permute-start(bf16[128,256]{1,0:T(8,128)(2,1)S(1)} %get-tuple-element.74), channel_id=1, source_target_pairs={{0,2},{2,0},{4,6},{6,4},{1,3},{3,1},{5,7},{7,5},{8,10},{10,8},{12,... | collective-permute-start | bytes 196616 | tf_op jit(solution)/shard_map/ppermute | solution.py:252

commit v4 on v3

--- a/solution.py
+++ b/solution.py
@@ -146,22 +146,29 @@
     key_at = lax.broadcasted_iota(jnp.int32, (tok_dev, rows), 0)
     query_at = lax.broadcasted_iota(jnp.int32, (tok_dev, rows), 1) % tok_dev
     causal = key_at <= query_at
-    for head in range(heads):
-        bias = block_bias(slots, selected_ref, head, tok_dev)
-        scores = contract(key_rows(kv_refs, head), head_rows(q_ref, head), ((1,), (1,)))
-        scores = scores * (SCALE * LOG2E)
-        parts = []
-        for kb in range(slots * tok_dev // BLK):
-            part = scores[kb * BLK : (kb + 1) * BLK] + bias[kb : kb + 1]
-            if kb * BLK < tok_dev:
-                part = jnp.where(causal[kb * BLK : (kb + 1) * BLK], part, -jnp.inf)
-            parts.append(part)
-        scores = jnp.concatenate(parts, axis=0)
-        shifted = jnp.exp2(scores - jnp.max(scores, axis=0, keepdims=True))
-        weights = (shifted * (1.0 / jnp.sum(shifted, axis=0, keepdims=True))).astype(BF16)
-        p_ref[head] = weights
-        turned = contract(value_rows(kv_refs, head).T, weights, ((1,), (0,))).astype(BF16)
-        store_rows(o_ref, head * HEAD_COLS, turned)
+    ahead = contract(key_rows(kv_refs, 0), head_rows(q_ref, 0), ((1,), (1,)))
+    weights = None
+    for head in range(heads + 1):
+        scores = ahead
+        if head + 1 < heads:
+            ahead = contract(key_rows(kv_refs, head + 1), head_rows(q_ref, head + 1), ((1,), (1,)))
+        before, weights = weights, None
+        if head < heads:
+            bias = block_bias(slots, selected_ref, head, tok_dev)
+            scores = scores * (SCALE * LOG2E)
+            parts = []
+            for kb in range(slots * tok_dev // BLK):
+                part = scores[kb * BLK : (kb + 1) * BLK] + bias[kb : kb + 1]
+                if kb * BLK < tok_dev:
+                    part = jnp.where(causal[kb * BLK : (kb + 1) * BLK], part, -jnp.inf)
+                parts.append(part)
+            scores = jnp.concatenate(parts, axis=0)
+            shifted = jnp.exp2(scores - jnp.max(scores, axis=0, keepdims=True))
+            weights = (shifted * (1.0 / jnp.sum(shifted, axis=0, keepdims=True))).astype(BF16)
+            p_ref[head] = weights
+        if before is not None:
+            turned = contract(value_rows(kv_refs, head - 1).T, before, ((1,), (0,))).astype(BF16)
+            store_rows(o_ref, (head - 1) * HEAD_COLS, turned)
 
 
 def sums_kernel(slots, first, count, sends, split, before, layout, p_ref, o_ref, q_ref, *refs):
@@ -177,35 +184,48 @@
         piece_refs = refs[: -2 - len(layout)]
         grad_ref, ds_ref, *sum_refs = refs[-2 - len(layout) :]
         put_pieces(sends, first, split, grad_ref, piece_refs)
+        grads_of = [(grad_ref, local) for local in range(count)]
     else:
-        grad_ref, ds_ref, *sum_refs = refs[0], *refs[-1 - len(layout) :]
+        ds_ref, *sum_refs = refs[-1 - len(layout) :]
+        grads_of = [(ref, at) for ref in refs[: -1 - len(layout)] for at in range(ref.shape[1] // HEAD_COLS)]
     tok_dev = q_ref.shape[0]
-    for local in range(count):
-        head = first + local
-        grads, queries, outs = head_rows(grad_ref, local), head_rows(q_ref, head), head_rows(o_ref, head)
-        delta = (grads.astype(F32) * outs.astype(F32)).astype(BF16)
-        weights = p_ref[head, begin * tok_dev : end * tok_dev]
-        values = value_rows(kv_refs, head)
-        left = jnp.concatenate([values, jnp.full(values.shape, -1, BF16)], axis=1)
-        centred = contract(left, jnp.concatenate([grads, delta], axis=1), ((1,), (1,)))
-        score_grad = (weights.astype(F32) * centred).astype(BF16)
-        ds_ref[local] = score_grad
-        sums = {
-            "key": contract(score_grad, queries, ((1,), (0,))) * SCALE,
-            "value": contract(weights, grads, ((1,), (0,))),
-        }
-        for ref, (from_slot, to_slot, kinds) in zip(sum_refs, layout):
-            for at, kind in enumerate(kinds):
-                column = (at * (before + count) + before + local) * HD
-                part = sums[kind][(from_slot - begin) * tok_dev : (to_slot - begin) * tok_dev]
-                ref[:, column : column + HD] = part.astype(ref.dtype)
+    here = lax.axis_index("ctx")
+    needed = functools.reduce(jnp.logical_or, [(here ^ slot) <= here for slot in range(begin, end)])
+
+    @pl.when(needed)
+    def work():
+        for local in range(count):
+            head = first + local
+            grads, queries, outs = head_rows(*grads_of[local]), head_rows(q_ref, head), head_rows(o_ref, head)
+            delta = (grads.astype(F32) * outs.astype(F32)).astype(BF16)
+            weights = p_ref[head, begin * tok_dev : end * tok_dev]
+            values = value_rows(kv_refs, head)
+            left = jnp.concatenate([values, jnp.full(values.shape, -1, BF16)], axis=1)
+            centred = contract(left, jnp.concatenate([grads, delta], axis=1), ((1,), (1,)))
+            score_grad = (weights.astype(F32) * centred).astype(BF16)
+            ds_ref[local] = score_grad
+            sums = {
+                "key": contract(score_grad, queries, ((1,), (0,))) * SCALE,
+                "value": contract(weights, grads, ((1,), (0,))),
+            }
+            for ref, (from_slot, to_slot, kinds) in zip(sum_refs, layout):
+                for at, kind in enumerate(kinds):
+                    column = (at * (before + count) + before + local) * HD
+                    part = sums[kind][(from_slot - begin) * tok_dev : (to_slot - begin) * tok_dev]
+                    ref[:, column : column + HD] = part.astype(ref.dtype)
+
+    @pl.when(jnp.logical_not(needed))
+    def rest():
+        ds_ref[...] = jnp.zeros_like(ds_ref)
+        for ref in sum_refs:
+            ref[...] = jnp.zeros_like(ref)
 
 
 def query_kernel(slots, places, parts, *refs):
     ds_refs, kv_refs, (dq_ref, stage_ref, sem) = refs[:parts], refs[parts : parts + slots], refs[-3:]
     copies = []
-    for head, (found, row) in enumerate(places):
-        score_grad = jnp.concatenate([ds_refs[at][row] for at in found], axis=0)
+    for head, place in enumerate(places):
+        score_grad = jnp.concatenate([ds_refs[at][row] for at, row in place], axis=0)
         turned = (contract(key_rows(kv_refs, head).T, score_grad, ((1,), (0,))) * SCALE).astype(BF16)
         store_rows(stage_ref, head * HEAD_COLS, turned)
         columns = slice(head * HEAD_COLS, (head + 1) * HEAD_COLS)
@@ -313,11 +333,11 @@
         [spec()] * 2,
     )(*ins)
 
-    def sums_of(name, group, span, layout, grads=None, done=()):
+    def sums_of(name, group, span, layout, grads=None, done=(), after=()):
         first, count = group
-        used = pieces_of(first, count) if grads is None else [grads]
+        used = pieces_of(first, count) if grads is None else grads
         before = done[0].shape[1] // (len(layout[0][2]) * HD) if done else 0
-        ins = (weights, outs, own_queries, *kv[span[0] : span[1]], *done, *used)
+        ins = (weights, outs, own_queries, *kv[span[0] : span[1]], *done, *used, *after)
         results = [shape((tok_dev, count * HEAD_COLS))] if grads is None else []
         results.append(shape((count, (span[1] - span[0]) * tok_dev, rows)))
         results.extend(
@@ -363,28 +383,33 @@
 
     both = ("key", "value")
     if paired:
-        _, scores_a, keep, send = sums_of("sums_early", (0, 2), (0, 4), [(0, 2, both, F32), (2, 4, both, BF16)])
-        part = (tok_dev, 4 * HD)
-        own, send = added(keep, swapped(send, 2), [shape(part, F32), shape(part)])
-        found = [own, swapped(send, 1)]
+        _, scores_a, keep_a, send = sums_of(
+            "sums_early", (0, 2), (0, 4), [(0, 2, both, F32), (2, 4, both, BF16)]
+        )
+        arrived = swapped(send, 2)
 
         near = [(0, 1, both, F32), (1, 2, ("key",), BF16), (1, 2, ("value",), BF16)]
         kept, sent = (2, 3, both, F32), (3, 4, both, BF16)
-        _, scores_b, *near_done, keep, send = sums_of("sums_middle", (2, 1), (0, 4), [*near, kept, sent])
-        grads, scores_3, send = sums_of("sums_3", (3, 1), (3, 4), [sent], done=[send])
-        scores_2, keep = sums_of("sums_2", (3, 1), (2, 3), [kept], grads, [keep])
-        scores_01, own, *sends_1 = sums_of("sums_01", (3, 1), (0, 2), near, grads, near_done)
-        (send,) = added(keep, swapped(send, 1), [shape(part)], own)
+        grads_b, scores_b, keep, send = sums_of("sums_middle", (2, 1), (2, 4), [kept, sent])
+        grads_c, scores_3, send = sums_of("sums_3", (3, 1), (3, 4), [sent], done=[send])
+        scores_2, keep = sums_of("sums_2", (3, 1), (2, 3), [kept], [grads_c], [keep])
+        part = (tok_dev, 4 * HD)
+        (send,) = added(keep, swapped(send, 1), [shape(part)])
+        scores_01, own, *sends_1 = sums_of(
+            "sums_01", (2, 2), (0, 2), near, [grads_b, grads_c], after=[send]
+        )
         query_grad = query_of(
             [scores_a, scores_b, scores_01, scores_2, scores_3],
-            [((0,), 0), ((0,), 1), ((1,), 0), ((2, 3, 4), 0)],
+            [((0, 0),), ((0, 1),), ((2, 0), (1, 0)), ((2, 1), (3, 0), (4, 0))],
         )
+        own_a, send_a = added(keep_a, arrived, [shape(part, F32), shape(part)], own)
+        found = [own_a, swapped(send_a, 1)]
         found.extend([own, swapped(send, 2), *(swapped(part, 1) for part in sends_1)])
         counts = [(2, 0), (2, 1)]
     else:
         layout = [(0, 1, both, F32)] + [(slot, slot + 1, both, BF16) for slot in range(1, slots)]
         _, scores, own, *send = sums_of("sums", groups[0], (0, slots), layout)
-        query_grad = query_of([scores], [((0,), head) for head in range(heads)])
+        query_grad = query_of([scores], [((0, head),) for head in range(heads)])
         found = [own, *(swapped(part, slot) for slot, part in enumerate(send, 1))]
         counts = [(slots, 0)]
 

time: 38.3 us -> 38.1 us (level)
  Pallas kernels: 14 us -> 12 us
  waiting for transfers between devices: 12.2 us -> 13.1 us
  starting transfers between devices: 11.2 us -> 11.8 us
    pallas_call x5, Pallas kernels: 4.62 us -> 3.1 us  [sums_of(): call(functools.partial(sums_kernel, span, first, count, sends, 0 if grads...]
    ppermute x4, waiting for transfers between devices: 2.04 us -> 3.4 us  [across(): return lax.ppermute(part, ('pipe', 'head'), route)]
    ppermute x9, starting transfers between devices: 5.28 us -> 5.84 us  [swapped(): lax.ppermute(value, 'ctx', [(place, place ^ mask) for place in range(slot...]
    ppermute x9, waiting for transfers between devices: 10.1 us -> 9.69 us  [swapped(): lax.ppermute(value, 'ctx', [(place, place ^ mask) for place in range(slot...]
    pallas_call x1, Pallas kernels: 4.09 us -> 3.67 us  [per_device(): call(functools.partial(weights_kernel, slots, heads), 'weights', [shape((...]
  transfers between devices with their start and end apart: 13 -> 13, of which waited for: 6 -> 6; matrix products, arithmetic and copies ran while one was open for 0% -> 0% of each run, Pallas kernels for 31% -> 27%
where the time goes in v4:
time: 38.1 us; the launch traced here: 37.7 us
  waiting for transfers between devices  13.1 us (34%)
  Pallas kernels  12 us (31%)
  starting transfers between devices  11.8 us (31%)
  between operations  0.77 us (2%)
    ppermute x9, waiting for transfers between devices, swapped(): lax.ppermute(value, 'ctx', [(place, place ^ mask) for place in range(slot...  9.69 us
    ppermute x4, starting transfers between devices, across(): return lax.ppermute(part, ('pipe', 'head'), route)  5.95 us
    ppermute x9, starting transfers between devices, swapped(): lax.ppermute(value, 'ctx', [(place, place ^ mask) for place in range(slot...  5.84 us
    pallas_call x1, Pallas kernels, per_device(): call(functools.partial(weights_kernel, slots, heads), 'weights', [shape((...  3.67 us
    ppermute x4, waiting for transfers between devices, across(): return lax.ppermute(part, ('pipe', 'head'), route)  3.4 us
    pallas_call x5, Pallas kernels, sums_of(): call(functools.partial(sums_kernel, span, first, count, sends, 0 if grads...  3.1 us
    pallas_call x1, Pallas kernels, per_device(): call(functools.partial(later_load_kernel, sends[1:], split, heads, others...  1.66 us
    pallas_call x1, Pallas kernels, query_of(): call(functools.partial(query_kernel, slots, places, len(score_grads)), 'q...  1.58 us
  transfers between devices with their start and end apart: 13, of which 6 were waited for; matrix products, arithmetic and copies ran while one was open for 0% of the time, Pallas kernels for 27%

profile of v4, /device:TPU:24, one launch (start us, length us, event | category | flops | bytes accessed | tf_op | source)
XLA Modules:
  0.0 37.7 jit_solution(1052881456668326576)
XLA Ops:
  0.6 0.0 copy-start
  0.6 1.2 %first_load.1 = (bf16[64,3072]{1,0:T(8,128)(2,1)S(1)}, bf16[64,3072]{1,0:T(8,128)(2,1)S(1)}, bf16[128,1024]{1,0:T(8,128)(2,1)S(1)}) custom-call(bf16[64,8192]{1,0:T(8,128)(2,1)} %bitcast.9, bf16[128,512]{1,0:T(8,128)(2,1)} %bitcast.13, bf16[128,512]{1,0:T(8,128)(2,1)} %bitcast.14), custom_call_target="tpu_custom_call" | custom-call | flops 1024 | bytes 1024 | tf_op jit(solution)/shard_map/first_load/pallas_call | solution.py:289
  1.9 0.5 %collective-permute-start.3 = (bf16[64,3072]{1,0:T(8,128)(2,1)S(1)}, bf16[64,3072]{1,0:T(8,128)(2,1)S(1)}, u32[]{:S(2)}, u32[]{:S(2)}) collective-permute-start(bf16[64,3072]{1,0:T(8,128)(2,1)S(1)} %get-tuple-element.49), channel_id=1, source_target_pairs={{0,24},{1,25},{8,0},{9,1},{16,8},{17,9},{24,16},{25,17},{2,26},{3,... | collective-permute-start | bytes 1179656 | tf_op jit(solution)/shard_map/ppermute | solution.py:280
  2.4 1.4 %collective-permute-start.4 = (bf16[64,3072]{1,0:T(8,128)(2,1)S(1)}, bf16[64,3072]{1,0:T(8,128)(2,1)S(1)}, u32[]{:S(2)}, u32[]{:S(2)}) collective-permute-start(bf16[64,3072]{1,0:T(8,128)(2,1)S(1)} %get-tuple-element.50), channel_id=1, source_target_pairs={{0,25},{1,24},{8,1},{9,0},{16,9},{17,8},{24,17},{25,16},{2,27},{3,... | collective-permute-start | bytes 1179656 | tf_op jit(solution)/shard_map/ppermute | solution.py:280
  3.8 9.5 %conditional.1 = (bf16[128,1024]{1,0:T(8,128)(2,1)}, bf16[128,1024]{1,0:T(8,128)(2,1)}, bf16[128,1024]{1,0:T(8,128)(2,1)}) conditional(s32[]{:T(128)} %convert_element_type.3, bf16[128,1024]{1,0:T(8,128)(2,1)S(1)} %get-tuple-element.39.refs_0_.refs_5_, bf16[128,1024]{1,0:T(8,128)(2,1)S(1)} %get-tuple-element.39.refs_0_.refs_5_), branch_computations={%region_0.0_spmd, %region_1.0_spmd} | conditional | bytes 3145872 | solution.py:308
  3.8 1.5 %collective-permute-start.1 = (bf16[128,1024]{1,0:T(8,128)(2,1)S(1)}, bf16[128,1024]{1,0:T(8,128)(2,1)}, u32[]{:S(2)}, u32[]{:S(2)}) collective-permute-start(bf16[128,1024]{1,0:T(8,128)(2,1)S(1)} %param.1), channel_id=1, source_target_pairs={{0,4},{2,6},{4,0},{6,2},{1,5},{3,7},{5,1},{7,3},{8,12},{10,14},{12... | collective-permute-start | bytes 786440 | tf_op jit(solution)/shard_map/cond/branch_1_fun/ppermute | solution.py:272
  5.3 0.0 collective-permute-start
  5.3 6.1 %collective-permute-done.1 = bf16[128,1024]{1,0:T(8,128)(2,1)} collective-permute-done((bf16[128,1024]{1,0:T(8,128)(2,1)S(1)}, bf16[128,1024]{1,0:T(8,128)(2,1)}, u32[]{:S(2)}, u32[]{:S(2)}) %collective-permute-start.1) | collective-permute-done | bytes 262176 | tf_op jit(solution)/shard_map/cond/branch_1_fun/ppermute | solution.py:272
  11.4 0.0 collective-permute-start.2
  11.4 0.0 collective-permute-done
  11.4 1.9 %collective-permute-done.2 = bf16[128,1024]{1,0:T(8,128)(2,1)} collective-permute-done((bf16[128,1024]{1,0:T(8,128)(2,1)}, bf16[128,1024]{1,0:T(8,128)(2,1)}, u32[]{:S(2)}, u32[]{:S(2)}) %collective-permute-start.2) | collective-permute-done | bytes 262176 | tf_op jit(solution)/shard_map/cond/branch_1_fun/ppermute | solution.py:272
  13.3 1.7 %later_load.1 = (bf16[64,1024]{1,0:T(8,128)(2,1)S(1)}, bf16[64,1024]{1,0:T(8,128)(2,1)S(1)}, bf16[128,4096]{1,0:T(8,128)(2,1)S(1)}, bf16[128,1024]{1,0:T(8,128)(...) custom-call(bf16[64,8192]{1,0:T(8,128)(2,1)} %bitcast.10, bf16[128,4096]{1,0:T(8,128)(2,1)} %bitcast.11, ...), custom_call_target="tpu_custom_call" | custom-call | flops 1024 | bytes 1024 | tf_op jit(solution)/shard_map/later_load/pallas_call | solution.py:310
  14.9 0.5 %collective-permute-start.5 = (bf16[64,1024]{1,0:T(8,128)(2,1)S(1)}, bf16[64,1024]{1,0:T(8,128)(2,1)S(1)}, u32[]{:S(2)}, u32[]{:S(2)}) collective-permute-start(bf16[64,1024]{1,0:T(8,128)(2,1)S(1)} %get-tuple-element.55), channel_id=1, source_target_pairs={{0,24},{1,25},{8,0},{9,1},{16,8},{17,9},{24,16},{25,17},{2,26},{3,... | collective-permute-start | bytes 393224 | tf_op jit(solution)/shard_map/ppermute | solution.py:280
  15.4 3.5 %collective-permute-start.6 = (bf16[64,1024]{1,0:T(8,128)(2,1)S(1)}, bf16[64,1024]{1,0:T(8,128)(2,1)S(1)}, u32[]{:S(2)}, u32[]{:S(2)}) collective-permute-start(bf16[64,1024]{1,0:T(8,128)(2,1)S(1)} %get-tuple-element.56), channel_id=1, source_target_pairs={{0,25},{1,24},{8,1},{9,0},{16,9},{17,8},{24,17},{25,16},{2,27},{3,... | collective-permute-start | bytes 393224 | tf_op jit(solution)/shard_map/ppermute | solution.py:280
  19.0 0.0 copy-done
  19.0 3.7 %weights.1 = (bf16[4,512,1024]{2,1,0:T(8,128)(2,1)S(1)}, bf16[128,4096]{1,0:T(8,128)(2,1)S(1)}) custom-call(bf16[128,4096]{1,0:T(8,128)(2,1)S(1)} %get-tuple-element.43.q_ref, s32[4,2,8]{2,1,0:T(2,128)S(1)} %bitcast.8, bf16[128,1024]{1,0:T(8,128)(2,1)S(1)} %get-tuple-element.39.refs_0_.refs_5_, bf16[128,1024]{1,0:T(8,128)(2,1)S(1)} %get-tuple-element.44.refs_1_.refs_6_, ...), custom_call_target="tpu_custom_call" | custom-call | flops 1024 | bytes 1024 | tf_op jit(solution)/shard_map/weights/pallas_call | solution.py:328
  22.6 0.0 collective-permute-done.3.refs_4_.refs_2_
  22.7 2.4 %collective-permute-done.4.refs_5_.refs_3_ = bf16[64,3072]{1,0:T(8,128)(2,1)S(1)} collective-permute-done((bf16[64,3072]{1,0:T(8,128)(2,1)S(1)}, bf16[64,3072]{1,0:T(8,128)(2,1)S(1)}, u32[]{:S(2)}, u32[]{:S(2)}) %collective-permute-start.4) | collective-permute-done | bytes 393248 | tf_op jit(solution)/shard_map/ppermute | solution.py:280
  25.1 1.9 %sums_early.1 = (bf16[128,2048]{1,0:T(8,128)(2,1)}, bf16[2,512,1024]{2,1,0:T(8,128)(2,1)S(1)}, f32[256,512]{1,0:T(8,128)S(1)}, bf16[256,512]{1,0:T(8,128)(2,1)S(1)}) custom-call(bf16[4,512,1024]{2,1,0:T(8,128)(2,1)S(1)} %get-tuple-element.47.p_ref, bf16[128,4096]{1,0:T(8,128)(2,1)S(1)} %get-tuple-element.48.o_ref, ...), custom_call_target="tpu_custom_call" | custom-call | flops 1024 | bytes 1024 | tf_op jit(solution)/shard_map/sums_early/pallas_call | solution.py:347
  27.0 1.6 %collective-permute-start.8 = (bf16[256,512]{1,0:T(8,128)(2,1)S(1)}, bf16[256,512]{1,0:T(8,128)(2,1)S(1)}, u32[]{:S(2)}, u32[]{:S(2)}) collective-permute-start(bf16[256,512]{1,0:T(8,128)(2,1)S(1)} %get-tuple-element.65), channel_id=1, source_target_pairs={{0,4},{2,6},{4,0},{6,2},{1,5},{3,7},{5,1},{7,3},{8,12},{10,14},{12... | collective-permute-start | bytes 786440 | tf_op jit(solution)/shard_map/ppermute | solution.py:272
  28.5 0.1 sums_middle.1
  28.6 0.0 collective-permute-done.5.refs_2_
  28.6 0.9 %collective-permute-done.6.refs_3_ = bf16[64,1024]{1,0:T(8,128)(2,1)S(1)} collective-permute-done((bf16[64,1024]{1,0:T(8,128)(2,1)S(1)}, bf16[64,1024]{1,0:T(8,128)(2,1)S(1)}, u32[]{:S(2)}, u32[]{:S(2)}) %collective-permute-start.6) | collective-permute-done | bytes 131104 | tf_op jit(solution)/shard_map/ppermute | solution.py:280
  29.6 0.1 sums_3.1
  29.6 0.1 collective-permute-start.7
  29.7 0.1 sums_2.1
  29.8 1.3 %collective-permute-done.7.received_ref = bf16[128,512]{1,0:T(8,128)(2,1)S(1)} collective-permute-done((bf16[128,512]{1,0:T(8,128)(2,1)S(1)}, bf16[128,512]{1,0:T(8,128)(2,1)S(1)}, u32[]{:S(2)}, u32[]{:S(2)}) %collective-permute-start.7) | collective-permute-done | bytes 131104 | tf_op jit(solution)/shard_map/ppermute | solution.py:272
  31.1 2.1 %collective-permute-start.10 = (bf16[128,512]{1,0:T(8,128)(2,1)S(1)}, bf16[128,512]{1,0:T(8,128)(2,1)S(1)}, u32[]{:S(2)}, u32[]{:S(2)}) collective-permute-start(bf16[128,512]{1,0:T(8,128)(2,1)S(1)} %add.2.refs_4_), channel_id=1, source_target_pairs={{0,4},{2,6},{4,0},{6,2},{1,5},{3,7},{5,1},{7,3},{8,12},{10,14},{12... | collective-permute-start | bytes 393224 | tf_op jit(solution)/shard_map/ppermute | solution.py:272
  33.2 1.0 %sums_01.1 = (bf16[2,256,1024]{2,1,0:T(8,128)(2,1)S(1)}, f32[128,512]{1,0:T(8,128)S(1)}, bf16[128,256]{1,0:T(8,128)(2,1)S(1)}, bf16[128,256]{1,0:T(8,128)(2,1)S(1)}) custom-call(bf16[4,512,1024]{2,1,0:T(8,128)(2,1)S(1)} %get-tuple-element.47.p_ref, bf16[128,4096]{1,0:T(8,128)(2,1)S(1)} %get-tuple-element.48.o_ref, ...), custom_call_target="tpu_custom_call" | custom-call | flops 1024 | bytes 1024 | tf_op jit(solution)/shard_map/sums_01/pallas_call | solution.py:347
  34.2 0.0 collective-permute-done.8.received_ref
  34.3 0.1 collective-permute-start.9
  34.4 0.5 %collective-permute-start.11 = (bf16[128,256]{1,0:T(8,128)(2,1)S(1)}, bf16[128,256]{1,0:T(8,128)(2,1)S(1)}, u32[]{:S(2)}, u32[]{:S(2)}) collective-permute-start(bf16[128,256]{1,0:T(8,128)(2,1)S(1)} %get-tuple-element.69), channel_id=1, source_target_pairs={{0,2},{2,0},{4,6},{6,4},{1,3},{3,1},{5,7},{7,5},{8,10},{10,8},{12,... | collective-permute-start | bytes 196616 | tf_op jit(solution)/shard_map/ppermute | solution.py:272
  34.8 0.1 collective-permute-start.12
  34.9 1.6 %query.1 = bf16[128,4096]{1,0:T(8,128)(2,1)} custom-call(bf16[2,512,1024]{2,1,0:T(8,128)(2,1)S(1)} %get-tuple-element.51.refs_0_, bf16[1,256,1024]{2,1,0:T(8,128)(2,1)S(1)} %get-tuple-element.52.refs_1_, bf16[2,256,1024]{2,1,0:T(8,128)(2,1)S(1)} %get-tuple-element.61.refs_2_, bf16[1,128,1024]{2,1,0:T(8,128)(2,1)S(1)} %get-tuple-element.62.refs_3_, ...), custom_call_target="tpu_custom_call" | custom-call | flops 1024 | bytes 1024 | tf_op jit(solution)/shard_map/query/pallas_call | solution.py:366
  36.5 0.0 collective-permute-done.11.refs_4_
  36.5 0.0 collective-permute-done.12.refs_5_
  36.5 0.4 %collective-permute-done.10.refs_3_ = bf16[128,512]{1,0:T(8,128)(2,1)S(1)} collective-permute-done((bf16[128,512]{1,0:T(8,128)(2,1)S(1)}, bf16[128,512]{1,0:T(8,128)(2,1)S(1)}, u32[]{:S(2)}, u32[]{:S(2)}) %collective-permute-start.10) | collective-permute-done | bytes 131104 | tf_op jit(solution)/shard_map/ppermute | solution.py:272
  37.0 0.0 collective-permute-done.9.refs_1_
  37.0 0.7 %finish.1 = (bf16[128,512]{1,0:T(8,128)(2,1)}, bf16[128,512]{1,0:T(8,128)(2,1)}) custom-call(f32[128,512]{1,0:T(8,128)S(1)} %get-tuple-element.67.refs_0_, bf16[128,512]{1,0:T(8,128)(2,1)S(1)} %collective-permute-done.9.refs_1_, f32[128,512]{1,0:T(8,128)S(1)} %get-tuple-element.66.refs_0_.refs_2_, bf16[128,512]{1,0:T(8,128)(2,1)S(1)} %collective-permute-done.10.refs_3_, ...), custom_call_target="tpu_custom_call" | custom-call | flops 1024 | bytes 1024 | tf_op jit(solution)/shard_map/finish/pallas_call | solution.py:416
  (2 shorter events, 0.1 us)
Async XLA Ops:
  0.6 18.3 %copy-start = (s32[1,4,2,8]{3,2,1,0:T(2,128)S(1)}, s32[1,4,2,8]{3,2,1,0:T(2,128)}, u32[]{:S(2)}) copy-start(s32[1,4,2,8]{3,2,1,0:T(2,128)} %param.11) | copy-start | bytes 772
  1.9 20.8 %collective-permute-start.3 = (bf16[64,3072]{1,0:T(8,128)(2,1)S(1)}, bf16[64,3072]{1,0:T(8,128)(2,1)S(1)}, u32[]{:S(2)}, u32[]{:S(2)}) collective-permute-start(bf16[64,3072]{1,0:T(8,128)(2,1)S(1)} %get-tuple-element.49), channel_id=1, source_target_pairs={{0,24},{1,25},{8,0},{9,1},{16,8},{17,9},{24,16},{25,17},{2,26},{3,... | collective-permute-start | bytes 1179656 | tf_op jit(solution)/shard_map/ppermute | solution.py:280
  2.4 22.7 %collective-permute-start.4 = (bf16[64,3072]{1,0:T(8,128)(2,1)S(1)}, bf16[64,3072]{1,0:T(8,128)(2,1)S(1)}, u32[]{:S(2)}, u32[]{:S(2)}) collective-permute-start(bf16[64,3072]{1,0:T(8,128)(2,1)S(1)} %get-tuple-element.50), channel_id=1, source_target_pairs={{0,25},{1,24},{8,1},{9,0},{16,9},{17,8},{24,17},{25,16},{2,27},{3,... | collective-permute-start | bytes 1179656 | tf_op jit(solution)/shard_map/ppermute | solution.py:280
  3.8 7.6 %collective-permute-start.1 = (bf16[128,1024]{1,0:T(8,128)(2,1)S(1)}, bf16[128,1024]{1,0:T(8,128)(2,1)}, u32[]{:S(2)}, u32[]{:S(2)}) collective-permute-start(bf16[128,1024]{1,0:T(8,128)(2,1)S(1)} %param.1), channel_id=1, source_target_pairs={{0,4},{2,6},{4,0},{6,2},{1,5},{3,7},{5,1},{7,3},{8,12},{10,14},{12... | collective-permute-start | bytes 786440 | tf_op jit(solution)/shard_map/cond/branch_1_fun/ppermute | solution.py:272
  5.3 6.1 %collective-permute-start = (bf16[128,1024]{1,0:T(8,128)(2,1)S(1)}, bf16[128,1024]{1,0:T(8,128)(2,1)}, u32[]{:S(2)}, u32[]{:S(2)}) collective-permute-start(bf16[128,1024]{1,0:T(8,128)(2,1)S(1)} %param.1), channel_id=1, source_target_pairs={{0,2},{2,0},{4,6},{6,4},{1,3},{3,1},{5,7},{7,5},{8,10},{10,8},{12,... | collective-permute-start | bytes 786440 | tf_op jit(solution)/shard_map/cond/branch_1_fun/ppermute | solution.py:272
  11.4 1.9 %collective-permute-start.2 = (bf16[128,1024]{1,0:T(8,128)(2,1)}, bf16[128,1024]{1,0:T(8,128)(2,1)}, u32[]{:S(2)}, u32[]{:S(2)}) collective-permute-start(bf16[128,1024]{1,0:T(8,128)(2,1)} %collective-permute-done.1), channel_id=1, source_target_pairs={{0,2},{2,0},{4,6},{6,4},{1,3},{3,1},{5,7},{7,5},{8,10},{10,8},{12,... | collective-permute-start | bytes 786440 | tf_op jit(solution)/shard_map/cond/branch_1_fun/ppermute | solution.py:272
  14.9 13.7 %collective-permute-start.5 = (bf16[64,1024]{1,0:T(8,128)(2,1)S(1)}, bf16[64,1024]{1,0:T(8,128)(2,1)S(1)}, u32[]{:S(2)}, u32[]{:S(2)}) collective-permute-start(bf16[64,1024]{1,0:T(8,128)(2,1)S(1)} %get-tuple-element.55), channel_id=1, source_target_pairs={{0,24},{1,25},{8,0},{9,1},{16,8},{17,9},{24,16},{25,17},{2,26},{3,... | collective-permute-start | bytes 393224 | tf_op jit(solution)/shard_map/ppermute | solution.py:280
  15.4 14.2 %collective-permute-start.6 = (bf16[64,1024]{1,0:T(8,128)(2,1)S(1)}, bf16[64,1024]{1,0:T(8,128)(2,1)S(1)}, u32[]{:S(2)}, u32[]{:S(2)}) collective-permute-start(bf16[64,1024]{1,0:T(8,128)(2,1)S(1)} %get-tuple-element.56), channel_id=1, source_target_pairs={{0,25},{1,24},{8,1},{9,0},{16,9},{17,8},{24,17},{25,16},{2,27},{3,... | collective-permute-start | bytes 393224 | tf_op jit(solution)/shard_map/ppermute | solution.py:280
  27.0 7.2 %collective-permute-start.8 = (bf16[256,512]{1,0:T(8,128)(2,1)S(1)}, bf16[256,512]{1,0:T(8,128)(2,1)S(1)}, u32[]{:S(2)}, u32[]{:S(2)}) collective-permute-start(bf16[256,512]{1,0:T(8,128)(2,1)S(1)} %get-tuple-element.65), channel_id=1, source_target_pairs={{0,4},{2,6},{4,0},{6,2},{1,5},{3,7},{5,1},{7,3},{8,12},{10,14},{12... | collective-permute-start | bytes 786440 | tf_op jit(solution)/shard_map/ppermute | solution.py:272
  29.6 1.4 %collective-permute-start.7 = (bf16[128,512]{1,0:T(8,128)(2,1)S(1)}, bf16[128,512]{1,0:T(8,128)(2,1)S(1)}, u32[]{:S(2)}, u32[]{:S(2)}) collective-permute-start(bf16[128,512]{1,0:T(8,128)(2,1)S(1)} %get-tuple-element.60), channel_id=1, source_target_pairs={{0,2},{2,0},{4,6},{6,4},{1,3},{3,1},{5,7},{7,5},{8,10},{10,8},{12,... | collective-permute-start | bytes 393224 | tf_op jit(solution)/shard_map/ppermute | solution.py:272
  31.1 5.9 %collective-permute-start.10 = (bf16[128,512]{1,0:T(8,128)(2,1)S(1)}, bf16[128,512]{1,0:T(8,128)(2,1)S(1)}, u32[]{:S(2)}, u32[]{:S(2)}) collective-permute-start(bf16[128,512]{1,0:T(8,128)(2,1)S(1)} %add.2.refs_4_), channel_id=1, source_target_pairs={{0,4},{2,6},{4,0},{6,2},{1,5},{3,7},{5,1},{7,3},{8,12},{10,14},{12... | collective-permute-start | bytes 393224 | tf_op jit(solution)/shard_map/ppermute | solution.py:272
  34.3 2.7 %collective-permute-start.9 = (bf16[128,512]{1,0:T(8,128)(2,1)S(1)}, bf16[128,512]{1,0:T(8,128)(2,1)S(1)}, u32[]{:S(2)}, u32[]{:S(2)}) collective-permute-start(bf16[128,512]{1,0:T(8,128)(2,1)S(1)} %get-tuple-element.68), channel_id=1, source_target_pairs={{0,2},{2,0},{4,6},{6,4},{1,3},{3,1},{5,7},{7,5},{8,10},{10,8},{12,... | collective-permute-start | bytes 393224 | tf_op jit(solution)/shard_map/ppermute | solution.py:272
  34.4 2.2 %collective-permute-start.11 = (bf16[128,256]{1,0:T(8,128)(2,1)S(1)}, bf16[128,256]{1,0:T(8,128)(2,1)S(1)}, u32[]{:S(2)}, u32[]{:S(2)}) collective-permute-start(bf16[128,256]{1,0:T(8,128)(2,1)S(1)} %get-tuple-element.69), channel_id=1, source_target_pairs={{0,2},{2,0},{4,6},{6,4},{1,3},{3,1},{5,7},{7,5},{8,10},{10,8},{12,... | collective-permute-start | bytes 196616 | tf_op jit(solution)/shard_map/ppermute | solution.py:272
  34.8 1.7 %collective-permute-start.12 = (bf16[128,256]{1,0:T(8,128)(2,1)S(1)}, bf16[128,256]{1,0:T(8,128)(2,1)S(1)}, u32[]{:S(2)}, u32[]{:S(2)}) collective-permute-start(bf16[128,256]{1,0:T(8,128)(2,1)S(1)} %get-tuple-element.70), channel_id=1, source_target_pairs={{0,2},{2,0},{4,6},{6,4},{1,3},{3,1},{5,7},{7,5},{8,10},{10,8},{12,... | collective-permute-start | bytes 196616 | tf_op jit(solution)/shard_map/ppermute | solution.py:272

commit v5 on v4

--- a/solution.py
+++ b/solution.py
@@ -167,8 +167,20 @@
             weights = (shifted * (1.0 / jnp.sum(shifted, axis=0, keepdims=True))).astype(BF16)
             p_ref[head] = weights
         if before is not None:
-            turned = contract(value_rows(kv_refs, head - 1).T, before, ((1,), (0,))).astype(BF16)
-            store_rows(o_ref, (head - 1) * HEAD_COLS, turned)
+            values = value_rows(kv_refs, head - 1).T
+            left = jnp.concatenate([values, jnp.ones((16, values.shape[1]), BF16)], axis=0)
+            turned = contract(left, before, ((1,), (0,)))
+            store_rows(o_ref, (head - 1) * HEAD_COLS, turned[:HD] * (1.0 / turned[HD : HD + 1]))
+
+
+def in_parts(column):
+    lane = lax.broadcasted_iota(jnp.int32, (column.shape[0], HD), 1)
+    parts = jnp.zeros((column.shape[0], HD), F32)
+    for at in range(3):
+        part = column.astype(BF16).astype(F32)
+        column = column - part
+        parts = jnp.where(lane == at, part, parts)
+    return parts.astype(BF16)
 
 
 def sums_kernel(slots, first, count, sends, split, before, layout, p_ref, o_ref, q_ref, *refs):
@@ -197,7 +209,7 @@
         for local in range(count):
             head = first + local
             grads, queries, outs = head_rows(*grads_of[local]), head_rows(q_ref, head), head_rows(o_ref, head)
-            delta = (grads.astype(F32) * outs.astype(F32)).astype(BF16)
+            delta = in_parts(jnp.sum(grads.astype(F32) * outs, axis=1, keepdims=True))
             weights = p_ref[head, begin * tok_dev : end * tok_dev]
             values = value_rows(kv_refs, head)
             left = jnp.concatenate([values, jnp.full(values.shape, -1, BF16)], axis=1)
@@ -328,7 +340,7 @@
     weights, outs = call(
         functools.partial(weights_kernel, slots, heads),
         "weights",
-        [shape((heads, slots * tok_dev, rows)), shape((tok_dev, heads * HEAD_COLS))],
+        [shape((heads, slots * tok_dev, rows)), shape((tok_dev, heads * HEAD_COLS), F32)],
         [spec()] * len(ins),
         [spec()] * 2,
     )(*ins)

time: 38.1 us -> 38.4 us (level)
  Pallas kernels: 12 us -> 12.6 us
  waiting for transfers between devices: 13.1 us -> 12.5 us
  transfers between devices with their start and end apart: 13 -> 13, of which waited for: 6 -> 6; matrix products, arithmetic and copies ran while one was open for 0% -> 0% of each run, Pallas kernels for 27% -> 28%
where the time goes in v5:
time: 38.4 us; the launch traced here: 37.8 us
  Pallas kernels  12.6 us (33%)
  waiting for transfers between devices  12.5 us (33%)
  starting transfers between devices  11.9 us (31%)
  between operations  0.76 us (2%)
    ppermute x9, waiting for transfers between devices, swapped(): lax.ppermute(value, 'ctx', [(place, place ^ mask) for place in range(slot...  9.44 us
    ppermute x4, starting transfers between devices, across(): return lax.ppermute(part, ('pipe', 'head'), route)  5.95 us
    ppermute x9, starting transfers between devices, swapped(): lax.ppermute(value, 'ctx', [(place, place ^ mask) for place in range(slot...  5.92 us
    pallas_call x1, Pallas kernels, per_device(): call(functools.partial(weights_kernel, slots, heads), 'weights', [shape((...  3.84 us
    pallas_call x5, Pallas kernels, sums_of(): call(functools.partial(sums_kernel, span, first, count, sends, 0 if grads...  3.46 us
    ppermute x4, waiting for transfers between devices, across(): return lax.ppermute(part, ('pipe', 'head'), route)  3.08 us
    pallas_call x1, Pallas kernels, per_device(): call(functools.partial(later_load_kernel, sends[1:], split, heads, others...  1.66 us
    pallas_call x1, Pallas kernels, query_of(): call(functools.partial(query_kernel, slots, places, len(score_grads)), 'q...  1.61 us
  transfers between devices with their start and end apart: 13, of which 6 were waited for; matrix products, arithmetic and copies ran while one was open for 0% of the time, Pallas kernels for 28%

profile of v5, /device:TPU:24, one launch (start us, length us, event | category | flops | bytes accessed | tf_op | source)
XLA Modules:
  0.0 37.8 jit_solution(4990341305913184562)
XLA Ops:
  0.6 1.2 %first_load.1 = (bf16[64,3072]{1,0:T(8,128)(2,1)S(1)}, bf16[64,3072]{1,0:T(8,128)(2,1)S(1)}, bf16[128,1024]{1,0:T(8,128)(2,1)S(1)}) custom-call(bf16[64,8192]{1,0:T(8,128)(2,1)} %bitcast.9, bf16[128,512]{1,0:T(8,128)(2,1)} %bitcast.13, bf16[128,512]{1,0:T(8,128)(2,1)} %bitcast.14), custom_call_target="tpu_custom_call" | custom-call | flops 1024 | bytes 1024 | tf_op jit(solution)/shard_map/first_load/pallas_call | solution.py:301
  1.9 0.5 %collective-permute-start.3 = (bf16[64,3072]{1,0:T(8,128)(2,1)S(1)}, bf16[64,3072]{1,0:T(8,128)(2,1)S(1)}, u32[]{:S(2)}, u32[]{:S(2)}) collective-permute-start(bf16[64,3072]{1,0:T(8,128)(2,1)S(1)} %get-tuple-element.49), channel_id=1, source_target_pairs={{0,24},{1,25},{8,0},{9,1},{16,8},{17,9},{24,16},{25,17},{2,26},{3,... | collective-permute-start | bytes 1179656 | tf_op jit(solution)/shard_map/ppermute | solution.py:292
  2.4 1.4 %collective-permute-start.4 = (bf16[64,3072]{1,0:T(8,128)(2,1)S(1)}, bf16[64,3072]{1,0:T(8,128)(2,1)S(1)}, u32[]{:S(2)}, u32[]{:S(2)}) collective-permute-start(bf16[64,3072]{1,0:T(8,128)(2,1)S(1)} %get-tuple-element.50), channel_id=1, source_target_pairs={{0,25},{1,24},{8,1},{9,0},{16,9},{17,8},{24,17},{25,16},{2,27},{3,... | collective-permute-start | bytes 1179656 | tf_op jit(solution)/shard_map/ppermute | solution.py:292
  3.8 0.0 copy-start
  3.8 9.5 %conditional.1 = (bf16[128,1024]{1,0:T(8,128)(2,1)}, bf16[128,1024]{1,0:T(8,128)(2,1)}, bf16[128,1024]{1,0:T(8,128)(2,1)}) conditional(s32[]{:T(128)} %convert_element_type.3, bf16[128,1024]{1,0:T(8,128)(2,1)S(1)} %get-tuple-element.39.refs_0_.refs_5_, bf16[128,1024]{1,0:T(8,128)(2,1)S(1)} %get-tuple-element.39.refs_0_.refs_5_), branch_computations={%region_0.0_spmd, %region_1.0_spmd} | conditional | bytes 3145872 | solution.py:320
  3.8 1.5 %collective-permute-start.1 = (bf16[128,1024]{1,0:T(8,128)(2,1)S(1)}, bf16[128,1024]{1,0:T(8,128)(2,1)}, u32[]{:S(2)}, u32[]{:S(2)}) collective-permute-start(bf16[128,1024]{1,0:T(8,128)(2,1)S(1)} %param.1), channel_id=1, source_target_pairs={{0,4},{2,6},{4,0},{6,2},{1,5},{3,7},{5,1},{7,3},{8,12},{10,14},{12... | collective-permute-start | bytes 786440 | tf_op jit(solution)/shard_map/cond/branch_1_fun/ppermute | solution.py:284
  5.3 0.0 collective-permute-start
  5.3 6.1 %collective-permute-done.1 = bf16[128,1024]{1,0:T(8,128)(2,1)} collective-permute-done((bf16[128,1024]{1,0:T(8,128)(2,1)S(1)}, bf16[128,1024]{1,0:T(8,128)(2,1)}, u32[]{:S(2)}, u32[]{:S(2)}) %collective-permute-start.1) | collective-permute-done | bytes 262176 | tf_op jit(solution)/shard_map/cond/branch_1_fun/ppermute | solution.py:284
  11.4 0.0 collective-permute-start.2
  11.4 0.0 collective-permute-done
  11.4 1.9 %collective-permute-done.2 = bf16[128,1024]{1,0:T(8,128)(2,1)} collective-permute-done((bf16[128,1024]{1,0:T(8,128)(2,1)}, bf16[128,1024]{1,0:T(8,128)(2,1)}, u32[]{:S(2)}, u32[]{:S(2)}) %collective-permute-start.2) | collective-permute-done | bytes 262176 | tf_op jit(solution)/shard_map/cond/branch_1_fun/ppermute | solution.py:284
  13.2 1.7 %later_load.1 = (bf16[64,1024]{1,0:T(8,128)(2,1)S(1)}, bf16[64,1024]{1,0:T(8,128)(2,1)S(1)}, bf16[128,4096]{1,0:T(8,128)(2,1)S(1)}, bf16[128,1024]{1,0:T(8,128)(...) custom-call(bf16[64,8192]{1,0:T(8,128)(2,1)} %bitcast.10, bf16[128,4096]{1,0:T(8,128)(2,1)} %bitcast.11, ...), custom_call_target="tpu_custom_call" | custom-call | flops 1024 | bytes 1024 | tf_op jit(solution)/shard_map/later_load/pallas_call | solution.py:322
  14.9 0.5 %collective-permute-start.5 = (bf16[64,1024]{1,0:T(8,128)(2,1)S(1)}, bf16[64,1024]{1,0:T(8,128)(2,1)S(1)}, u32[]{:S(2)}, u32[]{:S(2)}) collective-permute-start(bf16[64,1024]{1,0:T(8,128)(2,1)S(1)} %get-tuple-element.55), channel_id=1, source_target_pairs={{0,24},{1,25},{8,0},{9,1},{16,8},{17,9},{24,16},{25,17},{2,26},{3,... | collective-permute-start | bytes 393224 | tf_op jit(solution)/shard_map/ppermute | solution.py:292
  15.4 3.5 %collective-permute-start.6 = (bf16[64,1024]{1,0:T(8,128)(2,1)S(1)}, bf16[64,1024]{1,0:T(8,128)(2,1)S(1)}, u32[]{:S(2)}, u32[]{:S(2)}) collective-permute-start(bf16[64,1024]{1,0:T(8,128)(2,1)S(1)} %get-tuple-element.56), channel_id=1, source_target_pairs={{0,25},{1,24},{8,1},{9,0},{16,9},{17,8},{24,17},{25,16},{2,27},{3,... | collective-permute-start | bytes 393224 | tf_op jit(solution)/shard_map/ppermute | solution.py:292
  19.0 0.0 copy-done
  19.0 3.8 %weights.1 = (bf16[4,512,1024]{2,1,0:T(8,128)(2,1)S(1)}, f32[128,4096]{1,0:T(8,128)S(1)}) custom-call(bf16[128,4096]{1,0:T(8,128)(2,1)S(1)} %get-tuple-element.43.q_ref, s32[4,2,8]{2,1,0:T(2,128)S(1)} %bitcast.8, bf16[128,1024]{1,0:T(8,128)(2,1)S(1)} %get-tuple-element.39.refs_0_.refs_5_, bf16[128,1024]{1,0:T(8,128)(2,1)S(1)} %get-tuple-element.44.refs_1_.refs_6_, ...), custom_call_target="tpu_custom_call" | custom-call | flops 1024 | bytes 1024 | tf_op jit(solution)/shard_map/weights/pallas_call | solution.py:340
  22.8 0.0 collective-permute-done.3.refs_4_.refs_2_
  22.8 2.3 %collective-permute-done.4.refs_5_.refs_3_ = bf16[64,3072]{1,0:T(8,128)(2,1)S(1)} collective-permute-done((bf16[64,3072]{1,0:T(8,128)(2,1)S(1)}, bf16[64,3072]{1,0:T(8,128)(2,1)S(1)}, u32[]{:S(2)}, u32[]{:S(2)}) %collective-permute-start.4) | collective-permute-done | bytes 393248 | tf_op jit(solution)/shard_map/ppermute | solution.py:292
  25.1 2.0 %sums_early.1 = (bf16[128,2048]{1,0:T(8,128)(2,1)}, bf16[2,512,1024]{2,1,0:T(8,128)(2,1)S(1)}, f32[256,512]{1,0:T(8,128)S(1)}, bf16[256,512]{1,0:T(8,128)(2,1)S(1)}) custom-call(bf16[4,512,1024]{2,1,0:T(8,128)(2,1)S(1)} %get-tuple-element.47.p_ref, f32[128,4096]{1,0:T(8,128)S(1)} %get-tuple-element.48.o_ref, bf16[128,4096]{1,0:T(8,128)(2,1)S(1)} %get-tuple-element.43.q_ref, ...), custom_call_target="tpu_custom_call" | custom-call | flops 1024 | bytes 1024 | tf_op jit(solution)/shard_map/sums_early/pallas_call | solution.py:359
  27.1 1.6 %collective-permute-start.8 = (bf16[256,512]{1,0:T(8,128)(2,1)S(1)}, bf16[256,512]{1,0:T(8,128)(2,1)S(1)}, u32[]{:S(2)}, u32[]{:S(2)}) collective-permute-start(bf16[256,512]{1,0:T(8,128)(2,1)S(1)} %get-tuple-element.65), channel_id=1, source_target_pairs={{0,4},{2,6},{4,0},{6,2},{1,5},{3,7},{5,1},{7,3},{8,12},{10,14},{12... | collective-permute-start | bytes 786440 | tf_op jit(solution)/shard_map/ppermute | solution.py:284
  28.7 0.1 sums_middle.1
  28.8 0.0 collective-permute-done.5.refs_2_
  28.8 0.8 %collective-permute-done.6.refs_3_ = bf16[64,1024]{1,0:T(8,128)(2,1)S(1)} collective-permute-done((bf16[64,1024]{1,0:T(8,128)(2,1)S(1)}, bf16[64,1024]{1,0:T(8,128)(2,1)S(1)}, u32[]{:S(2)}, u32[]{:S(2)}) %collective-permute-start.6) | collective-permute-done | bytes 131104 | tf_op jit(solution)/shard_map/ppermute | solution.py:292
  29.6 0.1 sums_3.1
  29.6 0.1 collective-permute-start.7
  29.7 0.1 sums_2.1
  29.8 1.3 %collective-permute-done.7.received_ref = bf16[128,512]{1,0:T(8,128)(2,1)S(1)} collective-permute-done((bf16[128,512]{1,0:T(8,128)(2,1)S(1)}, bf16[128,512]{1,0:T(8,128)(2,1)S(1)}, u32[]{:S(2)}, u32[]{:S(2)}) %collective-permute-start.7) | collective-permute-done | bytes 131104 | tf_op jit(solution)/shard_map/ppermute | solution.py:284
  31.1 2.2 %collective-permute-start.10 = (bf16[128,512]{1,0:T(8,128)(2,1)S(1)}, bf16[128,512]{1,0:T(8,128)(2,1)S(1)}, u32[]{:S(2)}, u32[]{:S(2)}) collective-permute-start(bf16[128,512]{1,0:T(8,128)(2,1)S(1)} %add.2.refs_4_), channel_id=1, source_target_pairs={{0,4},{2,6},{4,0},{6,2},{1,5},{3,7},{5,1},{7,3},{8,12},{10,14},{12... | collective-permute-start | bytes 393224 | tf_op jit(solution)/shard_map/ppermute | solution.py:284
  33.2 1.2 %sums_01.1 = (bf16[2,256,1024]{2,1,0:T(8,128)(2,1)S(1)}, f32[128,512]{1,0:T(8,128)S(1)}, bf16[128,256]{1,0:T(8,128)(2,1)S(1)}, bf16[128,256]{1,0:T(8,128)(2,1)S(1)}) custom-call(bf16[4,512,1024]{2,1,0:T(8,128)(2,1)S(1)} %get-tuple-element.47.p_ref, f32[128,4096]{1,0:T(8,128)S(1)} %get-tuple-element.48.o_ref, bf16[128,4096]{1,0:T(8,128)(2,1)S(1)} %get-tuple-element.43.q_ref, ...), custom_call_target="tpu_custom_call" | custom-call | flops 1024 | bytes 1024 | tf_op jit(solution)/shard_map/sums_01/pallas_call | solution.py:359
  34.5 0.0 collective-permute-done.8.received_ref
  34.5 0.1 add.3
  34.6 0.1 collective-permute-start.9
  34.6 0.5 %collective-permute-start.11 = (bf16[128,256]{1,0:T(8,128)(2,1)S(1)}, bf16[128,256]{1,0:T(8,128)(2,1)S(1)}, u32[]{:S(2)}, u32[]{:S(2)}) collective-permute-start(bf16[128,256]{1,0:T(8,128)(2,1)S(1)} %get-tuple-element.69), channel_id=1, source_target_pairs={{0,2},{2,0},{4,6},{6,4},{1,3},{3,1},{5,7},{7,5},{8,10},{10,8},{12,... | collective-permute-start | bytes 196616 | tf_op jit(solution)/shard_map/ppermute | solution.py:284
  35.1 0.1 collective-permute-start.12
  35.2 1.6 %query.1 = bf16[128,4096]{1,0:T(8,128)(2,1)} custom-call(bf16[2,512,1024]{2,1,0:T(8,128)(2,1)S(1)} %get-tuple-element.51.refs_0_, bf16[1,256,1024]{2,1,0:T(8,128)(2,1)S(1)} %get-tuple-element.52.refs_1_, bf16[2,256,1024]{2,1,0:T(8,128)(2,1)S(1)} %get-tuple-element.61.refs_2_, bf16[1,128,1024]{2,1,0:T(8,128)(2,1)S(1)} %get-tuple-element.62.refs_3_, ...), custom_call_target="tpu_custom_call" | custom-call | flops 1024 | bytes 1024 | tf_op jit(solution)/shard_map/query/pallas_call | solution.py:378
  36.8 0.0 collective-permute-done.11.refs_4_
  36.8 0.0 collective-permute-done.12.refs_5_
  36.9 0.2 collective-permute-done.10.refs_3_
  37.0 0.0 collective-permute-done.9.refs_1_
  37.0 0.7 %finish.1 = (bf16[128,512]{1,0:T(8,128)(2,1)}, bf16[128,512]{1,0:T(8,128)(2,1)}) custom-call(f32[128,512]{1,0:T(8,128)S(1)} %get-tuple-element.67.refs_0_, bf16[128,512]{1,0:T(8,128)(2,1)S(1)} %collective-permute-done.9.refs_1_, f32[128,512]{1,0:T(8,128)S(1)} %get-tuple-element.66.refs_0_.refs_2_, bf16[128,512]{1,0:T(8,128)(2,1)S(1)} %collective-permute-done.10.refs_3_, ...), custom_call_target="tpu_custom_call" | custom-call | flops 1024 | bytes 1024 | tf_op jit(solution)/shard_map/finish/pallas_call | solution.py:428
  (1 shorter events, 0.0 us)
Async XLA Ops:
  1.9 20.9 %collective-permute-start.3 = (bf16[64,3072]{1,0:T(8,128)(2,1)S(1)}, bf16[64,3072]{1,0:T(8,128)(2,1)S(1)}, u32[]{:S(2)}, u32[]{:S(2)}) collective-permute-start(bf16[64,3072]{1,0:T(8,128)(2,1)S(1)} %get-tuple-element.49), channel_id=1, source_target_pairs={{0,24},{1,25},{8,0},{9,1},{16,8},{17,9},{24,16},{25,17},{2,26},{3,... | collective-permute-start | bytes 1179656 | tf_op jit(solution)/shard_map/ppermute | solution.py:292
  2.4 22.7 %collective-permute-start.4 = (bf16[64,3072]{1,0:T(8,128)(2,1)S(1)}, bf16[64,3072]{1,0:T(8,128)(2,1)S(1)}, u32[]{:S(2)}, u32[]{:S(2)}) collective-permute-start(bf16[64,3072]{1,0:T(8,128)(2,1)S(1)} %get-tuple-element.50), channel_id=1, source_target_pairs={{0,25},{1,24},{8,1},{9,0},{16,9},{17,8},{24,17},{25,16},{2,27},{3,... | collective-permute-start | bytes 1179656 | tf_op jit(solution)/shard_map/ppermute | solution.py:292
  3.8 15.2 %copy-start = (s32[1,4,2,8]{3,2,1,0:T(2,128)S(1)}, s32[1,4,2,8]{3,2,1,0:T(2,128)}, u32[]{:S(2)}) copy-start(s32[1,4,2,8]{3,2,1,0:T(2,128)} %param.11) | copy-start | bytes 772
  3.8 7.6 %collective-permute-start.1 = (bf16[128,1024]{1,0:T(8,128)(2,1)S(1)}, bf16[128,1024]{1,0:T(8,128)(2,1)}, u32[]{:S(2)}, u32[]{:S(2)}) collective-permute-start(bf16[128,1024]{1,0:T(8,128)(2,1)S(1)} %param.1), channel_id=1, source_target_pairs={{0,4},{2,6},{4,0},{6,2},{1,5},{3,7},{5,1},{7,3},{8,12},{10,14},{12... | collective-permute-start | bytes 786440 | tf_op jit(solution)/shard_map/cond/branch_1_fun/ppermute | solution.py:284
  5.3 6.1 %collective-permute-start = (bf16[128,1024]{1,0:T(8,128)(2,1)S(1)}, bf16[128,1024]{1,0:T(8,128)(2,1)}, u32[]{:S(2)}, u32[]{:S(2)}) collective-permute-start(bf16[128,1024]{1,0:T(8,128)(2,1)S(1)} %param.1), channel_id=1, source_target_pairs={{0,2},{2,0},{4,6},{6,4},{1,3},{3,1},{5,7},{7,5},{8,10},{10,8},{12,... | collective-permute-start | bytes 786440 | tf_op jit(solution)/shard_map/cond/branch_1_fun/ppermute | solution.py:284
  11.4 1.9 %collective-permute-start.2 = (bf16[128,1024]{1,0:T(8,128)(2,1)}, bf16[128,1024]{1,0:T(8,128)(2,1)}, u32[]{:S(2)}, u32[]{:S(2)}) collective-permute-start(bf16[128,1024]{1,0:T(8,128)(2,1)} %collective-permute-done.1), channel_id=1, source_target_pairs={{0,2},{2,0},{4,6},{6,4},{1,3},{3,1},{5,7},{7,5},{8,10},{10,8},{12,... | collective-permute-start | bytes 786440 | tf_op jit(solution)/shard_map/cond/branch_1_fun/ppermute | solution.py:284
  14.9 13.9 %collective-permute-start.5 = (bf16[64,1024]{1,0:T(8,128)(2,1)S(1)}, bf16[64,1024]{1,0:T(8,128)(2,1)S(1)}, u32[]{:S(2)}, u32[]{:S(2)}) collective-permute-start(bf16[64,1024]{1,0:T(8,128)(2,1)S(1)} %get-tuple-element.55), channel_id=1, source_target_pairs={{0,24},{1,25},{8,0},{9,1},{16,8},{17,9},{24,16},{25,17},{2,26},{3,... | collective-permute-start | bytes 393224 | tf_op jit(solution)/shard_map/ppermute | solution.py:292
  15.4 14.2 %collective-permute-start.6 = (bf16[64,1024]{1,0:T(8,128)(2,1)S(1)}, bf16[64,1024]{1,0:T(8,128)(2,1)S(1)}, u32[]{:S(2)}, u32[]{:S(2)}) collective-permute-start(bf16[64,1024]{1,0:T(8,128)(2,1)S(1)} %get-tuple-element.56), channel_id=1, source_target_pairs={{0,25},{1,24},{8,1},{9,0},{16,9},{17,8},{24,17},{25,16},{2,27},{3,... | collective-permute-start | bytes 393224 | tf_op jit(solution)/shard_map/ppermute | solution.py:292
  27.1 7.4 %collective-permute-start.8 = (bf16[256,512]{1,0:T(8,128)(2,1)S(1)}, bf16[256,512]{1,0:T(8,128)(2,1)S(1)}, u32[]{:S(2)}, u32[]{:S(2)}) collective-permute-start(bf16[256,512]{1,0:T(8,128)(2,1)S(1)} %get-tuple-element.65), channel_id=1, source_target_pairs={{0,4},{2,6},{4,0},{6,2},{1,5},{3,7},{5,1},{7,3},{8,12},{10,14},{12... | collective-permute-start | bytes 786440 | tf_op jit(solution)/shard_map/ppermute | solution.py:284
  29.6 1.4 %collective-permute-start.7 = (bf16[128,512]{1,0:T(8,128)(2,1)S(1)}, bf16[128,512]{1,0:T(8,128)(2,1)S(1)}, u32[]{:S(2)}, u32[]{:S(2)}) collective-permute-start(bf16[128,512]{1,0:T(8,128)(2,1)S(1)} %get-tuple-element.60), channel_id=1, source_target_pairs={{0,2},{2,0},{4,6},{6,4},{1,3},{3,1},{5,7},{7,5},{8,10},{10,8},{12,... | collective-permute-start | bytes 393224 | tf_op jit(solution)/shard_map/ppermute | solution.py:284
  31.1 6.0 %collective-permute-start.10 = (bf16[128,512]{1,0:T(8,128)(2,1)S(1)}, bf16[128,512]{1,0:T(8,128)(2,1)S(1)}, u32[]{:S(2)}, u32[]{:S(2)}) collective-permute-start(bf16[128,512]{1,0:T(8,128)(2,1)S(1)} %add.2.refs_4_), channel_id=1, source_target_pairs={{0,4},{2,6},{4,0},{6,2},{1,5},{3,7},{5,1},{7,3},{8,12},{10,14},{12... | collective-permute-start | bytes 393224 | tf_op jit(solution)/shard_map/ppermute | solution.py:284
  34.6 2.5 %collective-permute-start.9 = (bf16[128,512]{1,0:T(8,128)(2,1)S(1)}, bf16[128,512]{1,0:T(8,128)(2,1)S(1)}, u32[]{:S(2)}, u32[]{:S(2)}) collective-permute-start(bf16[128,512]{1,0:T(8,128)(2,1)S(1)} %get-tuple-element.68), channel_id=1, source_target_pairs={{0,2},{2,0},{4,6},{6,4},{1,3},{3,1},{5,7},{7,5},{8,10},{10,8},{12,... | collective-permute-start | bytes 393224 | tf_op jit(solution)/shard_map/ppermute | solution.py:284
  34.6 2.2 %collective-permute-start.11 = (bf16[128,256]{1,0:T(8,128)(2,1)S(1)}, bf16[128,256]{1,0:T(8,128)(2,1)S(1)}, u32[]{:S(2)}, u32[]{:S(2)}) collective-permute-start(bf16[128,256]{1,0:T(8,128)(2,1)S(1)} %get-tuple-element.69), channel_id=1, source_target_pairs={{0,2},{2,0},{4,6},{6,4},{1,3},{3,1},{5,7},{7,5},{8,10},{10,8},{12,... | collective-permute-start | bytes 196616 | tf_op jit(solution)/shard_map/ppermute | solution.py:284
  35.1 1.7 %collective-permute-start.12 = (bf16[128,256]{1,0:T(8,128)(2,1)S(1)}, bf16[128,256]{1,0:T(8,128)(2,1)S(1)}, u32[]{:S(2)}, u32[]{:S(2)}) collective-permute-start(bf16[128,256]{1,0:T(8,128)(2,1)S(1)} %get-tuple-element.70), channel_id=1, source_target_pairs={{0,2},{2,0},{4,6},{6,4},{1,3},{3,1},{5,7},{7,5},{8,10},{10,8},{12,... | collective-permute-start | bytes 196616 | tf_op jit(solution)/shard_map/ppermute | solution.py:284

commit v6 on v5

--- a/solution.py
+++ b/solution.py
@@ -402,17 +402,15 @@
 
         near = [(0, 1, both, F32), (1, 2, ("key",), BF16), (1, 2, ("value",), BF16)]
         kept, sent = (2, 3, both, F32), (3, 4, both, BF16)
-        grads_b, scores_b, keep, send = sums_of("sums_middle", (2, 1), (2, 4), [kept, sent])
+        _, scores_b, *near_done, keep, send = sums_of("sums_middle", (2, 1), (0, 4), [*near, kept, sent])
         grads_c, scores_3, send = sums_of("sums_3", (3, 1), (3, 4), [sent], done=[send])
         scores_2, keep = sums_of("sums_2", (3, 1), (2, 3), [kept], [grads_c], [keep])
         part = (tok_dev, 4 * HD)
         (send,) = added(keep, swapped(send, 1), [shape(part)])
-        scores_01, own, *sends_1 = sums_of(
-            "sums_01", (2, 2), (0, 2), near, [grads_b, grads_c], after=[send]
-        )
+        scores_01, own, *sends_1 = sums_of("sums_01", (3, 1), (0, 2), near, [grads_c], near_done, [send])
         query_grad = query_of(
             [scores_a, scores_b, scores_01, scores_2, scores_3],
-            [((0, 0),), ((0, 1),), ((2, 0), (1, 0)), ((2, 1), (3, 0), (4, 0))],
+            [((0, 0),), ((0, 1),), ((1, 0),), ((2, 0), (3, 0), (4, 0))],
         )
         own_a, send_a = added(keep_a, arrived, [shape(part, F32), shape(part)], own)
         found = [own_a, swapped(send_a, 1)]

time: 38.4 us -> 38.2 us (level)
  Pallas kernels: 12.6 us -> 13.2 us
    ppermute x4, waiting for transfers between devices: 3.08 us -> 2.29 us  [across(): return lax.ppermute(part, ('pipe', 'head'), route)]
    pallas_call x5, Pallas kernels: 3.46 us -> 4.03 us  [sums_of(): call(functools.partial(sums_kernel, span, first, count, sends, 0 if grads...]
    ppermute x9, waiting for transfers between devices: 9.44 us -> 9.97 us  [swapped(): lax.ppermute(value, 'ctx', [(place, place ^ mask) for place in range(slot...]
  transfers between devices with their start and end apart: 13 -> 13, of which waited for: 6 -> 5; matrix products, arithmetic and copies ran while one was open for 0% -> 0% of each run, Pallas kernels for 28% -> 30%
where the time goes in v6:
time: 38.2 us; the launch traced here: 37.8 us
  Pallas kernels  13.2 us (35%)
  waiting for transfers between devices  12.3 us (32%)
  starting transfers between devices  11.6 us (30%)
  between operations  0.78 us (2%)
    ppermute x9, waiting for transfers between devices, swapped(): lax.ppermute(value, 'ctx', [(place, place ^ mask) for place in range(slot...  9.97 us
    ppermute x4, starting transfers between devices, across(): return lax.ppermute(part, ('pipe', 'head'), route)  5.95 us
    ppermute x9, starting transfers between devices, swapped(): lax.ppermute(value, 'ctx', [(place, place ^ mask) for place in range(slot...  5.62 us
    pallas_call x5, Pallas kernels, sums_of(): call(functools.partial(sums_kernel, span, first, count, sends, 0 if grads...  4.03 us
    pallas_call x1, Pallas kernels, per_device(): call(functools.partial(weights_kernel, slots, heads), 'weights', [shape((...  3.84 us
    ppermute x4, waiting for transfers between devices, across(): return lax.ppermute(part, ('pipe', 'head'), route)  2.29 us
    pallas_call x1, Pallas kernels, per_device(): call(functools.partial(later_load_kernel, sends[1:], split, heads, others...  1.66 us
    pallas_call x1, Pallas kernels, query_of(): call(functools.partial(query_kernel, slots, places, len(score_grads)), 'q...  1.61 us
  transfers between devices with their start and end apart: 13, of which 5 were waited for; matrix products, arithmetic and copies ran while one was open for 0% of the time, Pallas kernels for 30%

profile of v6, /device:TPU:24, one launch (start us, length us, event | category | flops | bytes accessed | tf_op | source)
XLA Modules:
  0.0 37.8 jit_solution(7901059658278067054)
XLA Ops:
  0.6 1.2 %first_load.1 = (bf16[64,3072]{1,0:T(8,128)(2,1)S(1)}, bf16[64,3072]{1,0:T(8,128)(2,1)S(1)}, bf16[128,1024]{1,0:T(8,128)(2,1)S(1)}) custom-call(bf16[64,8192]{1,0:T(8,128)(2,1)} %bitcast.9, bf16[128,512]{1,0:T(8,128)(2,1)} %bitcast.13, bf16[128,512]{1,0:T(8,128)(2,1)} %bitcast.14), custom_call_target="tpu_custom_call" | custom-call | flops 1024 | bytes 1024 | tf_op jit(solution)/shard_map/first_load/pallas_call | solution.py:301
  1.9 0.5 %collective-permute-start.3 = (bf16[64,3072]{1,0:T(8,128)(2,1)S(1)}, bf16[64,3072]{1,0:T(8,128)(2,1)S(1)}, u32[]{:S(2)}, u32[]{:S(2)}) collective-permute-start(bf16[64,3072]{1,0:T(8,128)(2,1)S(1)} %get-tuple-element.51), channel_id=1, source_target_pairs={{0,24},{1,25},{8,0},{9,1},{16,8},{17,9},{24,16},{25,17},{2,26},{3,... | collective-permute-start | bytes 1179656 | tf_op jit(solution)/shard_map/ppermute | solution.py:292
  2.4 1.4 %collective-permute-start.4 = (bf16[64,3072]{1,0:T(8,128)(2,1)S(1)}, bf16[64,3072]{1,0:T(8,128)(2,1)S(1)}, u32[]{:S(2)}, u32[]{:S(2)}) collective-permute-start(bf16[64,3072]{1,0:T(8,128)(2,1)S(1)} %get-tuple-element.52), channel_id=1, source_target_pairs={{0,25},{1,24},{8,1},{9,0},{16,9},{17,8},{24,17},{25,16},{2,27},{3,... | collective-permute-start | bytes 1179656 | tf_op jit(solution)/shard_map/ppermute | solution.py:292
  3.8 0.0 copy-start
  3.8 9.5 %conditional.1 = (bf16[128,1024]{1,0:T(8,128)(2,1)}, bf16[128,1024]{1,0:T(8,128)(2,1)}, bf16[128,1024]{1,0:T(8,128)(2,1)}) conditional(s32[]{:T(128)} %convert_element_type.3, bf16[128,1024]{1,0:T(8,128)(2,1)S(1)} %get-tuple-element.41.refs_0_.refs_5_, bf16[128,1024]{1,0:T(8,128)(2,1)S(1)} %get-tuple-element.41.refs_0_.refs_5_), branch_computations={%region_0.0_spmd, %region_1.0_spmd} | conditional | bytes 3145872 | solution.py:320
  3.8 1.5 %collective-permute-start.1 = (bf16[128,1024]{1,0:T(8,128)(2,1)S(1)}, bf16[128,1024]{1,0:T(8,128)(2,1)}, u32[]{:S(2)}, u32[]{:S(2)}) collective-permute-start(bf16[128,1024]{1,0:T(8,128)(2,1)S(1)} %param.1), channel_id=1, source_target_pairs={{0,4},{2,6},{4,0},{6,2},{1,5},{3,7},{5,1},{7,3},{8,12},{10,14},{12... | collective-permute-start | bytes 786440 | tf_op jit(solution)/shard_map/cond/branch_1_fun/ppermute | solution.py:284
  5.3 0.0 collective-permute-start
  5.3 6.1 %collective-permute-done.1 = bf16[128,1024]{1,0:T(8,128)(2,1)} collective-permute-done((bf16[128,1024]{1,0:T(8,128)(2,1)S(1)}, bf16[128,1024]{1,0:T(8,128)(2,1)}, u32[]{:S(2)}, u32[]{:S(2)}) %collective-permute-start.1) | collective-permute-done | bytes 262176 | tf_op jit(solution)/shard_map/cond/branch_1_fun/ppermute | solution.py:284
  11.4 0.0 collective-permute-start.2
  11.4 0.0 collective-permute-done
  11.4 1.9 %collective-permute-done.2 = bf16[128,1024]{1,0:T(8,128)(2,1)} collective-permute-done((bf16[128,1024]{1,0:T(8,128)(2,1)}, bf16[128,1024]{1,0:T(8,128)(2,1)}, u32[]{:S(2)}, u32[]{:S(2)}) %collective-permute-start.2) | collective-permute-done | bytes 262176 | tf_op jit(solution)/shard_map/cond/branch_1_fun/ppermute | solution.py:284
  13.2 1.7 %later_load.1 = (bf16[64,1024]{1,0:T(8,128)(2,1)S(1)}, bf16[64,1024]{1,0:T(8,128)(2,1)S(1)}, bf16[128,4096]{1,0:T(8,128)(2,1)S(1)}, bf16[128,1024]{1,0:T(8,128)(...) custom-call(bf16[64,8192]{1,0:T(8,128)(2,1)} %bitcast.10, bf16[128,4096]{1,0:T(8,128)(2,1)} %bitcast.11, ...), custom_call_target="tpu_custom_call" | custom-call | flops 1024 | bytes 1024 | tf_op jit(solution)/shard_map/later_load/pallas_call | solution.py:322
  14.9 0.5 %collective-permute-start.5 = (bf16[64,1024]{1,0:T(8,128)(2,1)S(1)}, bf16[64,1024]{1,0:T(8,128)(2,1)S(1)}, u32[]{:S(2)}, u32[]{:S(2)}) collective-permute-start(bf16[64,1024]{1,0:T(8,128)(2,1)S(1)} %get-tuple-element.59), channel_id=1, source_target_pairs={{0,24},{1,25},{8,0},{9,1},{16,8},{17,9},{24,16},{25,17},{2,26},{3,... | collective-permute-start | bytes 393224 | tf_op jit(solution)/shard_map/ppermute | solution.py:292
  15.4 3.5 %collective-permute-start.6 = (bf16[64,1024]{1,0:T(8,128)(2,1)S(1)}, bf16[64,1024]{1,0:T(8,128)(2,1)S(1)}, u32[]{:S(2)}, u32[]{:S(2)}) collective-permute-start(bf16[64,1024]{1,0:T(8,128)(2,1)S(1)} %get-tuple-element.60), channel_id=1, source_target_pairs={{0,25},{1,24},{8,1},{9,0},{16,9},{17,8},{24,17},{25,16},{2,27},{3,... | collective-permute-start | bytes 393224 | tf_op jit(solution)/shard_map/ppermute | solution.py:292
  19.0 0.0 copy-done
  19.0 3.8 %weights.1 = (bf16[4,512,1024]{2,1,0:T(8,128)(2,1)S(1)}, f32[128,4096]{1,0:T(8,128)S(1)}) custom-call(bf16[128,4096]{1,0:T(8,128)(2,1)S(1)} %get-tuple-element.45.q_ref, s32[4,2,8]{2,1,0:T(2,128)S(1)} %bitcast.8, bf16[128,1024]{1,0:T(8,128)(2,1)S(1)} %get-tuple-element.41.refs_0_.refs_5_, bf16[128,1024]{1,0:T(8,128)(2,1)S(1)} %get-tuple-element.46.refs_1_.refs_6_, ...), custom_call_target="tpu_custom_call" | custom-call | flops 1024 | bytes 1024 | tf_op jit(solution)/shard_map/weights/pallas_call | solution.py:340
  22.8 0.0 collective-permute-done.3.refs_4_
  22.8 2.3 %collective-permute-done.4.refs_5_ = bf16[64,3072]{1,0:T(8,128)(2,1)S(1)} collective-permute-done((bf16[64,3072]{1,0:T(8,128)(2,1)S(1)}, bf16[64,3072]{1,0:T(8,128)(2,1)S(1)}, u32[]{:S(2)}, u32[]{:S(2)}) %collective-permute-start.4) | collective-permute-done | bytes 393248 | tf_op jit(solution)/shard_map/ppermute | solution.py:292
  25.1 2.0 %sums_early.1 = (bf16[128,2048]{1,0:T(8,128)(2,1)}, bf16[2,512,1024]{2,1,0:T(8,128)(2,1)S(1)}, f32[256,512]{1,0:T(8,128)S(1)}, bf16[256,512]{1,0:T(8,128)(2,1)S(1)}) custom-call(bf16[4,512,1024]{2,1,0:T(8,128)(2,1)S(1)} %get-tuple-element.49.p_ref, f32[128,4096]{1,0:T(8,128)S(1)} %get-tuple-element.50.o_ref, bf16[128,4096]{1,0:T(8,128)(2,1)S(1)} %get-tuple-element.45.q_ref, ...), custom_call_target="tpu_custom_call" | custom-call | flops 1024 | bytes 1024 | tf_op jit(solution)/shard_map/sums_early/pallas_call | solution.py:359
  27.1 1.6 %collective-permute-start.8 = (bf16[256,512]{1,0:T(8,128)(2,1)S(1)}, bf16[256,512]{1,0:T(8,128)(2,1)S(1)}, u32[]{:S(2)}, u32[]{:S(2)}) collective-permute-start(bf16[256,512]{1,0:T(8,128)(2,1)S(1)} %get-tuple-element.69), channel_id=1, source_target_pairs={{0,4},{2,6},{4,0},{6,2},{1,5},{3,7},{5,1},{7,3},{8,12},{10,14},{12... | collective-permute-start | bytes 786440 | tf_op jit(solution)/shard_map/ppermute | solution.py:284
  28.7 1.2 %sums_middle.1 = (bf16[128,1024]{1,0:T(8,128)(2,1)}, bf16[1,512,1024]{2,1,0:T(8,128)(2,1)S(1)}, f32[128,256]{1,0:T(8,128)S(1)}, bf16[128,128]{1,0:T(8,128)(2,1)S...) custom-call(bf16[4,512,1024]{2,1,0:T(8,128)(2,1)S(1)} %get-tuple-element.49.p_ref, ...), custom_call_target="tpu_custom_call" | custom-call | flops 1024 | bytes 1024 | tf_op jit(solution)/shard_map/sums_middle/pallas_call | solution.py:359
  29.9 0.0 collective-permute-done.5.refs_2_
  29.9 0.0 collective-permute-done.6.refs_3_
  29.9 0.1 sums_3.1
  29.9 0.1 collective-permute-start.7
  30.0 0.1 sums_2.1
  30.1 1.3 %collective-permute-done.7.received_ref = bf16[128,512]{1,0:T(8,128)(2,1)S(1)} collective-permute-done((bf16[128,512]{1,0:T(8,128)(2,1)S(1)}, bf16[128,512]{1,0:T(8,128)(2,1)S(1)}, u32[]{:S(2)}, u32[]{:S(2)}) %collective-permute-start.7) | collective-permute-done | bytes 131104 | tf_op jit(solution)/shard_map/ppermute | solution.py:284
  31.4 1.8 %collective-permute-start.10 = (bf16[128,512]{1,0:T(8,128)(2,1)S(1)}, bf16[128,512]{1,0:T(8,128)(2,1)S(1)}, u32[]{:S(2)}, u32[]{:S(2)}) collective-permute-start(bf16[128,512]{1,0:T(8,128)(2,1)S(1)} %add.2.refs_6_), channel_id=1, source_target_pairs={{0,4},{2,6},{4,0},{6,2},{1,5},{3,7},{5,1},{7,3},{8,12},{10,14},{12... | collective-permute-start | bytes 393224 | tf_op jit(solution)/shard_map/ppermute | solution.py:284
  33.2 0.7 %sums_01.1 = (bf16[1,256,1024]{2,1,0:T(8,128)(2,1)S(1)}, f32[128,512]{1,0:T(8,128)S(1)}, bf16[128,256]{1,0:T(8,128)(2,1)S(1)}, bf16[128,256]{1,0:T(8,128)(2,1)S(1)}) custom-call(bf16[4,512,1024]{2,1,0:T(8,128)(2,1)S(1)} %get-tuple-element.49.p_ref, f32[128,4096]{1,0:T(8,128)S(1)} %get-tuple-element.50.o_ref, bf16[128,4096]{1,0:T(8,128)(2,1)S(1)} %get-tuple-element.45.q_ref, ...), custom_call_target="tpu_custom_call" | custom-call | flops 1024 | bytes 1024 | tf_op jit(solution)/shard_map/sums_01/pallas_call | solution.py:359
  34.0 0.0 collective-permute-done.8.received_ref
  34.0 0.1 collective-permute-start.9
  34.1 0.5 %collective-permute-start.11 = (bf16[128,256]{1,0:T(8,128)(2,1)S(1)}, bf16[128,256]{1,0:T(8,128)(2,1)S(1)}, u32[]{:S(2)}, u32[]{:S(2)}) collective-permute-start(bf16[128,256]{1,0:T(8,128)(2,1)S(1)} %get-tuple-element.73), channel_id=1, source_target_pairs={{0,2},{2,0},{4,6},{6,4},{1,3},{3,1},{5,7},{7,5},{8,10},{10,8},{12,... | collective-permute-start | bytes 196616 | tf_op jit(solution)/shard_map/ppermute | solution.py:284
  34.6 0.1 collective-permute-start.12
  34.7 1.6 %query.1 = bf16[128,4096]{1,0:T(8,128)(2,1)} custom-call(bf16[2,512,1024]{2,1,0:T(8,128)(2,1)S(1)} %get-tuple-element.53.refs_0_, bf16[1,512,1024]{2,1,0:T(8,128)(2,1)S(1)} %get-tuple-element.54.refs_1_, bf16[1,256,1024]{2,1,0:T(8,128)(2,1)S(1)} %get-tuple-element.65.refs_2_, bf16[1,128,1024]{2,1,0:T(8,128)(2,1)S(1)} %get-tuple-element.66.refs_3_, ...), custom_call_target="tpu_custom_call" | custom-call | flops 1024 | bytes 1024 | tf_op jit(solution)/shard_map/query/pallas_call | solution.py:378
  36.3 0.0 collective-permute-done.11.refs_4_
  36.3 0.0 collective-permute-done.12.refs_5_
  36.3 0.7 %collective-permute-done.10.refs_3_ = bf16[128,512]{1,0:T(8,128)(2,1)S(1)} collective-permute-done((bf16[128,512]{1,0:T(8,128)(2,1)S(1)}, bf16[128,512]{1,0:T(8,128)(2,1)S(1)}, u32[]{:S(2)}, u32[]{:S(2)}) %collective-permute-start.10) | collective-permute-done | bytes 131104 | tf_op jit(solution)/shard_map/ppermute | solution.py:284
  37.0 0.0 collective-permute-done.9.refs_1_
  37.0 0.7 %finish.1 = (bf16[128,512]{1,0:T(8,128)(2,1)}, bf16[128,512]{1,0:T(8,128)(2,1)}) custom-call(f32[128,512]{1,0:T(8,128)S(1)} %get-tuple-element.71.refs_0_, bf16[128,512]{1,0:T(8,128)(2,1)S(1)} %collective-permute-done.9.refs_1_, f32[128,512]{1,0:T(8,128)S(1)} %get-tuple-element.70.refs_0_.refs_2_, bf16[128,512]{1,0:T(8,128)(2,1)S(1)} %collective-permute-done.10.refs_3_, ...), custom_call_target="tpu_custom_call" | custom-call | flops 1024 | bytes 1024 | tf_op jit(solution)/shard_map/finish/pallas_call | solution.py:426
  (2 shorter events, 0.1 us)
Async XLA Ops:
  1.9 20.9 %collective-permute-start.3 = (bf16[64,3072]{1,0:T(8,128)(2,1)S(1)}, bf16[64,3072]{1,0:T(8,128)(2,1)S(1)}, u32[]{:S(2)}, u32[]{:S(2)}) collective-permute-start(bf16[64,3072]{1,0:T(8,128)(2,1)S(1)} %get-tuple-element.51), channel_id=1, source_target_pairs={{0,24},{1,25},{8,0},{9,1},{16,8},{17,9},{24,16},{25,17},{2,26},{3,... | collective-permute-start | bytes 1179656 | tf_op jit(solution)/shard_map/ppermute | solution.py:292
  2.4 22.7 %collective-permute-start.4 = (bf16[64,3072]{1,0:T(8,128)(2,1)S(1)}, bf16[64,3072]{1,0:T(8,128)(2,1)S(1)}, u32[]{:S(2)}, u32[]{:S(2)}) collective-permute-start(bf16[64,3072]{1,0:T(8,128)(2,1)S(1)} %get-tuple-element.52), channel_id=1, source_target_pairs={{0,25},{1,24},{8,1},{9,0},{16,9},{17,8},{24,17},{25,16},{2,27},{3,... | collective-permute-start | bytes 1179656 | tf_op jit(solution)/shard_map/ppermute | solution.py:292
  3.8 15.2 %copy-start = (s32[1,4,2,8]{3,2,1,0:T(2,128)S(1)}, s32[1,4,2,8]{3,2,1,0:T(2,128)}, u32[]{:S(2)}) copy-start(s32[1,4,2,8]{3,2,1,0:T(2,128)} %param.11) | copy-start | bytes 772
  3.8 7.6 %collective-permute-start.1 = (bf16[128,1024]{1,0:T(8,128)(2,1)S(1)}, bf16[128,1024]{1,0:T(8,128)(2,1)}, u32[]{:S(2)}, u32[]{:S(2)}) collective-permute-start(bf16[128,1024]{1,0:T(8,128)(2,1)S(1)} %param.1), channel_id=1, source_target_pairs={{0,4},{2,6},{4,0},{6,2},{1,5},{3,7},{5,1},{7,3},{8,12},{10,14},{12... | collective-permute-start | bytes 786440 | tf_op jit(solution)/shard_map/cond/branch_1_fun/ppermute | solution.py:284
  5.3 6.1 %collective-permute-start = (bf16[128,1024]{1,0:T(8,128)(2,1)S(1)}, bf16[128,1024]{1,0:T(8,128)(2,1)}, u32[]{:S(2)}, u32[]{:S(2)}) collective-permute-start(bf16[128,1024]{1,0:T(8,128)(2,1)S(1)} %param.1), channel_id=1, source_target_pairs={{0,2},{2,0},{4,6},{6,4},{1,3},{3,1},{5,7},{7,5},{8,10},{10,8},{12,... | collective-permute-start | bytes 786440 | tf_op jit(solution)/shard_map/cond/branch_1_fun/ppermute | solution.py:284
  11.4 1.9 %collective-permute-start.2 = (bf16[128,1024]{1,0:T(8,128)(2,1)}, bf16[128,1024]{1,0:T(8,128)(2,1)}, u32[]{:S(2)}, u32[]{:S(2)}) collective-permute-start(bf16[128,1024]{1,0:T(8,128)(2,1)} %collective-permute-done.1), channel_id=1, source_target_pairs={{0,2},{2,0},{4,6},{6,4},{1,3},{3,1},{5,7},{7,5},{8,10},{10,8},{12,... | collective-permute-start | bytes 786440 | tf_op jit(solution)/shard_map/cond/branch_1_fun/ppermute | solution.py:284
  14.9 14.9 %collective-permute-start.5 = (bf16[64,1024]{1,0:T(8,128)(2,1)S(1)}, bf16[64,1024]{1,0:T(8,128)(2,1)S(1)}, u32[]{:S(2)}, u32[]{:S(2)}) collective-permute-start(bf16[64,1024]{1,0:T(8,128)(2,1)S(1)} %get-tuple-element.59), channel_id=1, source_target_pairs={{0,24},{1,25},{8,0},{9,1},{16,8},{17,9},{24,16},{25,17},{2,26},{3,... | collective-permute-start | bytes 393224 | tf_op jit(solution)/shard_map/ppermute | solution.py:292
  15.4 14.5 %collective-permute-start.6 = (bf16[64,1024]{1,0:T(8,128)(2,1)S(1)}, bf16[64,1024]{1,0:T(8,128)(2,1)S(1)}, u32[]{:S(2)}, u32[]{:S(2)}) collective-permute-start(bf16[64,1024]{1,0:T(8,128)(2,1)S(1)} %get-tuple-element.60), channel_id=1, source_target_pairs={{0,25},{1,24},{8,1},{9,0},{16,9},{17,8},{24,17},{25,16},{2,27},{3,... | collective-permute-start | bytes 393224 | tf_op jit(solution)/shard_map/ppermute | solution.py:292
  27.1 6.8 %collective-permute-start.8 = (bf16[256,512]{1,0:T(8,128)(2,1)S(1)}, bf16[256,512]{1,0:T(8,128)(2,1)S(1)}, u32[]{:S(2)}, u32[]{:S(2)}) collective-permute-start(bf16[256,512]{1,0:T(8,128)(2,1)S(1)} %get-tuple-element.69), channel_id=1, source_target_pairs={{0,4},{2,6},{4,0},{6,2},{1,5},{3,7},{5,1},{7,3},{8,12},{10,14},{12... | collective-permute-start | bytes 786440 | tf_op jit(solution)/shard_map/ppermute | solution.py:284
  29.9 1.4 %collective-permute-start.7 = (bf16[128,512]{1,0:T(8,128)(2,1)S(1)}, bf16[128,512]{1,0:T(8,128)(2,1)S(1)}, u32[]{:S(2)}, u32[]{:S(2)}) collective-permute-start(bf16[128,512]{1,0:T(8,128)(2,1)S(1)} %get-tuple-element.64), channel_id=1, source_target_pairs={{0,2},{2,0},{4,6},{6,4},{1,3},{3,1},{5,7},{7,5},{8,10},{10,8},{12,... | collective-permute-start | bytes 393224 | tf_op jit(solution)/shard_map/ppermute | solution.py:284
  31.4 5.7 %collective-permute-start.10 = (bf16[128,512]{1,0:T(8,128)(2,1)S(1)}, bf16[128,512]{1,0:T(8,128)(2,1)S(1)}, u32[]{:S(2)}, u32[]{:S(2)}) collective-permute-start(bf16[128,512]{1,0:T(8,128)(2,1)S(1)} %add.2.refs_6_), channel_id=1, source_target_pairs={{0,4},{2,6},{4,0},{6,2},{1,5},{3,7},{5,1},{7,3},{8,12},{10,14},{12... | collective-permute-start | bytes 393224 | tf_op jit(solution)/shard_map/ppermute | solution.py:284
  34.0 3.0 %collective-permute-start.9 = (bf16[128,512]{1,0:T(8,128)(2,1)S(1)}, bf16[128,512]{1,0:T(8,128)(2,1)S(1)}, u32[]{:S(2)}, u32[]{:S(2)}) collective-permute-start(bf16[128,512]{1,0:T(8,128)(2,1)S(1)} %get-tuple-element.72), channel_id=1, source_target_pairs={{0,2},{2,0},{4,6},{6,4},{1,3},{3,1},{5,7},{7,5},{8,10},{10,8},{12,... | collective-permute-start | bytes 393224 | tf_op jit(solution)/shard_map/ppermute | solution.py:284
  34.1 2.2 %collective-permute-start.11 = (bf16[128,256]{1,0:T(8,128)(2,1)S(1)}, bf16[128,256]{1,0:T(8,128)(2,1)S(1)}, u32[]{:S(2)}, u32[]{:S(2)}) collective-permute-start(bf16[128,256]{1,0:T(8,128)(2,1)S(1)} %get-tuple-element.73), channel_id=1, source_target_pairs={{0,2},{2,0},{4,6},{6,4},{1,3},{3,1},{5,7},{7,5},{8,10},{10,8},{12,... | collective-permute-start | bytes 196616 | tf_op jit(solution)/shard_map/ppermute | solution.py:284
  34.6 1.7 %collective-permute-start.12 = (bf16[128,256]{1,0:T(8,128)(2,1)S(1)}, bf16[128,256]{1,0:T(8,128)(2,1)S(1)}, u32[]{:S(2)}, u32[]{:S(2)}) collective-permute-start(bf16[128,256]{1,0:T(8,128)(2,1)S(1)} %get-tuple-element.74), channel_id=1, source_target_pairs={{0,2},{2,0},{4,6},{6,4},{1,3},{3,1},{5,7},{7,5},{8,10},{10,8},{12,... | collective-permute-start | bytes 196616 | tf_op jit(solution)/shard_map/ppermute | solution.py:284

commit v7 on v6

--- a/solution.py
+++ b/solution.py
@@ -400,7 +400,7 @@
         )
         arrived = swapped(send, 2)
 
-        near = [(0, 1, both, F32), (1, 2, ("key",), BF16), (1, 2, ("value",), BF16)]
+        near = [(0, 1, both, F32), (1, 2, both, BF16)]
         kept, sent = (2, 3, both, F32), (3, 4, both, BF16)
         _, scores_b, *near_done, keep, send = sums_of("sums_middle", (2, 1), (0, 4), [*near, kept, sent])
         grads_c, scores_3, send = sums_of("sums_3", (3, 1), (3, 4), [sent], done=[send])
@@ -415,7 +415,7 @@
         own_a, send_a = added(keep_a, arrived, [shape(part, F32), shape(part)], own)
         found = [own_a, swapped(send_a, 1)]
         found.extend([own, swapped(send, 2), *(swapped(part, 1) for part in sends_1)])
-        counts = [(2, 0), (2, 1)]
+        counts = [(2, 0), (3, 0)]
     else:
         layout = [(0, 1, both, F32)] + [(slot, slot + 1, both, BF16) for slot in range(1, slots)]
         _, scores, own, *send = sums_of("sums", groups[0], (0, slots), layout)

time: 38.2 us -> 38.2 us (level)
    ppermute x9 -> x8, waiting for transfers between devices: 9.97 us -> 10 us  [swapped(): lax.ppermute(value, 'ctx', [(place, place ^ mask) for place in range(slot...]
    ppermute x9 -> x8, starting transfers between devices: 5.62 us -> 5.59 us  [swapped(): lax.ppermute(value, 'ctx', [(place, place ^ mask) for place in range(slot...]
  transfers between devices with their start and end apart: 13 -> 12, of which waited for: 5 -> 5; matrix products, arithmetic and copies ran while one was open for 0% -> 0% of each run, Pallas kernels for 30% -> 30%
where the time goes in v7:
time: 38.2 us; the launch traced here: 37.8 us
  Pallas kernels  13.2 us (35%)
  waiting for transfers between devices  12.3 us (32%)
  starting transfers between devices  11.5 us (30%)
  between operations  0.76 us (2%)
    ppermute x8, waiting for transfers between devices, swapped(): lax.ppermute(value, 'ctx', [(place, place ^ mask) for place in range(slot...  10 us
    ppermute x4, starting transfers between devices, across(): return lax.ppermute(part, ('pipe', 'head'), route)  5.95 us
    ppermute x8, starting transfers between devices, swapped(): lax.ppermute(value, 'ctx', [(place, place ^ mask) for place in range(slot...  5.59 us
    pallas_call x5, Pallas kernels, sums_of(): call(functools.partial(sums_kernel, span, first, count, sends, 0 if grads...  4.03 us
    pallas_call x1, Pallas kernels, per_device(): call(functools.partial(weights_kernel, slots, heads), 'weights', [shape((...  3.84 us
    ppermute x4, waiting for transfers between devices, across(): return lax.ppermute(part, ('pipe', 'head'), route)  2.29 us
    pallas_call x1, Pallas kernels, per_device(): call(functools.partial(later_load_kernel, sends[1:], split, heads, others...  1.66 us
    pallas_call x1, Pallas kernels, query_of(): call(functools.partial(query_kernel, slots, places, len(score_grads)), 'q...  1.6 us
  transfers between devices with their start and end apart: 12, of which 5 were waited for; matrix products, arithmetic and copies ran while one was open for 0% of the time, Pallas kernels for 30%

profile of v7, /device:TPU:24, one launch (start us, length us, event | category | flops | bytes accessed | tf_op | source)
XLA Modules:
  0.0 37.8 jit_solution(15345345486009733956)
XLA Ops:
  0.6 1.2 %first_load.1 = (bf16[64,3072]{1,0:T(8,128)(2,1)S(1)}, bf16[64,3072]{1,0:T(8,128)(2,1)S(1)}, bf16[128,1024]{1,0:T(8,128)(2,1)S(1)}) custom-call(bf16[64,8192]{1,0:T(8,128)(2,1)} %bitcast.9, bf16[128,512]{1,0:T(8,128)(2,1)} %bitcast.13, bf16[128,512]{1,0:T(8,128)(2,1)} %bitcast.14), custom_call_target="tpu_custom_call" | custom-call | flops 1024 | bytes 1024 | tf_op jit(solution)/shard_map/first_load/pallas_call | solution.py:301
  1.9 0.5 %collective-permute-start.3 = (bf16[64,3072]{1,0:T(8,128)(2,1)S(1)}, bf16[64,3072]{1,0:T(8,128)(2,1)S(1)}, u32[]{:S(2)}, u32[]{:S(2)}) collective-permute-start(bf16[64,3072]{1,0:T(8,128)(2,1)S(1)} %get-tuple-element.49), channel_id=1, source_target_pairs={{0,24},{1,25},{8,0},{9,1},{16,8},{17,9},{24,16},{25,17},{2,26},{3,... | collective-permute-start | bytes 1179656 | tf_op jit(solution)/shard_map/ppermute | solution.py:292
  2.4 1.4 %collective-permute-start.4 = (bf16[64,3072]{1,0:T(8,128)(2,1)S(1)}, bf16[64,3072]{1,0:T(8,128)(2,1)S(1)}, u32[]{:S(2)}, u32[]{:S(2)}) collective-permute-start(bf16[64,3072]{1,0:T(8,128)(2,1)S(1)} %get-tuple-element.50), channel_id=1, source_target_pairs={{0,25},{1,24},{8,1},{9,0},{16,9},{17,8},{24,17},{25,16},{2,27},{3,... | collective-permute-start | bytes 1179656 | tf_op jit(solution)/shard_map/ppermute | solution.py:292
  3.8 0.0 copy-start
  3.8 9.5 %conditional.1 = (bf16[128,1024]{1,0:T(8,128)(2,1)}, bf16[128,1024]{1,0:T(8,128)(2,1)}, bf16[128,1024]{1,0:T(8,128)(2,1)}) conditional(s32[]{:T(128)} %convert_element_type.3, bf16[128,1024]{1,0:T(8,128)(2,1)S(1)} %get-tuple-element.39.refs_0_.refs_5_, bf16[128,1024]{1,0:T(8,128)(2,1)S(1)} %get-tuple-element.39.refs_0_.refs_5_), branch_computations={%region_0.0_spmd, %region_1.0_spmd} | conditional | bytes 3145872 | solution.py:320
  3.8 1.5 %collective-permute-start.1 = (bf16[128,1024]{1,0:T(8,128)(2,1)S(1)}, bf16[128,1024]{1,0:T(8,128)(2,1)}, u32[]{:S(2)}, u32[]{:S(2)}) collective-permute-start(bf16[128,1024]{1,0:T(8,128)(2,1)S(1)} %param.1), channel_id=1, source_target_pairs={{0,4},{2,6},{4,0},{6,2},{1,5},{3,7},{5,1},{7,3},{8,12},{10,14},{12... | collective-permute-start | bytes 786440 | tf_op jit(solution)/shard_map/cond/branch_1_fun/ppermute | solution.py:284
  5.3 0.0 collective-permute-start
  5.3 6.1 %collective-permute-done.1 = bf16[128,1024]{1,0:T(8,128)(2,1)} collective-permute-done((bf16[128,1024]{1,0:T(8,128)(2,1)S(1)}, bf16[128,1024]{1,0:T(8,128)(2,1)}, u32[]{:S(2)}, u32[]{:S(2)}) %collective-permute-start.1) | collective-permute-done | bytes 262176 | tf_op jit(solution)/shard_map/cond/branch_1_fun/ppermute | solution.py:284
  11.4 0.0 collective-permute-start.2
  11.4 0.0 collective-permute-done
  11.4 1.9 %collective-permute-done.2 = bf16[128,1024]{1,0:T(8,128)(2,1)} collective-permute-done((bf16[128,1024]{1,0:T(8,128)(2,1)}, bf16[128,1024]{1,0:T(8,128)(2,1)}, u32[]{:S(2)}, u32[]{:S(2)}) %collective-permute-start.2) | collective-permute-done | bytes 262176 | tf_op jit(solution)/shard_map/cond/branch_1_fun/ppermute | solution.py:284
  13.2 1.7 %later_load.1 = (bf16[64,1024]{1,0:T(8,128)(2,1)S(1)}, bf16[64,1024]{1,0:T(8,128)(2,1)S(1)}, bf16[128,4096]{1,0:T(8,128)(2,1)S(1)}, bf16[128,1024]{1,0:T(8,128)(...) custom-call(bf16[64,8192]{1,0:T(8,128)(2,1)} %bitcast.10, bf16[128,4096]{1,0:T(8,128)(2,1)} %bitcast.11, ...), custom_call_target="tpu_custom_call" | custom-call | flops 1024 | bytes 1024 | tf_op jit(solution)/shard_map/later_load/pallas_call | solution.py:322
  14.9 0.5 %collective-permute-start.5 = (bf16[64,1024]{1,0:T(8,128)(2,1)S(1)}, bf16[64,1024]{1,0:T(8,128)(2,1)S(1)}, u32[]{:S(2)}, u32[]{:S(2)}) collective-permute-start(bf16[64,1024]{1,0:T(8,128)(2,1)S(1)} %get-tuple-element.56), channel_id=1, source_target_pairs={{0,24},{1,25},{8,0},{9,1},{16,8},{17,9},{24,16},{25,17},{2,26},{3,... | collective-permute-start | bytes 393224 | tf_op jit(solution)/shard_map/ppermute | solution.py:292
  15.4 3.5 %collective-permute-start.6 = (bf16[64,1024]{1,0:T(8,128)(2,1)S(1)}, bf16[64,1024]{1,0:T(8,128)(2,1)S(1)}, u32[]{:S(2)}, u32[]{:S(2)}) collective-permute-start(bf16[64,1024]{1,0:T(8,128)(2,1)S(1)} %get-tuple-element.57), channel_id=1, source_target_pairs={{0,25},{1,24},{8,1},{9,0},{16,9},{17,8},{24,17},{25,16},{2,27},{3,... | collective-permute-start | bytes 393224 | tf_op jit(solution)/shard_map/ppermute | solution.py:292
  19.0 0.0 copy-done
  19.0 3.8 %weights.1 = (bf16[4,512,1024]{2,1,0:T(8,128)(2,1)S(1)}, f32[128,4096]{1,0:T(8,128)S(1)}) custom-call(bf16[128,4096]{1,0:T(8,128)(2,1)S(1)} %get-tuple-element.43.q_ref, s32[4,2,8]{2,1,0:T(2,128)S(1)} %bitcast.8, bf16[128,1024]{1,0:T(8,128)(2,1)S(1)} %get-tuple-element.39.refs_0_.refs_5_, bf16[128,1024]{1,0:T(8,128)(2,1)S(1)} %get-tuple-element.44.refs_1_.refs_6_, ...), custom_call_target="tpu_custom_call" | custom-call | flops 1024 | bytes 1024 | tf_op jit(solution)/shard_map/weights/pallas_call | solution.py:340
  22.8 0.0 collective-permute-done.3.refs_4_
  22.8 2.3 %collective-permute-done.4.refs_5_ = bf16[64,3072]{1,0:T(8,128)(2,1)S(1)} collective-permute-done((bf16[64,3072]{1,0:T(8,128)(2,1)S(1)}, bf16[64,3072]{1,0:T(8,128)(2,1)S(1)}, u32[]{:S(2)}, u32[]{:S(2)}) %collective-permute-start.4) | collective-permute-done | bytes 393248 | tf_op jit(solution)/shard_map/ppermute | solution.py:292
  25.1 2.0 %sums_early.1 = (bf16[128,2048]{1,0:T(8,128)(2,1)}, bf16[2,512,1024]{2,1,0:T(8,128)(2,1)S(1)}, f32[256,512]{1,0:T(8,128)S(1)}, bf16[256,512]{1,0:T(8,128)(2,1)S(1)}) custom-call(bf16[4,512,1024]{2,1,0:T(8,128)(2,1)S(1)} %get-tuple-element.47.p_ref, f32[128,4096]{1,0:T(8,128)S(1)} %get-tuple-element.48.o_ref, bf16[128,4096]{1,0:T(8,128)(2,1)S(1)} %get-tuple-element.43.q_ref, ...), custom_call_target="tpu_custom_call" | custom-call | flops 1024 | bytes 1024 | tf_op jit(solution)/shard_map/sums_early/pallas_call | solution.py:359
  27.1 1.6 %collective-permute-start.8 = (bf16[256,512]{1,0:T(8,128)(2,1)S(1)}, bf16[256,512]{1,0:T(8,128)(2,1)S(1)}, u32[]{:S(2)}, u32[]{:S(2)}) collective-permute-start(bf16[256,512]{1,0:T(8,128)(2,1)S(1)} %get-tuple-element.66), channel_id=1, source_target_pairs={{0,4},{2,6},{4,0},{6,2},{1,5},{3,7},{5,1},{7,3},{8,12},{10,14},{12... | collective-permute-start | bytes 786440 | tf_op jit(solution)/shard_map/ppermute | solution.py:284
  28.7 1.2 %sums_middle.1 = (bf16[128,1024]{1,0:T(8,128)(2,1)}, bf16[1,512,1024]{2,1,0:T(8,128)(2,1)S(1)}, f32[128,256]{1,0:T(8,128)S(1)}, bf16[128,256]{1,0:T(8,128)(2,1)S...) custom-call(bf16[4,512,1024]{2,1,0:T(8,128)(2,1)S(1)} %get-tuple-element.47.p_ref, ...), custom_call_target="tpu_custom_call" | custom-call | flops 1024 | bytes 1024 | tf_op jit(solution)/shard_map/sums_middle/pallas_call | solution.py:359
  29.9 0.0 collective-permute-done.5.refs_2_
  29.9 0.0 collective-permute-done.6.refs_3_
  29.9 0.1 sums_3.1
  29.9 0.1 collective-permute-start.7
  30.0 0.1 sums_2.1
  30.1 1.3 %collective-permute-done.7.received_ref = bf16[128,512]{1,0:T(8,128)(2,1)S(1)} collective-permute-done((bf16[128,512]{1,0:T(8,128)(2,1)S(1)}, bf16[128,512]{1,0:T(8,128)(2,1)S(1)}, u32[]{:S(2)}, u32[]{:S(2)}) %collective-permute-start.7) | collective-permute-done | bytes 131104 | tf_op jit(solution)/shard_map/ppermute | solution.py:284
  31.4 1.8 %collective-permute-start.10 = (bf16[128,512]{1,0:T(8,128)(2,1)S(1)}, bf16[128,512]{1,0:T(8,128)(2,1)S(1)}, u32[]{:S(2)}, u32[]{:S(2)}) collective-permute-start(bf16[128,512]{1,0:T(8,128)(2,1)S(1)} %add.2.refs_5_), channel_id=1, source_target_pairs={{0,4},{2,6},{4,0},{6,2},{1,5},{3,7},{5,1},{7,3},{8,12},{10,14},{12... | collective-permute-start | bytes 393224 | tf_op jit(solution)/shard_map/ppermute | solution.py:284
  33.2 0.7 %sums_01.1 = (bf16[1,256,1024]{2,1,0:T(8,128)(2,1)S(1)}, f32[128,512]{1,0:T(8,128)S(1)}, bf16[128,512]{1,0:T(8,128)(2,1)S(1)}) custom-call(bf16[4,512,1024]{2,1,0:T(8,128)(2,1)S(1)} %get-tuple-element.47.p_ref, f32[128,4096]{1,0:T(8,128)S(1)} %get-tuple-element.48.o_ref, bf16[128,4096]{1,0:T(8,128)(2,1)S(1)} %get-tuple-element.43.q_ref, ...), custom_call_target="tpu_custom_call" | custom-call | flops 1024 | bytes 1024 | tf_op jit(solution)/shard_map/sums_01/pallas_call | solution.py:359
  34.0 0.1 collective-permute-start.11
  34.0 0.0 collective-permute-done.8.received_ref
  34.1 0.5 %collective-permute-start.9 = (bf16[128,512]{1,0:T(8,128)(2,1)S(1)}, bf16[128,512]{1,0:T(8,128)(2,1)S(1)}, u32[]{:S(2)}, u32[]{:S(2)}) collective-permute-start(bf16[128,512]{1,0:T(8,128)(2,1)S(1)} %get-tuple-element.69), channel_id=1, source_target_pairs={{0,2},{2,0},{4,6},{6,4},{1,3},{3,1},{5,7},{7,5},{8,10},{10,8},{12,... | collective-permute-start | bytes 393224 | tf_op jit(solution)/shard_map/ppermute | solution.py:284
  34.7 1.6 %query.1 = bf16[128,4096]{1,0:T(8,128)(2,1)} custom-call(bf16[2,512,1024]{2,1,0:T(8,128)(2,1)S(1)} %get-tuple-element.51.refs_0_, bf16[1,512,1024]{2,1,0:T(8,128)(2,1)S(1)} %get-tuple-element.52.refs_1_, bf16[1,256,1024]{2,1,0:T(8,128)(2,1)S(1)} %get-tuple-element.62.refs_2_, bf16[1,128,1024]{2,1,0:T(8,128)(2,1)S(1)} %get-tuple-element.63.refs_3_, ...), custom_call_target="tpu_custom_call" | custom-call | flops 1024 | bytes 1024 | tf_op jit(solution)/shard_map/query/pallas_call | solution.py:378
  36.3 0.8 %collective-permute-done.10.refs_3_ = bf16[128,512]{1,0:T(8,128)(2,1)S(1)} collective-permute-done((bf16[128,512]{1,0:T(8,128)(2,1)S(1)}, bf16[128,512]{1,0:T(8,128)(2,1)S(1)}, u32[]{:S(2)}, u32[]{:S(2)}) %collective-permute-start.10) | collective-permute-done | bytes 131104 | tf_op jit(solution)/shard_map/ppermute | solution.py:284
  37.0 0.0 collective-permute-done.11.refs_4_
  37.0 0.0 collective-permute-done.9.refs_1_
  37.0 0.7 %finish.1 = (bf16[128,512]{1,0:T(8,128)(2,1)}, bf16[128,512]{1,0:T(8,128)(2,1)}) custom-call(f32[128,512]{1,0:T(8,128)S(1)} %get-tuple-element.68.refs_0_, bf16[128,512]{1,0:T(8,128)(2,1)S(1)} %collective-permute-done.9.refs_1_, f32[128,512]{1,0:T(8,128)S(1)} %get-tuple-element.67.refs_0_.refs_2_, bf16[128,512]{1,0:T(8,128)(2,1)S(1)} %collective-permute-done.10.refs_3_, ...), custom_call_target="tpu_custom_call" | custom-call | flops 1024 | bytes 1024 | tf_op jit(solution)/shard_map/finish/pallas_call | solution.py:426
  (2 shorter events, 0.1 us)
Async XLA Ops:
  1.9 20.9 %collective-permute-start.3 = (bf16[64,3072]{1,0:T(8,128)(2,1)S(1)}, bf16[64,3072]{1,0:T(8,128)(2,1)S(1)}, u32[]{:S(2)}, u32[]{:S(2)}) collective-permute-start(bf16[64,3072]{1,0:T(8,128)(2,1)S(1)} %get-tuple-element.49), channel_id=1, source_target_pairs={{0,24},{1,25},{8,0},{9,1},{16,8},{17,9},{24,16},{25,17},{2,26},{3,... | collective-permute-start | bytes 1179656 | tf_op jit(solution)/shard_map/ppermute | solution.py:292
  2.4 22.7 %collective-permute-start.4 = (bf16[64,3072]{1,0:T(8,128)(2,1)S(1)}, bf16[64,3072]{1,0:T(8,128)(2,1)S(1)}, u32[]{:S(2)}, u32[]{:S(2)}) collective-permute-start(bf16[64,3072]{1,0:T(8,128)(2,1)S(1)} %get-tuple-element.50), channel_id=1, source_target_pairs={{0,25},{1,24},{8,1},{9,0},{16,9},{17,8},{24,17},{25,16},{2,27},{3,... | collective-permute-start | bytes 1179656 | tf_op jit(solution)/shard_map/ppermute | solution.py:292
  3.8 15.2 %copy-start = (s32[1,4,2,8]{3,2,1,0:T(2,128)S(1)}, s32[1,4,2,8]{3,2,1,0:T(2,128)}, u32[]{:S(2)}) copy-start(s32[1,4,2,8]{3,2,1,0:T(2,128)} %param.11) | copy-start | bytes 772
  3.8 7.6 %collective-permute-start.1 = (bf16[128,1024]{1,0:T(8,128)(2,1)S(1)}, bf16[128,1024]{1,0:T(8,128)(2,1)}, u32[]{:S(2)}, u32[]{:S(2)}) collective-permute-start(bf16[128,1024]{1,0:T(8,128)(2,1)S(1)} %param.1), channel_id=1, source_target_pairs={{0,4},{2,6},{4,0},{6,2},{1,5},{3,7},{5,1},{7,3},{8,12},{10,14},{12... | collective-permute-start | bytes 786440 | tf_op jit(solution)/shard_map/cond/branch_1_fun/ppermute | solution.py:284
  5.3 6.1 %collective-permute-start = (bf16[128,1024]{1,0:T(8,128)(2,1)S(1)}, bf16[128,1024]{1,0:T(8,128)(2,1)}, u32[]{:S(2)}, u32[]{:S(2)}) collective-permute-start(bf16[128,1024]{1,0:T(8,128)(2,1)S(1)} %param.1), channel_id=1, source_target_pairs={{0,2},{2,0},{4,6},{6,4},{1,3},{3,1},{5,7},{7,5},{8,10},{10,8},{12,... | collective-permute-start | bytes 786440 | tf_op jit(solution)/shard_map/cond/branch_1_fun/ppermute | solution.py:284
  11.4 1.9 %collective-permute-start.2 = (bf16[128,1024]{1,0:T(8,128)(2,1)}, bf16[128,1024]{1,0:T(8,128)(2,1)}, u32[]{:S(2)}, u32[]{:S(2)}) collective-permute-start(bf16[128,1024]{1,0:T(8,128)(2,1)} %collective-permute-done.1), channel_id=1, source_target_pairs={{0,2},{2,0},{4,6},{6,4},{1,3},{3,1},{5,7},{7,5},{8,10},{10,8},{12,... | collective-permute-start | bytes 786440 | tf_op jit(solution)/shard_map/cond/branch_1_fun/ppermute | solution.py:284
  14.9 14.9 %collective-permute-start.5 = (bf16[64,1024]{1,0:T(8,128)(2,1)S(1)}, bf16[64,1024]{1,0:T(8,128)(2,1)S(1)}, u32[]{:S(2)}, u32[]{:S(2)}) collective-permute-start(bf16[64,1024]{1,0:T(8,128)(2,1)S(1)} %get-tuple-element.56), channel_id=1, source_target_pairs={{0,24},{1,25},{8,0},{9,1},{16,8},{17,9},{24,16},{25,17},{2,26},{3,... | collective-permute-start | bytes 393224 | tf_op jit(solution)/shard_map/ppermute | solution.py:292
  15.4 14.5 %collective-permute-start.6 = (bf16[64,1024]{1,0:T(8,128)(2,1)S(1)}, bf16[64,1024]{1,0:T(8,128)(2,1)S(1)}, u32[]{:S(2)}, u32[]{:S(2)}) collective-permute-start(bf16[64,1024]{1,0:T(8,128)(2,1)S(1)} %get-tuple-element.57), channel_id=1, source_target_pairs={{0,25},{1,24},{8,1},{9,0},{16,9},{17,8},{24,17},{25,16},{2,27},{3,... | collective-permute-start | bytes 393224 | tf_op jit(solution)/shard_map/ppermute | solution.py:292
  27.1 6.9 %collective-permute-start.8 = (bf16[256,512]{1,0:T(8,128)(2,1)S(1)}, bf16[256,512]{1,0:T(8,128)(2,1)S(1)}, u32[]{:S(2)}, u32[]{:S(2)}) collective-permute-start(bf16[256,512]{1,0:T(8,128)(2,1)S(1)} %get-tuple-element.66), channel_id=1, source_target_pairs={{0,4},{2,6},{4,0},{6,2},{1,5},{3,7},{5,1},{7,3},{8,12},{10,14},{12... | collective-permute-start | bytes 786440 | tf_op jit(solution)/shard_map/ppermute | solution.py:284
  29.9 1.4 %collective-permute-start.7 = (bf16[128,512]{1,0:T(8,128)(2,1)S(1)}, bf16[128,512]{1,0:T(8,128)(2,1)S(1)}, u32[]{:S(2)}, u32[]{:S(2)}) collective-permute-start(bf16[128,512]{1,0:T(8,128)(2,1)S(1)} %get-tuple-element.61), channel_id=1, source_target_pairs={{0,2},{2,0},{4,6},{6,4},{1,3},{3,1},{5,7},{7,5},{8,10},{10,8},{12,... | collective-permute-start | bytes 393224 | tf_op jit(solution)/shard_map/ppermute | solution.py:284
  31.4 5.7 %collective-permute-start.10 = (bf16[128,512]{1,0:T(8,128)(2,1)S(1)}, bf16[128,512]{1,0:T(8,128)(2,1)S(1)}, u32[]{:S(2)}, u32[]{:S(2)}) collective-permute-start(bf16[128,512]{1,0:T(8,128)(2,1)S(1)} %add.2.refs_5_), channel_id=1, source_target_pairs={{0,4},{2,6},{4,0},{6,2},{1,5},{3,7},{5,1},{7,3},{8,12},{10,14},{12... | collective-permute-start | bytes 393224 | tf_op jit(solution)/shard_map/ppermute | solution.py:284
  34.0 3.1 %collective-permute-start.11 = (bf16[128,512]{1,0:T(8,128)(2,1)S(1)}, bf16[128,512]{1,0:T(8,128)(2,1)S(1)}, u32[]{:S(2)}, u32[]{:S(2)}) collective-permute-start(bf16[128,512]{1,0:T(8,128)(2,1)S(1)} %get-tuple-element.70), channel_id=1, source_target_pairs={{0,2},{2,0},{4,6},{6,4},{1,3},{3,1},{5,7},{7,5},{8,10},{10,8},{12,... | collective-permute-start | bytes 393224 | tf_op jit(solution)/shard_map/ppermute | solution.py:284
  34.1 2.9 %collective-permute-start.9 = (bf16[128,512]{1,0:T(8,128)(2,1)S(1)}, bf16[128,512]{1,0:T(8,128)(2,1)S(1)}, u32[]{:S(2)}, u32[]{:S(2)}) collective-permute-start(bf16[128,512]{1,0:T(8,128)(2,1)S(1)} %get-tuple-element.69), channel_id=1, source_target_pairs={{0,2},{2,0},{4,6},{6,4},{1,3},{3,1},{5,7},{7,5},{8,10},{10,8},{12,... | collective-permute-start | bytes 393224 | tf_op jit(solution)/shard_map/ppermute | solution.py:284

commit v8 on v6

--- a/solution.py
+++ b/solution.py
@@ -102,7 +102,7 @@
         refs[-1],
     )
     copies = cut_copies(sends, split, heads, up_ref, piece_refs)
-    run_copies([*copies, *zip(other_refs, other_outs), (q_ref, q_out)], sem)
+    run_copies([(q_ref, q_out), *zip(other_refs, other_outs), *copies], sem)
 
 
 def overlaps(sends, first, count):

time: 38.2 us -> 38.2 us (level)
  transfers between devices with their start and end apart: 13 -> 13, of which waited for: 5 -> 5; matrix products, arithmetic and copies ran while one was open for 0% -> 0% of each run, Pallas kernels for 30% -> 29%
where the time goes in v8:
time: 38.2 us; the launch traced here: 37.8 us
  Pallas kernels  13.1 us (34%)
  waiting for transfers between devices  12.4 us (32%)
  starting transfers between devices  11.6 us (30%)
  between operations  0.78 us (2%)
    ppermute x9, waiting for transfers between devices, swapped(): lax.ppermute(value, 'ctx', [(place, place ^ mask) for place in range(slot...  9.97 us
    ppermute x4, starting transfers between devices, across(): return lax.ppermute(part, ('pipe', 'head'), route)  5.95 us
    ppermute x9, starting transfers between devices, swapped(): lax.ppermute(value, 'ctx', [(place, place ^ mask) for place in range(slot...  5.62 us
    pallas_call x5, Pallas kernels, sums_of(): call(functools.partial(sums_kernel, span, first, count, sends, 0 if grads...  4.03 us
    pallas_call x1, Pallas kernels, per_device(): call(functools.partial(weights_kernel, slots, heads), 'weights', [shape((...  3.84 us
    ppermute x4, waiting for transfers between devices, across(): return lax.ppermute(part, ('pipe', 'head'), route)  2.39 us
    pallas_call x1, Pallas kernels, query_of(): call(functools.partial(query_kernel, slots, places, len(score_grads)), 'q...  1.61 us
    pallas_call x1, Pallas kernels, per_device(): call(functools.partial(later_load_kernel, sends[1:], split, heads, others...  1.55 us
  transfers between devices with their start and end apart: 13, of which 5 were waited for; matrix products, arithmetic and copies ran while one was open for 0% of the time, Pallas kernels for 29%

profile of v8, /device:TPU:24, one launch (start us, length us, event | category | flops | bytes accessed | tf_op | source)
XLA Modules:
  0.0 37.8 jit_solution(10676185762320949826)
XLA Ops:
  0.6 1.2 %first_load.1 = (bf16[64,3072]{1,0:T(8,128)(2,1)S(1)}, bf16[64,3072]{1,0:T(8,128)(2,1)S(1)}, bf16[128,1024]{1,0:T(8,128)(2,1)S(1)}) custom-call(bf16[64,8192]{1,0:T(8,128)(2,1)} %bitcast.9, bf16[128,512]{1,0:T(8,128)(2,1)} %bitcast.13, bf16[128,512]{1,0:T(8,128)(2,1)} %bitcast.14), custom_call_target="tpu_custom_call" | custom-call | flops 1024 | bytes 1024 | tf_op jit(solution)/shard_map/first_load/pallas_call | solution.py:301
  1.9 0.5 %collective-permute-start.3 = (bf16[64,3072]{1,0:T(8,128)(2,1)S(1)}, bf16[64,3072]{1,0:T(8,128)(2,1)S(1)}, u32[]{:S(2)}, u32[]{:S(2)}) collective-permute-start(bf16[64,3072]{1,0:T(8,128)(2,1)S(1)} %get-tuple-element.51), channel_id=1, source_target_pairs={{0,24},{1,25},{8,0},{9,1},{16,8},{17,9},{24,16},{25,17},{2,26},{3,... | collective-permute-start | bytes 1179656 | tf_op jit(solution)/shard_map/ppermute | solution.py:292
  2.4 1.4 %collective-permute-start.4 = (bf16[64,3072]{1,0:T(8,128)(2,1)S(1)}, bf16[64,3072]{1,0:T(8,128)(2,1)S(1)}, u32[]{:S(2)}, u32[]{:S(2)}) collective-permute-start(bf16[64,3072]{1,0:T(8,128)(2,1)S(1)} %get-tuple-element.52), channel_id=1, source_target_pairs={{0,25},{1,24},{8,1},{9,0},{16,9},{17,8},{24,17},{25,16},{2,27},{3,... | collective-permute-start | bytes 1179656 | tf_op jit(solution)/shard_map/ppermute | solution.py:292
  3.8 0.0 copy-start
  3.8 9.5 %conditional.1 = (bf16[128,1024]{1,0:T(8,128)(2,1)}, bf16[128,1024]{1,0:T(8,128)(2,1)}, bf16[128,1024]{1,0:T(8,128)(2,1)}) conditional(s32[]{:T(128)} %convert_element_type.3, bf16[128,1024]{1,0:T(8,128)(2,1)S(1)} %get-tuple-element.41.refs_0_.refs_5_, bf16[128,1024]{1,0:T(8,128)(2,1)S(1)} %get-tuple-element.41.refs_0_.refs_5_), branch_computations={%region_0.0_spmd, %region_1.0_spmd} | conditional | bytes 3145872 | solution.py:320
  3.8 1.5 %collective-permute-start.1 = (bf16[128,1024]{1,0:T(8,128)(2,1)S(1)}, bf16[128,1024]{1,0:T(8,128)(2,1)}, u32[]{:S(2)}, u32[]{:S(2)}) collective-permute-start(bf16[128,1024]{1,0:T(8,128)(2,1)S(1)} %param.1), channel_id=1, source_target_pairs={{0,4},{2,6},{4,0},{6,2},{1,5},{3,7},{5,1},{7,3},{8,12},{10,14},{12... | collective-permute-start | bytes 786440 | tf_op jit(solution)/shard_map/cond/branch_1_fun/ppermute | solution.py:284
  5.3 0.0 collective-permute-start
  5.3 6.1 %collective-permute-done.1 = bf16[128,1024]{1,0:T(8,128)(2,1)} collective-permute-done((bf16[128,1024]{1,0:T(8,128)(2,1)S(1)}, bf16[128,1024]{1,0:T(8,128)(2,1)}, u32[]{:S(2)}, u32[]{:S(2)}) %collective-permute-start.1) | collective-permute-done | bytes 262176 | tf_op jit(solution)/shard_map/cond/branch_1_fun/ppermute | solution.py:284
  11.4 0.0 collective-permute-start.2
  11.4 0.0 collective-permute-done
  11.4 1.9 %collective-permute-done.2 = bf16[128,1024]{1,0:T(8,128)(2,1)} collective-permute-done((bf16[128,1024]{1,0:T(8,128)(2,1)}, bf16[128,1024]{1,0:T(8,128)(2,1)}, u32[]{:S(2)}, u32[]{:S(2)}) %collective-permute-start.2) | collective-permute-done | bytes 262176 | tf_op jit(solution)/shard_map/cond/branch_1_fun/ppermute | solution.py:284
  13.2 1.5 %later_load.1 = (bf16[64,1024]{1,0:T(8,128)(2,1)S(1)}, bf16[64,1024]{1,0:T(8,128)(2,1)S(1)}, bf16[128,4096]{1,0:T(8,128)(2,1)S(1)}, bf16[128,1024]{1,0:T(8,128)(...) custom-call(bf16[64,8192]{1,0:T(8,128)(2,1)} %bitcast.10, bf16[128,4096]{1,0:T(8,128)(2,1)} %bitcast.11, ...), custom_call_target="tpu_custom_call" | custom-call | flops 1024 | bytes 1024 | tf_op jit(solution)/shard_map/later_load/pallas_call | solution.py:322
  14.8 0.5 %collective-permute-start.5 = (bf16[64,1024]{1,0:T(8,128)(2,1)S(1)}, bf16[64,1024]{1,0:T(8,128)(2,1)S(1)}, u32[]{:S(2)}, u32[]{:S(2)}) collective-permute-start(bf16[64,1024]{1,0:T(8,128)(2,1)S(1)} %get-tuple-element.59), channel_id=1, source_target_pairs={{0,24},{1,25},{8,0},{9,1},{16,8},{17,9},{24,16},{25,17},{2,26},{3,... | collective-permute-start | bytes 393224 | tf_op jit(solution)/shard_map/ppermute | solution.py:292
  15.3 3.5 %collective-permute-start.6 = (bf16[64,1024]{1,0:T(8,128)(2,1)S(1)}, bf16[64,1024]{1,0:T(8,128)(2,1)S(1)}, u32[]{:S(2)}, u32[]{:S(2)}) collective-permute-start(bf16[64,1024]{1,0:T(8,128)(2,1)S(1)} %get-tuple-element.60), channel_id=1, source_target_pairs={{0,25},{1,24},{8,1},{9,0},{16,9},{17,8},{24,17},{25,16},{2,27},{3,... | collective-permute-start | bytes 393224 | tf_op jit(solution)/shard_map/ppermute | solution.py:292
  18.8 0.0 copy-done
  18.9 3.8 %weights.1 = (bf16[4,512,1024]{2,1,0:T(8,128)(2,1)S(1)}, f32[128,4096]{1,0:T(8,128)S(1)}) custom-call(bf16[128,4096]{1,0:T(8,128)(2,1)S(1)} %get-tuple-element.45.q_ref, s32[4,2,8]{2,1,0:T(2,128)S(1)} %bitcast.8, bf16[128,1024]{1,0:T(8,128)(2,1)S(1)} %get-tuple-element.41.refs_0_.refs_5_, bf16[128,1024]{1,0:T(8,128)(2,1)S(1)} %get-tuple-element.46.refs_1_.refs_6_, ...), custom_call_target="tpu_custom_call" | custom-call | flops 1024 | bytes 1024 | tf_op jit(solution)/shard_map/weights/pallas_call | solution.py:340
  22.7 0.0 collective-permute-done.3.refs_4_
  22.7 2.4 %collective-permute-done.4.refs_5_ = bf16[64,3072]{1,0:T(8,128)(2,1)S(1)} collective-permute-done((bf16[64,3072]{1,0:T(8,128)(2,1)S(1)}, bf16[64,3072]{1,0:T(8,128)(2,1)S(1)}, u32[]{:S(2)}, u32[]{:S(2)}) %collective-permute-start.4) | collective-permute-done | bytes 393248 | tf_op jit(solution)/shard_map/ppermute | solution.py:292
  25.1 2.0 %sums_early.1 = (bf16[128,2048]{1,0:T(8,128)(2,1)}, bf16[2,512,1024]{2,1,0:T(8,128)(2,1)S(1)}, f32[256,512]{1,0:T(8,128)S(1)}, bf16[256,512]{1,0:T(8,128)(2,1)S(1)}) custom-call(bf16[4,512,1024]{2,1,0:T(8,128)(2,1)S(1)} %get-tuple-element.49.p_ref, f32[128,4096]{1,0:T(8,128)S(1)} %get-tuple-element.50.o_ref, bf16[128,4096]{1,0:T(8,128)(2,1)S(1)} %get-tuple-element.45.q_ref, ...), custom_call_target="tpu_custom_call" | custom-call | flops 1024 | bytes 1024 | tf_op jit(solution)/shard_map/sums_early/pallas_call | solution.py:359
  27.1 1.6 %collective-permute-start.8 = (bf16[256,512]{1,0:T(8,128)(2,1)S(1)}, bf16[256,512]{1,0:T(8,128)(2,1)S(1)}, u32[]{:S(2)}, u32[]{:S(2)}) collective-permute-start(bf16[256,512]{1,0:T(8,128)(2,1)S(1)} %get-tuple-element.69), channel_id=1, source_target_pairs={{0,4},{2,6},{4,0},{6,2},{1,5},{3,7},{5,1},{7,3},{8,12},{10,14},{12... | collective-permute-start | bytes 786440 | tf_op jit(solution)/shard_map/ppermute | solution.py:284
  28.7 1.2 %sums_middle.1 = (bf16[128,1024]{1,0:T(8,128)(2,1)}, bf16[1,512,1024]{2,1,0:T(8,128)(2,1)S(1)}, f32[128,256]{1,0:T(8,128)S(1)}, bf16[128,128]{1,0:T(8,128)(2,1)S...) custom-call(bf16[4,512,1024]{2,1,0:T(8,128)(2,1)S(1)} %get-tuple-element.49.p_ref, ...), custom_call_target="tpu_custom_call" | custom-call | flops 1024 | bytes 1024 | tf_op jit(solution)/shard_map/sums_middle/pallas_call | solution.py:359
  29.9 0.0 collective-permute-done.5.refs_2_
  29.9 0.0 collective-permute-done.6.refs_3_
  29.9 0.1 sums_3.1
  29.9 0.1 collective-permute-start.7
  30.0 0.1 sums_2.1
  30.1 1.3 %collective-permute-done.7.received_ref = bf16[128,512]{1,0:T(8,128)(2,1)S(1)} collective-permute-done((bf16[128,512]{1,0:T(8,128)(2,1)S(1)}, bf16[128,512]{1,0:T(8,128)(2,1)S(1)}, u32[]{:S(2)}, u32[]{:S(2)}) %collective-permute-start.7) | collective-permute-done | bytes 131104 | tf_op jit(solution)/shard_map/ppermute | solution.py:284
  31.4 1.8 %collective-permute-start.10 = (bf16[128,512]{1,0:T(8,128)(2,1)S(1)}, bf16[128,512]{1,0:T(8,128)(2,1)S(1)}, u32[]{:S(2)}, u32[]{:S(2)}) collective-permute-start(bf16[128,512]{1,0:T(8,128)(2,1)S(1)} %add.2.refs_6_), channel_id=1, source_target_pairs={{0,4},{2,6},{4,0},{6,2},{1,5},{3,7},{5,1},{7,3},{8,12},{10,14},{12... | collective-permute-start | bytes 393224 | tf_op jit(solution)/shard_map/ppermute | solution.py:284
  33.2 0.7 %sums_01.1 = (bf16[1,256,1024]{2,1,0:T(8,128)(2,1)S(1)}, f32[128,512]{1,0:T(8,128)S(1)}, bf16[128,256]{1,0:T(8,128)(2,1)S(1)}, bf16[128,256]{1,0:T(8,128)(2,1)S(1)}) custom-call(bf16[4,512,1024]{2,1,0:T(8,128)(2,1)S(1)} %get-tuple-element.49.p_ref, f32[128,4096]{1,0:T(8,128)S(1)} %get-tuple-element.50.o_ref, bf16[128,4096]{1,0:T(8,128)(2,1)S(1)} %get-tuple-element.45.q_ref, ...), custom_call_target="tpu_custom_call" | custom-call | flops 1024 | bytes 1024 | tf_op jit(solution)/shard_map/sums_01/pallas_call | solution.py:359
  34.0 0.0 collective-permute-done.8.received_ref
  34.0 0.1 collective-permute-start.9
  34.1 0.5 %collective-permute-start.11 = (bf16[128,256]{1,0:T(8,128)(2,1)S(1)}, bf16[128,256]{1,0:T(8,128)(2,1)S(1)}, u32[]{:S(2)}, u32[]{:S(2)}) collective-permute-start(bf16[128,256]{1,0:T(8,128)(2,1)S(1)} %get-tuple-element.73), channel_id=1, source_target_pairs={{0,2},{2,0},{4,6},{6,4},{1,3},{3,1},{5,7},{7,5},{8,10},{10,8},{12,... | collective-permute-start | bytes 196616 | tf_op jit(solution)/shard_map/ppermute | solution.py:284
  34.6 0.1 collective-permute-start.12
  34.7 1.6 %query.1 = bf16[128,4096]{1,0:T(8,128)(2,1)} custom-call(bf16[2,512,1024]{2,1,0:T(8,128)(2,1)S(1)} %get-tuple-element.53.refs_0_, bf16[1,512,1024]{2,1,0:T(8,128)(2,1)S(1)} %get-tuple-element.54.refs_1_, bf16[1,256,1024]{2,1,0:T(8,128)(2,1)S(1)} %get-tuple-element.65.refs_2_, bf16[1,128,1024]{2,1,0:T(8,128)(2,1)S(1)} %get-tuple-element.66.refs_3_, ...), custom_call_target="tpu_custom_call" | custom-call | flops 1024 | bytes 1024 | tf_op jit(solution)/shard_map/query/pallas_call | solution.py:378
  36.3 0.0 collective-permute-done.11.refs_4_
  36.3 0.0 collective-permute-done.12.refs_5_
  36.3 0.7 %collective-permute-done.10.refs_3_ = bf16[128,512]{1,0:T(8,128)(2,1)S(1)} collective-permute-done((bf16[128,512]{1,0:T(8,128)(2,1)S(1)}, bf16[128,512]{1,0:T(8,128)(2,1)S(1)}, u32[]{:S(2)}, u32[]{:S(2)}) %collective-permute-start.10) | collective-permute-done | bytes 131104 | tf_op jit(solution)/shard_map/ppermute | solution.py:284
  37.0 0.0 collective-permute-done.9.refs_1_
  37.0 0.7 %finish.1 = (bf16[128,512]{1,0:T(8,128)(2,1)}, bf16[128,512]{1,0:T(8,128)(2,1)}) custom-call(f32[128,512]{1,0:T(8,128)S(1)} %get-tuple-element.71.refs_0_, bf16[128,512]{1,0:T(8,128)(2,1)S(1)} %collective-permute-done.9.refs_1_, f32[128,512]{1,0:T(8,128)S(1)} %get-tuple-element.70.refs_0_.refs_2_, bf16[128,512]{1,0:T(8,128)(2,1)S(1)} %collective-permute-done.10.refs_3_, ...), custom_call_target="tpu_custom_call" | custom-call | flops 1024 | bytes 1024 | tf_op jit(solution)/shard_map/finish/pallas_call | solution.py:426
  (2 shorter events, 0.1 us)
Async XLA Ops:
  1.9 20.8 %collective-permute-start.3 = (bf16[64,3072]{1,0:T(8,128)(2,1)S(1)}, bf16[64,3072]{1,0:T(8,128)(2,1)S(1)}, u32[]{:S(2)}, u32[]{:S(2)}) collective-permute-start(bf16[64,3072]{1,0:T(8,128)(2,1)S(1)} %get-tuple-element.51), channel_id=1, source_target_pairs={{0,24},{1,25},{8,0},{9,1},{16,8},{17,9},{24,16},{25,17},{2,26},{3,... | collective-permute-start | bytes 1179656 | tf_op jit(solution)/shard_map/ppermute | solution.py:292
  2.4 22.7 %collective-permute-start.4 = (bf16[64,3072]{1,0:T(8,128)(2,1)S(1)}, bf16[64,3072]{1,0:T(8,128)(2,1)S(1)}, u32[]{:S(2)}, u32[]{:S(2)}) collective-permute-start(bf16[64,3072]{1,0:T(8,128)(2,1)S(1)} %get-tuple-element.52), channel_id=1, source_target_pairs={{0,25},{1,24},{8,1},{9,0},{16,9},{17,8},{24,17},{25,16},{2,27},{3,... | collective-permute-start | bytes 1179656 | tf_op jit(solution)/shard_map/ppermute | solution.py:292
  3.8 15.1 %copy-start = (s32[1,4,2,8]{3,2,1,0:T(2,128)S(1)}, s32[1,4,2,8]{3,2,1,0:T(2,128)}, u32[]{:S(2)}) copy-start(s32[1,4,2,8]{3,2,1,0:T(2,128)} %param.11) | copy-start | bytes 772
  3.8 7.6 %collective-permute-start.1 = (bf16[128,1024]{1,0:T(8,128)(2,1)S(1)}, bf16[128,1024]{1,0:T(8,128)(2,1)}, u32[]{:S(2)}, u32[]{:S(2)}) collective-permute-start(bf16[128,1024]{1,0:T(8,128)(2,1)S(1)} %param.1), channel_id=1, source_target_pairs={{0,4},{2,6},{4,0},{6,2},{1,5},{3,7},{5,1},{7,3},{8,12},{10,14},{12... | collective-permute-start | bytes 786440 | tf_op jit(solution)/shard_map/cond/branch_1_fun/ppermute | solution.py:284
  5.3 6.1 %collective-permute-start = (bf16[128,1024]{1,0:T(8,128)(2,1)S(1)}, bf16[128,1024]{1,0:T(8,128)(2,1)}, u32[]{:S(2)}, u32[]{:S(2)}) collective-permute-start(bf16[128,1024]{1,0:T(8,128)(2,1)S(1)} %param.1), channel_id=1, source_target_pairs={{0,2},{2,0},{4,6},{6,4},{1,3},{3,1},{5,7},{7,5},{8,10},{10,8},{12,... | collective-permute-start | bytes 786440 | tf_op jit(solution)/shard_map/cond/branch_1_fun/ppermute | solution.py:284
  11.4 1.9 %collective-permute-start.2 = (bf16[128,1024]{1,0:T(8,128)(2,1)}, bf16[128,1024]{1,0:T(8,128)(2,1)}, u32[]{:S(2)}, u32[]{:S(2)}) collective-permute-start(bf16[128,1024]{1,0:T(8,128)(2,1)} %collective-permute-done.1), channel_id=1, source_target_pairs={{0,2},{2,0},{4,6},{6,4},{1,3},{3,1},{5,7},{7,5},{8,10},{10,8},{12,... | collective-permute-start | bytes 786440 | tf_op jit(solution)/shard_map/cond/branch_1_fun/ppermute | solution.py:284
  14.8 15.1 %collective-permute-start.5 = (bf16[64,1024]{1,0:T(8,128)(2,1)S(1)}, bf16[64,1024]{1,0:T(8,128)(2,1)S(1)}, u32[]{:S(2)}, u32[]{:S(2)}) collective-permute-start(bf16[64,1024]{1,0:T(8,128)(2,1)S(1)} %get-tuple-element.59), channel_id=1, source_target_pairs={{0,24},{1,25},{8,0},{9,1},{16,8},{17,9},{24,16},{25,17},{2,26},{3,... | collective-permute-start | bytes 393224 | tf_op jit(solution)/shard_map/ppermute | solution.py:292
  15.3 14.6 %collective-permute-start.6 = (bf16[64,1024]{1,0:T(8,128)(2,1)S(1)}, bf16[64,1024]{1,0:T(8,128)(2,1)S(1)}, u32[]{:S(2)}, u32[]{:S(2)}) collective-permute-start(bf16[64,1024]{1,0:T(8,128)(2,1)S(1)} %get-tuple-element.60), channel_id=1, source_target_pairs={{0,25},{1,24},{8,1},{9,0},{16,9},{17,8},{24,17},{25,16},{2,27},{3,... | collective-permute-start | bytes 393224 | tf_op jit(solution)/shard_map/ppermute | solution.py:292
  27.1 6.8 %collective-permute-start.8 = (bf16[256,512]{1,0:T(8,128)(2,1)S(1)}, bf16[256,512]{1,0:T(8,128)(2,1)S(1)}, u32[]{:S(2)}, u32[]{:S(2)}) collective-permute-start(bf16[256,512]{1,0:T(8,128)(2,1)S(1)} %get-tuple-element.69), channel_id=1, source_target_pairs={{0,4},{2,6},{4,0},{6,2},{1,5},{3,7},{5,1},{7,3},{8,12},{10,14},{12... | collective-permute-start | bytes 786440 | tf_op jit(solution)/shard_map/ppermute | solution.py:284
  29.9 1.4 %collective-permute-start.7 = (bf16[128,512]{1,0:T(8,128)(2,1)S(1)}, bf16[128,512]{1,0:T(8,128)(2,1)S(1)}, u32[]{:S(2)}, u32[]{:S(2)}) collective-permute-start(bf16[128,512]{1,0:T(8,128)(2,1)S(1)} %get-tuple-element.64), channel_id=1, source_target_pairs={{0,2},{2,0},{4,6},{6,4},{1,3},{3,1},{5,7},{7,5},{8,10},{10,8},{12,... | collective-permute-start | bytes 393224 | tf_op jit(solution)/shard_map/ppermute | solution.py:284
  31.4 5.7 %collective-permute-start.10 = (bf16[128,512]{1,0:T(8,128)(2,1)S(1)}, bf16[128,512]{1,0:T(8,128)(2,1)S(1)}, u32[]{:S(2)}, u32[]{:S(2)}) collective-permute-start(bf16[128,512]{1,0:T(8,128)(2,1)S(1)} %add.2.refs_6_), channel_id=1, source_target_pairs={{0,4},{2,6},{4,0},{6,2},{1,5},{3,7},{5,1},{7,3},{8,12},{10,14},{12... | collective-permute-start | bytes 393224 | tf_op jit(solution)/shard_map/ppermute | solution.py:284
  34.0 3.0 %collective-permute-start.9 = (bf16[128,512]{1,0:T(8,128)(2,1)S(1)}, bf16[128,512]{1,0:T(8,128)(2,1)S(1)}, u32[]{:S(2)}, u32[]{:S(2)}) collective-permute-start(bf16[128,512]{1,0:T(8,128)(2,1)S(1)} %get-tuple-element.72), channel_id=1, source_target_pairs={{0,2},{2,0},{4,6},{6,4},{1,3},{3,1},{5,7},{7,5},{8,10},{10,8},{12,... | collective-permute-start | bytes 393224 | tf_op jit(solution)/shard_map/ppermute | solution.py:284
  34.1 2.2 %collective-permute-start.11 = (bf16[128,256]{1,0:T(8,128)(2,1)S(1)}, bf16[128,256]{1,0:T(8,128)(2,1)S(1)}, u32[]{:S(2)}, u32[]{:S(2)}) collective-permute-start(bf16[128,256]{1,0:T(8,128)(2,1)S(1)} %get-tuple-element.73), channel_id=1, source_target_pairs={{0,2},{2,0},{4,6},{6,4},{1,3},{3,1},{5,7},{7,5},{8,10},{10,8},{12,... | collective-permute-start | bytes 196616 | tf_op jit(solution)/shard_map/ppermute | solution.py:284
  34.6 1.7 %collective-permute-start.12 = (bf16[128,256]{1,0:T(8,128)(2,1)S(1)}, bf16[128,256]{1,0:T(8,128)(2,1)S(1)}, u32[]{:S(2)}, u32[]{:S(2)}) collective-permute-start(bf16[128,256]{1,0:T(8,128)(2,1)S(1)} %get-tuple-element.74), channel_id=1, source_target_pairs={{0,2},{2,0},{4,6},{6,4},{1,3},{3,1},{5,7},{7,5},{8,10},{10,8},{12,... | collective-permute-start | bytes 196616 | tf_op jit(solution)/shard_map/ppermute | solution.py:284
